TPU v7x, 256 devices: a whole 4x4x8 slice. The times are simulated.
256 devices in a mesh: dp: 8 (over z_hi, y), seq: 32 (over z_lo, x, core).
Axes of the slice: x: 4, y: 4, z: 8 (z_hi: 2, z_lo: 4; z = z_hi * 4 + z_lo), core: 2. Of those that a mesh axis runs over, the one named last changes fastest.
Arguments:
- q_img: bfloat16 [8, 4096, 2048], P('dp', 'seq'), may hold values from -6 to 6
- k_img: bfloat16 [8, 4096, 2048], P('dp', 'seq'), may hold values from -6 to 6
- v_img: bfloat16 [8, 4096, 2048], P('dp', 'seq'), may hold values from -12 to 12
- x_txt: bfloat16 [8, 77, 2432], P('dp'), may hold values from -9 to 9
- w_txt: bfloat16 [3, 2432, 2048], P(None, 'dp', 'seq'), may hold values from -0.125 to 0.125
- grad_img: bfloat16 [8, 4096, 2048], P('dp', 'seq'), may hold values from -6 to 6
- grad_txt: bfloat16 [8, 77, 2048], P('dp', None, 'seq'), may hold values from -6 to 6
Outputs:
- o_img: bfloat16 [8, 4096, 2048], P('dp', 'seq')
- o_txt: bfloat16 [8, 77, 2048], P('dp', None, 'seq')
- grad_qkv_img: bfloat16 [3, 8, 4096, 2048], P(None, 'dp', 'seq')
- dx_txt: float32 [8, 77, 2432], P('dp', None, 'seq')
- dw_txt: float32 [3, 2432, 2048], P(None, 'dp', 'seq')
All inputs are finite; a program needn't handle non-finite values.
Results may differ from a plain program's by a relative error of at most 0.014.
Values may be sent and summed in bfloat16 or wider, within the bound.
No kernel may reach another device: no remote copies, remote signals or barrier semaphores. Data moves between devices by JAX's collectives and lax.ppermute only.
A program may use at most 64 MiB of HBM per device.

v0:
```python
import math

import jax
import jax.numpy as jnp
from jax import lax
from jax.sharding import PartitionSpec as P

HEAD_DIM = 64


def block_pass(query, cotangent, keys, values, scale):
    scores = jnp.einsum("gbd,gkd->gbk", query, keys, preferred_element_type=jnp.float32) * scale
    shifted = jnp.exp(scores - jnp.max(scores, axis=2, keepdims=True))
    softmax_rows = shifted / jnp.sum(shifted, axis=2, keepdims=True)
    rounded_probs = softmax_rows.astype(jnp.bfloat16)
    out_rows = jnp.einsum(
        "gbk,gkd->gbd", rounded_probs, values, preferred_element_type=jnp.float32
    ).astype(jnp.bfloat16)
    value_terms = jnp.einsum(
        "gbk,gbd->gkd", rounded_probs, cotangent, preferred_element_type=jnp.float32
    )
    prob_grads = jnp.einsum("gbd,gkd->gbk", cotangent, values, preferred_element_type=jnp.float32)
    row_terms = jnp.sum(
        cotangent.astype(jnp.float32) * out_rows.astype(jnp.float32), axis=2, keepdims=True
    )
    score_grads = (softmax_rows * (prob_grads - row_terms)).astype(jnp.bfloat16)
    query_grads = (
        jnp.einsum("gbk,gkd->gbd", score_grads, keys, preferred_element_type=jnp.float32) * scale
    ).astype(jnp.bfloat16)
    key_terms = (
        jnp.einsum("gbk,gbd->gkd", score_grads, query, preferred_element_type=jnp.float32) * scale
    )
    return (out_rows, query_grads, key_terms, value_terms)


def local(q_img, k_img, v_img, x_txt, w_txt, grad_img, grad_txt):
    scale = 1.0 / math.sqrt(HEAD_DIM)
    full_weights = lax.all_gather(w_txt, "dp", axis=1, tiled=True)
    projected = jnp.einsum("std,idh->isth", x_txt, full_weights, preferred_element_type=jnp.float32)
    text_qkv = projected.astype(jnp.bfloat16)
    query_heads, key_heads, value_heads, cotangent_heads = (
        lax.all_to_all(q_img, "seq", split_axis=2, concat_axis=1, tiled=True),
        lax.all_to_all(k_img, "seq", split_axis=2, concat_axis=1, tiled=True),
        lax.all_to_all(v_img, "seq", split_axis=2, concat_axis=1, tiled=True),
        lax.all_to_all(grad_img, "seq", split_axis=2, concat_axis=1, tiled=True),
    )
    samples, img_rows, local_cols = query_heads.shape
    txt_rows = x_txt.shape[1]
    head_count = local_cols // HEAD_DIM
    length = img_rows + txt_rows

    def split_heads(image_part, text_part):
        whole = jnp.concatenate([image_part, text_part], axis=1)
        whole = whole.reshape(samples, length, head_count, HEAD_DIM).transpose(0, 2, 1, 3)
        return whole.reshape(samples * head_count, length, HEAD_DIM)

    def merge_heads(stacked, rows):
        shaped = stacked.reshape(samples, head_count, rows, HEAD_DIM).transpose(0, 2, 1, 3)
        return shaped.reshape(samples, rows, head_count * HEAD_DIM)

    queries = split_heads(query_heads, text_qkv[0])
    keys = split_heads(key_heads, text_qkv[1])
    values = split_heads(value_heads, text_qkv[2])
    cotangents = split_heads(cotangent_heads, grad_txt)
    row_block = min(512, img_rows)
    block_count = img_rows // row_block
    group = samples * head_count
    text_queries = queries[:, img_rows:]
    text_cotangents = cotangents[:, img_rows:]
    steps_range = jnp.arange(block_count)

    def unblock(blocked):
        return blocked.transpose(1, 0, 2, 3).reshape(group, img_rows, HEAD_DIM)

    def image_step(carry, step_index):
        first_row = step_index * row_block
        query_rows = lax.dynamic_slice_in_dim(queries, first_row, row_block, 1)
        cotangent_rows = lax.dynamic_slice_in_dim(cotangents, first_row, row_block, 1)
        out_rows, query_grads, key_terms, value_terms = block_pass(
            query_rows, cotangent_rows, keys, values, scale
        )
        return ((carry[0] + key_terms, carry[1] + value_terms), (out_rows, query_grads))

    zeros = jnp.zeros(keys.shape, jnp.float32)
    (key_sums, value_sums), (image_out, image_query_grads) = lax.scan(
        image_step, (zeros, zeros), steps_range
    )
    text_out, text_query_grads, text_key_terms, text_value_terms = block_pass(
        text_queries, text_cotangents, keys, values, scale
    )
    key_grads = (key_sums + text_key_terms).astype(jnp.bfloat16)
    value_grads = (value_sums + text_value_terms).astype(jnp.bfloat16)
    out_tokens, dq_tokens, dk_tokens, dv_tokens = (
        lax.all_to_all(
            merge_heads(unblock(image_out), img_rows),
            "seq",
            split_axis=1,
            concat_axis=2,
            tiled=True,
        ),
        lax.all_to_all(
            merge_heads(unblock(image_query_grads), img_rows),
            "seq",
            split_axis=1,
            concat_axis=2,
            tiled=True,
        ),
        lax.all_to_all(
            merge_heads(key_grads[:, :img_rows], img_rows),
            "seq",
            split_axis=1,
            concat_axis=2,
            tiled=True,
        ),
        lax.all_to_all(
            merge_heads(value_grads[:, :img_rows], img_rows),
            "seq",
            split_axis=1,
            concat_axis=2,
            tiled=True,
        ),
    )
    o_txt = merge_heads(text_out, txt_rows)
    text_grads = jnp.stack(
        [
            merge_heads(text_query_grads, txt_rows),
            merge_heads(key_grads[:, img_rows:], txt_rows),
            merge_heads(value_grads[:, img_rows:], txt_rows),
        ]
    )
    weight_rows = lax.psum_scatter(
        jnp.einsum("std,isth->dih", x_txt, text_grads, preferred_element_type=jnp.float32),
        "dp",
        scatter_dimension=0,
        tiled=True,
    )
    dw_txt = weight_rows.transpose(1, 0, 2)
    partial_grads = jnp.einsum(
        "isth,idh->std", text_grads, full_weights, preferred_element_type=jnp.float32
    )
    dx_txt = lax.psum_scatter(partial_grads, "seq", scatter_dimension=2, tiled=True)
    grad_qkv_img = jnp.stack([dq_tokens, dk_tokens, dv_tokens])
    return (out_tokens, o_txt, grad_qkv_img, dx_txt, dw_txt)


def solution(mesh):
    in_specs = (
        P("dp", "seq", None),
        P("dp", "seq", None),
        P("dp", "seq", None),
        P("dp", None, None),
        P(None, "dp", "seq"),
        P("dp", "seq", None),
        P("dp", None, "seq"),
    )
    out_specs = (
        P("dp", "seq", None),
        P("dp", None, "seq"),
        P(None, "dp", "seq", None),
        P("dp", None, "seq"),
        P(None, "dp", "seq"),
    )
    return jax.shard_map(local, mesh=mesh, in_specs=in_specs, out_specs=out_specs, check_vma=False)
```

profile of v0, /device:TPU:8, one launch (start us, length us, event | category | flops | bytes accessed | tf_op | source)
XLA Modules:
  0.0 697.1 jit_solution(2444918634482222307)
XLA Ops:
  11.0 11.6 %reduce.10 = bf16[2048,128]{1,0:T(8,128)(2,1)S(1)} reduce(bf16[2048,1,128]{2,1,0:T(2,128)(2,1)S(1)} %bitcast.278, bf16[]{:T(256)} %broadcast.61), dimensions={1}, to_apply=%bitcast.185.reduce_sub_computation | reduce | bytes 1048578
  23.5 8.7 %all-to-all-start = ((bf16[32,2,4096]{2,1,0:T(2,128)(2,1)}), bf16[32,2,4096]{2,1,0:T(2,128)(2,1)S(1)}, u32[]{:S(2)}, u32[]{:S(2)}) async-start(bf16[32,2,4096]{2,1,0:T(2,128)(2,1)} %reshape.168), calls=%async_computation | async-start | bytes 1048576 | tf_op jit(solution)/shard_map/all_to_all | solution.py:42
  33.0 11.6 %reduce.11 = bf16[2048,128]{1,0:T(8,128)(2,1)S(1)} reduce(bf16[2048,1,128]{2,1,0:T(2,128)(2,1)S(1)} %bitcast.279, bf16[]{:T(256)} %broadcast.61), dimensions={1}, to_apply=%bitcast.187.reduce_sub_computation | reduce | bytes 1048578
  45.5 2.6 all-to-all-done
  48.1 5.3 all-to-all-start.1
  54.2 11.6 %reduce.13 = bf16[2048,128]{1,0:T(8,128)(2,1)S(1)} reduce(bf16[2048,1,128]{2,1,0:T(2,128)(2,1)S(1)} %bitcast.280, bf16[]{:T(256)} %broadcast.61), dimensions={1}, to_apply=%bitcast.191.reduce_sub_computation | reduce | bytes 1048578
  66.7 2.6 all-to-all-done.1
  69.3 5.3 all-to-all-start.3
  75.4 11.6 %reduce.12 = bf16[2048,128]{1,0:T(8,128)(2,1)S(1)} reduce(bf16[2048,1,128]{2,1,0:T(2,128)(2,1)S(1)} %bitcast.281, bf16[]{:T(256)} %broadcast.61), dimensions={1}, to_apply=%bitcast.189.reduce_sub_computation | reduce | bytes 1048578
  87.9 2.6 all-to-all-done.3
  90.5 5.3 all-to-all-start.2
  96.1 61.4 %all_gather.3 = bf16[3,2432,64]{2,0,1:T(4,128)(2,1)} all-gather(bf16[3,304,64]{2,0,1:T(4,128)(2,1)S(1)} %copy.87), channel_id=1, replica_groups=mesh['dp'=8,'seq'=32] {'dp'}, dimensions={1}, use_global_device_ids=true | all-gather | bytes 1050624 | tf_op jit(solution)/shard_map/all_gather | solution.py:38
  157.5 3.2 copy.88
  161.7 4.5 reshape.169
  171.6 4.5 reshape.175
  178.3 4.4 reshape.173
  194.9 149.7 %while.17 = (s32[]{:T(128)}, f32[1,4173,64]{1,2,0:T(8,128)S(1)}, f32[1,4173,64]{1,2,0:T(8,128)S(1)}, bf16[8,1,512,64]{2,3,1,0:T(8,128)(2,1)}, bf16[8,1,512,64]{2...) while((s32[]{:T(128)}, f32[1,4173,64]{1,2,0:T(8,128)S(1)}, ...), condition=%wide.region_4.5_spmd.clone, body=%wide.region_0.4_spmd.clone.sunk | while | flops 1668092544 | bytes 71650464 | solution.py:85
  196.2 2.6 fusion.95
  203.3 2.4 fusion.100
  205.7 3.4 multiply_convert_fusion.2
  214.9 2.6 fusion.95
  224.4 3.4 multiply_convert_fusion.2
  233.6 2.6 fusion.95
  243.1 3.4 multiply_convert_fusion.2
  252.3 2.6 fusion.95
  261.8 3.4 multiply_convert_fusion.2
  271.0 2.6 fusion.95
  280.6 3.4 multiply_convert_fusion.2
  289.7 2.6 fusion.95
  299.3 3.4 multiply_convert_fusion.2
  308.4 2.6 fusion.95
  318.0 3.4 multiply_convert_fusion.2
  327.2 2.6 fusion.95
  336.7 3.4 multiply_convert_fusion.2
  354.6 22.9 %reduce.14 = bf16[4096,64]{1,0:T(8,128)(2,1)S(1)} reduce(bf16[4096,1,64]{2,1,0:T(2,128)(2,1)S(1)} %bitcast.268, bf16[]{:T(256)} %broadcast.61), dimensions={1}, to_apply=%bitcast.193.reduce_sub_computation | reduce | bytes 1048578
  379.0 12.8 %all-to-all-start.4 = ((bf16[32,2,4096]{2,1,0:T(2,128)(2,1)}), bf16[32,2,4096]{2,1,0:T(2,128)(2,1)}, u32[]{:S(2)}, u32[]{:S(2)}) async-start(bf16[32,2,4096]{2,1,0:T(2,128)(2,1)} %reshape.176), calls=%async_computation.4 | async-start | bytes 1048576 | tf_op jit(solution)/shard_map/all_to_all | solution.py:94
  395.5 2.7 copy.106
  398.3 22.5 %reduce.16 = bf16[4096,64]{1,0:T(8,128)(2,1)S(1)} reduce(bf16[4096,1,64]{2,1,0:T(2,128)(2,1)S(1)} %bitcast.265, bf16[]{:T(256)} %broadcast.61), dimensions={1}, to_apply=%bitcast.197.reduce_sub_computation | reduce | bytes 1048578
  422.3 8.1 %all-to-all-start.6 = ((bf16[32,2,4096]{2,1,0:T(2,128)(2,1)}), bf16[32,2,4096]{2,1,0:T(2,128)(2,1)}, u32[]{:S(2)}, u32[]{:S(2)}) async-start(bf16[32,2,4096]{2,1,0:T(2,128)(2,1)} %reshape.180), calls=%async_computation.6 | async-start | bytes 1048576 | tf_op jit(solution)/shard_map/all_to_all | solution.py:108
  430.5 2.8 copy.109
  433.3 22.5 %reduce.15 = bf16[4096,64]{1,0:T(8,128)(2,1)S(1)} reduce(bf16[4096,1,64]{2,1,0:T(2,128)(2,1)S(1)} %bitcast.266, bf16[]{:T(256)} %broadcast.61), dimensions={1}, to_apply=%bitcast.195.reduce_sub_computation | reduce | bytes 1048578
  457.3 8.2 %all-to-all-start.7 = ((bf16[32,2,4096]{2,1,0:T(2,128)(2,1)}), bf16[32,2,4096]{2,1,0:T(2,128)(2,1)}, u32[]{:S(2)}, u32[]{:S(2)}) async-start(bf16[32,2,4096]{2,1,0:T(2,128)(2,1)} %reshape.178), calls=%async_computation.7 | async-start | bytes 1048576 | tf_op jit(solution)/shard_map/all_to_all | solution.py:115
  466.5 22.5 %reduce.17 = bf16[4096,64]{1,0:T(8,128)(2,1)S(1)} reduce(bf16[4096,1,64]{2,1,0:T(2,128)(2,1)S(1)} %bitcast.267, bf16[]{:T(256)} %broadcast.61), dimensions={1}, to_apply=%bitcast.199.reduce_sub_computation | reduce | bytes 1048578
  490.5 7.8 %all-to-all-start.5 = ((bf16[32,2,4096]{2,1,0:T(2,128)(2,1)}), bf16[32,2,4096]{2,1,0:T(2,128)(2,1)S(1)}, u32[]{:S(2)}, u32[]{:S(2)}) async-start(bf16[32,2,4096]{2,1,0:T(2,128)(2,1)} %reshape.182), calls=%async_computation.5 | async-start | bytes 1048576 | tf_op jit(solution)/shard_map/all_to_all | solution.py:101
  499.6 157.3 %all-reduce.3.cloned.1.call-done = f32[1,77,2432]{1,0,2:T(1,128)} async-done(((f32[1,77,2432]{1,0,2:T(1,128)}), f32[1,77,2432]{1,0,2:T(1,128)}) %all-reduce.3.cloned.1.call-update) | async-done | bytes 749072
  658.3 4.1 reshape.181
  665.8 4.1 reshape.179
  673.3 4.1 reshape.177
  (241 shorter events, 164.7 us)
Async XLA Ops:
  8.0 152.7 %copy-start = (bf16[1,77,2432]{2,1,0:T(8,128)(2,1)S(1)}, bf16[1,77,2432]{2,1,0:T(8,128)(2,1)}, u32[]{:S(2)}) copy-start(bf16[1,77,2432]{2,1,0:T(8,128)(2,1)} %param.12) | copy-start | bytes 1123588
  22.6 9.7 %copy-start.17 = (bf16[1,128,2048]{2,1,0:T(8,128)(2,1)S(1)}, bf16[1,128,2048]{2,1,0:T(8,128)(2,1)}, u32[]{:S(2)}) copy-start(bf16[1,128,2048]{2,1,0:T(8,128)(2,1)} %param.10) | copy-start | bytes 1572868
  23.5 24.6 %all-to-all-start = ((bf16[32,2,4096]{2,1,0:T(2,128)(2,1)}), bf16[32,2,4096]{2,1,0:T(2,128)(2,1)S(1)}, u32[]{:S(2)}, u32[]{:S(2)}) async-start(bf16[32,2,4096]{2,1,0:T(2,128)(2,1)} %reshape.168), calls=%async_computation | async-start | bytes 1048576 | tf_op jit(solution)/shard_map/all_to_all | solution.py:42
  44.6 8.8 %copy-start.18 = (bf16[1,128,2048]{2,1,0:T(8,128)(2,1)S(1)}, bf16[1,128,2048]{2,1,0:T(8,128)(2,1)}, u32[]{:S(2)}) copy-start(bf16[1,128,2048]{2,1,0:T(8,128)(2,1)} %param.11) | copy-start | bytes 1572868
  48.1 17.7 %copy-start.6 = (bf16[32,2,4096]{2,1,0:T(2,128)(2,1)}, bf16[32,2,4096]{2,1,0:T(2,128)(2,1)S(1)}, u32[]{:S(2)}) copy-start(bf16[32,2,4096]{2,1,0:T(2,128)(2,1)S(1)} %all-to-all-done) | copy-start | bytes 1572868
  48.1 21.2 %all-to-all-start.1 = ((bf16[32,2,4096]{2,1,0:T(2,128)(2,1)}), bf16[32,2,4096]{2,1,0:T(2,128)(2,1)S(1)}, u32[]{:S(2)}, u32[]{:S(2)}) async-start(bf16[32,2,4096]{2,1,0:T(2,128)(2,1)} %reshape.170), calls=%async_computation.1 | async-start | bytes 1048576 | tf_op jit(solution)/shard_map/all_to_all | solution.py:43
  65.8 8.8 %copy-start.19 = (bf16[1,128,2048]{2,1,0:T(8,128)(2,1)S(1)}, bf16[1,128,2048]{2,1,0:T(8,128)(2,1)}, u32[]{:S(2)}) copy-start(bf16[1,128,2048]{2,1,0:T(8,128)(2,1)} %param.14) | copy-start | bytes 1572868
  69.3 17.6 %copy-start.7 = (bf16[32,2,4096]{2,1,0:T(2,128)(2,1)}, bf16[32,2,4096]{2,1,0:T(2,128)(2,1)S(1)}, u32[]{:S(2)}) copy-start(bf16[32,2,4096]{2,1,0:T(2,128)(2,1)S(1)} %all-to-all-done.1) | copy-start | bytes 1572868
  69.3 21.1 %all-to-all-start.3 = ((bf16[32,2,4096]{2,1,0:T(2,128)(2,1)}), bf16[32,2,4096]{2,1,0:T(2,128)(2,1)S(1)}, u32[]{:S(2)}, u32[]{:S(2)}) async-start(bf16[32,2,4096]{2,1,0:T(2,128)(2,1)} %reshape.174), calls=%async_computation.3 | async-start | bytes 1048576 | tf_op jit(solution)/shard_map/all_to_all | solution.py:44
  87.0 8.9 %copy-start.26 = (bf16[3,304,64]{1,2,0:T(8,128)(2,1)S(1)}, bf16[3,304,64]{1,2,0:T(8,128)(2,1)}, u32[]{:S(2)}) copy-start(bf16[3,304,64]{1,2,0:T(8,128)(2,1)} %param.13) | copy-start | bytes 350212
  90.5 5.4 copy-start.9
  90.5 87.8 %all-to-all-start.2 = ((bf16[32,2,4096]{2,1,0:T(2,128)(2,1)}), bf16[32,2,4096]{2,1,0:T(2,128)(2,1)}, u32[]{:S(2)}, u32[]{:S(2)}) async-start(bf16[32,2,4096]{2,1,0:T(2,128)(2,1)} %reshape.172), calls=%async_computation.2 | async-start | bytes 1048576 | tf_op jit(solution)/shard_map/all_to_all | solution.py:45
  95.8 561.1 %all-reduce.3.cloned.1.call-start = ((), (), s32[]{:S(2)}) async-start(), calls=%async_computation.10 | async-start | bytes 2490368
  160.7 5.5 copy-start.2
  161.7 27.9 %copy-start.24 = (bf16[1,77,64]{1,2,0:T(8,128)(2,1)}, bf16[1,77,64]{1,2,0:T(8,128)(2,1)S(1)}, u32[]{:S(2)}) copy-start(bf16[1,77,64]{1,2,0:T(8,128)(2,1)S(1)} %get-tuple-element.177) | copy-start | bytes 29572
  166.2 2.2 copy-start.8
  182.7 2.3 copy-start.11
  182.7 2.3 copy-start.29
  188.1 1.6 copy-start.13
  188.1 1.6 copy-start.30
  189.7 3.3 copy-start.31
  200.0 1.5 copy-start.16
  205.7 3.4 copy-start.1
  218.7 1.5 copy-start.16
  224.4 3.4 copy-start.1
  237.4 1.5 copy-start.16
  243.1 3.4 copy-start.1
  256.1 1.5 copy-start.16
  261.8 3.4 copy-start.1
  280.5 3.4 copy-start.1
  299.3 3.4 copy-start.1
  318.0 3.4 copy-start.1
  336.7 3.4 copy-start.1
  344.6 1.8 copy-start.4
  350.7 2.8 copy-start.27
  351.0 2.5 copy-start.5
  351.9 1.7 copy-start.22
  351.9 1.7 copy-start.21
  377.4 14.4 %copy-start.23 = (bf16[1,1,77,64]{2,3,1,0:T(8,128)(2,1)S(1)}, bf16[1,1,77,64]{2,3,1,0:T(8,128)(2,1)}, u32[]{:S(2)}) copy-start(bf16[1,1,77,64]{2,3,1,0:T(8,128)(2,1)} %copy-done.22) | copy-start | bytes 29572
  377.4 14.4 %copy-start.28 = (bf16[1,1,77,64]{2,3,1,0:T(8,128)(2,1)S(1)}, bf16[1,1,77,64]{2,3,1,0:T(8,128)(2,1)}, u32[]{:S(2)}) copy-start(bf16[1,1,77,64]{2,3,1,0:T(8,128)(2,1)} %copy-done.27) | copy-start | bytes 29572
  379.0 43.3 %all-to-all-start.4 = ((bf16[32,2,4096]{2,1,0:T(2,128)(2,1)}), bf16[32,2,4096]{2,1,0:T(2,128)(2,1)}, u32[]{:S(2)}, u32[]{:S(2)}) async-start(bf16[32,2,4096]{2,1,0:T(2,128)(2,1)} %reshape.176), calls=%async_computation.4 | async-start | bytes 1048576 | tf_op jit(solution)/shard_map/all_to_all | solution.py:94
  391.8 295.8 %reduce-scatter.4.cloned.1.call-start = ((), (), s32[]{:S(2)}) async-start(), calls=%async_computation.9 | async-start | bytes 2801664
  422.3 8.1 %slice-start.1 = ((bf16[1,4173,64]{1,2,0:T(8,128)(2,1)}), bf16[1,4096,64]{1,2,0:T(8,128)(2,1)S(1)}, s32[]{:S(2)}) async-start(bf16[1,4173,64]{1,2,0:T(8,128)(2,1)} %copy-done.10), calls=%async_computation.12 | async-start | bytes 1048576 | tf_op jit(solution)/shard_map/slice | solution.py:116
  422.3 34.9 %all-to-all-start.6 = ((bf16[32,2,4096]{2,1,0:T(2,128)(2,1)}), bf16[32,2,4096]{2,1,0:T(2,128)(2,1)}, u32[]{:S(2)}, u32[]{:S(2)}) async-start(bf16[32,2,4096]{2,1,0:T(2,128)(2,1)} %reshape.180), calls=%async_computation.6 | async-start | bytes 1048576 | tf_op jit(solution)/shard_map/all_to_all | solution.py:108
  455.7 9.8 %copy-start.20 = (bf16[8,1,512,64]{2,3,1,0:T(8,128)(2,1)S(1)}, bf16[8,1,512,64]{2,3,1,0:T(8,128)(2,1)}, u32[]{:S(2)}) copy-start(bf16[8,1,512,64]{2,3,1,0:T(8,128)(2,1)} %get-tuple-element.61) | copy-start | bytes 1572868
  457.3 33.3 %all-to-all-start.7 = ((bf16[32,2,4096]{2,1,0:T(2,128)(2,1)}), bf16[32,2,4096]{2,1,0:T(2,128)(2,1)}, u32[]{:S(2)}, u32[]{:S(2)}) async-start(bf16[32,2,4096]{2,1,0:T(2,128)(2,1)} %reshape.178), calls=%async_computation.7 | async-start | bytes 1048576 | tf_op jit(solution)/shard_map/all_to_all | solution.py:115
  489.0 9.4 %copy-start.32 = (u32[256]{0:T(256)S(1)}, u32[256]{0:T(256)}, u32[]{:S(2)}) copy-start(u32[256]{0:T(256)} %constant.43) | copy-start | bytes 3076
  490.5 190.6 %all-to-all-start.5 = ((bf16[32,2,4096]{2,1,0:T(2,128)(2,1)}), bf16[32,2,4096]{2,1,0:T(2,128)(2,1)S(1)}, u32[]{:S(2)}, u32[]{:S(2)}) async-start(bf16[32,2,4096]{2,1,0:T(2,128)(2,1)} %reshape.182), calls=%async_computation.5 | async-start | bytes 1048576 | tf_op jit(solution)/shard_map/all_to_all | solution.py:101
  (11 other events, 13.2 us)
Sparse Core Ops, SparseCore 0:
  353.7 303.1 all-reduce.2
Sparse Core Ops, SparseCore 1:
  396.9 105.1 reduce-scatter.3
where the time goes:
time: 709 us; the launch traced here: 697 us
  waiting for transfers between devices  165 us (23%)
  other arithmetic  164 us (23%)
  matrix products  120 us (17%)
  local copies, waits for them, and re-layouts  102 us (14%)
  starting transfers between devices  61.7 us (9%)
  blocking collectives  61.4 us (9%)
  between operations  17.1 us (2%)
    unnamed x4, waiting for transfers between devices  157 us
    unnamed x10, other arithmetic  137 us
    unnamed x100, local copies, waits for them, and re-layouts  65.6 us
    all_gather x1, blocking collectives, local(): full_weights = lax.all_gather(w_txt, 'dp', axis=1, tiled=True)  61.4 us
    dot_general x9, matrix products, block_pass(): jnp.einsum('gbd,gkd->gbk', cotangent, values, preferred_element_type=jnp....  27.6 us
    dot_general x9, matrix products, block_pass(): jnp.einsum('gbd,gkd->gbk', query, keys, preferred_element_type=jnp.float32)  22.6 us
    dot_general x9, matrix products, block_pass(): jnp.einsum('gbk,gbd->gkd', rounded_probs, cotangent, preferred_element_ty...  19.7 us
    dot_general x9, matrix products, block_pass(): jnp.einsum('gbk,gbd->gkd', score_grads, query, preferred_element_type=jnp...  19.4 us
  transfers between devices with their start and end apart: 10, of which 4 were waited for; matrix products, arithmetic and copies ran while one was open for 28% of the time, Pallas kernels for 0%

commit v1 on v0

v1 whole, which is shorter than its diff:
```python
import functools

import jax
import jax.numpy as jnp
from jax import lax
from jax.experimental import pallas as pl
from jax.experimental.pallas import tpu as pltpu
from jax.sharding import PartitionSpec as P

bf16, f32 = jnp.bfloat16, jnp.float32
SDS = jax.ShapeDtypeStruct
LOG2E = 1.4426950408889634
DEVS = 32
TOK = 128
HALF = TOK // 2
IMG = DEVS * TOK
TXT = 77
TXT_PAD = 128
TXT_HALF = TXT_PAD // 2
KEYS = IMG + TXT_PAD
STEPS = 4
SRC_STEP = DEVS // STEPS
IMG_STEP = SRC_STEP * HALF
TXT_STEP = TXT_HALF // STEPS
ROWS = IMG_STEP + TXT_STEP
DX_ROWS = 48
EX_ROWS = IMG // 2 + TXT_HALF + TXT_PAD
CHUNK = 1024
VMEM = 60 << 20


def dot(a, b, ca, cb):
    return lax.dot_general(a, b, (((ca,), (cb,)), ((), ())), preferred_element_type=f32)


def low_lanes():
    return lax.broadcasted_iota(jnp.int32, (1, 128), 1) < 64


def swap(x):
    return jnp.concatenate([x[..., 64:], x[..., :64]], axis=-1)


def params(**kw):
    return pltpu.CompilerParams(vmem_limit_bytes=VMEM, **kw)


def whole(shape):
    return pl.BlockSpec(shape, lambda *i: (0,) * len(shape))


def cost(us):
    return pl.CostEstimate(flops=int(us * 1.15e9), bytes_accessed=1 << 20, transcendentals=0)


def pack_kernel(q_ref, k_ref, v_ref, g_ref, w_ref, x0_ref, x1_ref, w_out):
    low = low_lanes()
    tiles = q_ref.shape[1] // 128
    for c in range(tiles):
        cols = slice(128 * c, 128 * c + 128)
        q = q_ref[:, cols] * jnp.asarray(0.125, bf16)
        k, v, g = k_ref[:, cols], v_ref[:, cols], g_ref[:, cols]
        for which, (a, b) in enumerate(((q, g), (k, v))):
            first = jnp.where(low, a, swap(b))
            second = jnp.where(low, swap(a), b)
            for core in range(2):
                rows = slice(HALF * core, HALF * core + HALF)
                x0_ref[2 * c + core, which] = first[rows]
                x1_ref[2 * c + core, which] = second[rows]

    @pl.when(pl.program_id(0) == 0)
    def _():
        n = w_ref.shape[1]
        w_out[0:n] = jnp.concatenate([w_ref[0], w_ref[1]], axis=1)
        w_out[n : n + n // 2] = jnp.concatenate([w_ref[2, : n // 2], w_ref[2, n // 2 :]], axis=1)


def pack(q, k, v, g, w):
    n = w.shape[1]
    grid = 4
    cols = q.shape[1] // grid
    part = pl.BlockSpec((TOK, cols), lambda i: (0, i))
    out = pl.BlockSpec((DEVS // grid, 2, HALF, 128), lambda i: (i, 0, 0, 0))
    return pl.pallas_call(
        pack_kernel,
        grid=(grid,),
        out_shape=(
            SDS((DEVS, 2, HALF, 128), bf16),
            SDS((DEVS, 2, HALF, 128), bf16),
            SDS((n + n // 2, 128), bf16),
        ),
        in_specs=[part] * 4 + [whole(w.shape)],
        out_specs=(out, out, whole((n + n // 2, 128))),
        name="pack",
        cost_estimate=cost(4),
        compiler_params=params(),
    )(q, k, v, g, w)


def project_kernel(order_ref, x_ref, w_ref, g_ref, out_ref):
    qk = jnp.zeros((TXT, 128), f32)
    va = jnp.zeros((TXT, 128), f32)
    vb = jnp.zeros((TXT, 128), f32)
    blocks, n = w_ref.shape[0], x_ref.shape[2]
    for r in range(blocks):
        x = x_ref[order_ref[r]]
        qk += dot(x, w_ref[r, 0:n], 1, 0)
        va += dot(x[:, : n // 2], w_ref[r, n:], 1, 0)
        vb += dot(x[:, n // 2 :], w_ref[r, n:], 1, 0)
    v = va[:, :64] + vb[:, 64:]
    q = qk[:, :64].astype(bf16) * jnp.asarray(0.125, bf16)
    k = qk[:, 64:].astype(bf16)
    out_ref[...] = jnp.zeros_like(out_ref)
    out_ref[0:TXT] = jnp.concatenate([q, g_ref[...]], axis=1)
    out_ref[TXT_PAD : TXT_PAD + TXT] = jnp.concatenate([k, v.astype(bf16)], axis=1)


def project(order, x8, w, g):
    return pl.pallas_call(
        project_kernel,
        out_shape=SDS((2 * TXT_PAD, 128), bf16),
        in_specs=[pl.BlockSpec(memory_space=pltpu.SMEM)] + [pl.BlockSpec(memory_space=pltpu.VMEM)] * 3,
        out_specs=pl.BlockSpec(memory_space=pltpu.VMEM),
        name="project",
        cost_estimate=cost(3),
        compiler_params=params(),
    )(order, x8, w, g)


def key_chunks():
    return [(j, min(CHUNK, IMG - j)) for j in range(0, IMG, CHUNK)] + [(IMG, TXT_PAD)]


def attend_kernel(
    q_ref, tq_ref, k0_ref, k1_ref, tk_ref, out_ref, own_ref, ex_ref, dt_ref,
    kv, kz, vz, kvt, s_ref, e_ref, ds_ref, acc,
):
    step = pl.program_id(0)
    low = low_lanes()

    @pl.when(step == 0)
    def _():
        for j, n, src in ((0, IMG // 2, k0_ref), (IMG // 2, IMG // 2, k1_ref), (IMG, TXT_PAD, tk_ref)):
            x = src[...].reshape(n, 128)
            kz[j : j + n] = jnp.where(low, x, jnp.zeros_like(x))
            vz[j : j + n] = jnp.where(low, jnp.zeros_like(x), x)
            kvt[:, j : j + n] = x.T
        acc[...] = jnp.zeros_like(acc)

    qg = jnp.concatenate([q_ref[...].reshape(IMG_STEP, 128), tq_ref[...]], axis=0)
    padding = lax.broadcasted_iota(jnp.int32, (1, TXT_PAD), 1) >= TXT
    top = jnp.full((ROWS, 128), -jnp.inf, f32)
    for j, n in key_chunks():
        s = dot(qg, kz[j : j + n], 1, 1)
        if j == IMG:
            s = jnp.where(padding, -1e30, s)
        s_ref[:, j : j + n] = s
        for i in range(0, n, 128):
            top = jnp.maximum(top, s[:, i : i + 128])
    top = jnp.max(top, axis=1, keepdims=True) * LOG2E
    total = jnp.zeros((ROWS, 128), f32)
    for j, n in key_chunks():
        e = jnp.exp2(s_ref[:, j : j + n] * LOG2E - top)
        for i in range(0, n, 128):
            total = total + e[:, i : i + 128]
        e_ref[:, j : j + n] = e.astype(bf16)
    o = dot(kvt[...], e_ref[...], 1, 1).T
    inv = 1.0 / jnp.sum(total, axis=1, keepdims=True)
    o = (o * inv).astype(bf16).astype(f32)
    qf = qg.astype(f32)
    row_term = jnp.sum(jnp.where(low, 0.0, qf * o), axis=1, keepdims=True) * inv
    qs = jnp.where(low, qf, qf * inv).astype(bf16)
    qst = qs.T
    for j, n in key_chunks():
        dp = dot(qs, vz[j : j + n], 1, 1)
        e = e_ref[:, j : j + n]
        ds = (e.astype(f32) * (dp - row_term)).astype(bf16)
        ds_ref[:, j : j + n] = ds
        acc[0:64, j : j + n] += dot(qst[0:64], ds, 1, 0)
        acc[64:128, j : j + n] += dot(qst[64:128], e, 1, 0)
    dq = dot(kvt[...], ds_ref[...], 1, 1).T
    r = jnp.where(low, dq * 0.125, o).astype(bf16)
    out_ref[...] = r[:IMG_STEP].reshape(out_ref.shape)
    at = pl.multiple_of(IMG // 2 + TXT_STEP * step, 16)
    ex_ref[pl.ds(at, TXT_STEP)] = r[IMG_STEP:]

    @pl.when(step == STEPS - 1)
    def _():
        own_ref[...] = acc[:, : IMG // 2].T.reshape(own_ref.shape).astype(bf16)
        ex_ref[: IMG // 2] = acc[:, IMG // 2 : IMG].T.astype(bf16)
        dt = acc[:, IMG:].T
        dt_ref[...] = dt
        ex_ref[IMG // 2 + TXT_HALF :] = dt.astype(bf16)


def attend(received, tq, other, tk, name):
    half = (DEVS, HALF, 128)
    return pl.pallas_call(
        attend_kernel,
        grid=(STEPS,),
        out_shape=(SDS(half, bf16), SDS(half, bf16), SDS((EX_ROWS, 128), bf16), SDS((TXT_PAD, 128), f32)),
        in_specs=[
            pl.BlockSpec((SRC_STEP, None, HALF, 128), lambda i: (i, 0, 0, 0)),
            pl.BlockSpec((TXT_STEP, 128), lambda i: (i, 0)),
            pl.BlockSpec((DEVS, None, HALF, 128), lambda i: (0, 1, 0, 0)),
            whole(half),
            whole((TXT_PAD, 128)),
        ],
        out_specs=(
            pl.BlockSpec((SRC_STEP, HALF, 128), lambda i: (i, 0, 0)),
            whole(half),
            whole((EX_ROWS, 128)),
            whole((TXT_PAD, 128)),
        ),
        scratch_shapes=[
            pltpu.VMEM((8, 128), bf16),
            pltpu.VMEM((KEYS, 128), bf16),
            pltpu.VMEM((KEYS, 128), bf16),
            pltpu.VMEM((128, KEYS), bf16),
            pltpu.VMEM((ROWS, KEYS), f32),
            pltpu.VMEM((ROWS, KEYS), bf16),
            pltpu.VMEM((ROWS, KEYS), bf16),
            pltpu.VMEM((128, KEYS), f32),
        ],
        name=name,
        cost_estimate=cost(43),
        compiler_params=params(),
    )(received, tq, received, other, tk)


def finish_kernel(dqo_ref, own_ref, got_ref, y_ref):
    y_ref[:, :HALF] = dqo_ref[...]
    for i in range(DEVS):
        got = got_ref[HALF * i : HALF * i + HALF].astype(f32)
        y_ref[i, HALF:] = (own_ref[i].astype(f32) + got).astype(bf16)


def finish(dqo, own, got):
    return pl.pallas_call(
        finish_kernel,
        out_shape=SDS((DEVS, TOK, 128), bf16),
        in_specs=[pl.BlockSpec(memory_space=pltpu.VMEM)] * 3,
        out_specs=pl.BlockSpec(memory_space=pltpu.VMEM),
        name="finish_first",
        cost_estimate=cost(3),
        compiler_params=params(),
    )(dqo, own, got)


def text_rows(core, ex_ref, got_ref, dt_ref, scratch):
    tail = slice(IMG // 2, IMG // 2 + TXT_HALF)
    scratch[pl.ds(pl.multiple_of(TXT_HALF * core, 64), TXT_HALF)] = ex_ref[tail]
    scratch[pl.ds(pl.multiple_of(TXT_HALF * (1 - core), 64), TXT_HALF)] = got_ref[tail]
    sums = dt_ref[...] + got_ref[IMG // 2 + TXT_HALF :].astype(f32)
    return scratch[...], sums.astype(bf16)


def finish_last_kernel(
    ids_ref, dqo_ref, own_ref, ex0_ref, got0_ref, dt0_ref, ex1_ref, got1_ref, dt1_ref, w_ref, w_other_ref,
    y_ref, tg_ref, o_ref, rows_ref, g_own, g_other,
):
    core = ids_ref[0]
    low = low_lanes()
    y_ref[:, :HALF] = dqo_ref[...]
    for i in range(DEVS):
        got = got1_ref[HALF * i : HALF * i + HALF].astype(f32)
        y_ref[i, HALF:TOK] = (own_ref[i].astype(f32) + got).astype(bf16)
    qo0, kv0 = text_rows(core, ex0_ref, got0_ref, dt0_ref, rows_ref)
    qo1, kv1 = text_rows(core, ex1_ref, got1_ref, dt1_ref, rows_ref)
    first = core == 0
    for mine, target in ((first, g_own), (jnp.logical_not(first), g_other)):
        qo, kv = jnp.where(mine, qo0, qo1), jnp.where(mine, kv0, kv1)
        target[0] = jnp.where(low, qo, swap(kv))
        target[1] = jnp.where(low, swap(kv), jnp.zeros_like(kv))
        target[2] = jnp.where(low, jnp.zeros_like(kv), kv)
    o_ref[...] = jnp.where(first, qo0, qo1)[:TXT, 64:]
    tg_ref[0:80] = g_own[0, 0:80]
    tg_ref[80:160] = g_own[1, 0:80]
    here = pl.ds(pl.multiple_of(DX_ROWS * core, 16), DX_ROWS)
    n = w_ref.shape[1] * 2 // 3
    for r in range(w_ref.shape[0]):
        terms = []
        for grads, weights in ((g_own, w_ref), (g_other, w_other_ref)):
            qk = dot(grads[0, here], weights[r, 0:n], 1, 1)
            va = dot(grads[1, here], weights[r, n:], 1, 1)
            vb = dot(grads[2, here], weights[r, n:], 1, 1)
            terms.append(qk + jnp.concatenate([va, vb], axis=1))
        block = (terms[0] + terms[1]).astype(bf16)
        n4 = n // 4
        for part in range(4):
            piece = block[:, n4 * part : n4 * part + n4]
            piece = jnp.concatenate([piece, jnp.zeros((DX_ROWS, 128 - n4), bf16)], axis=1)
            y_ref[4 * ids_ref[1 + r] + part, TOK:] = piece


def finish_last(ids, dqo, own, ex0, got0, dt0, ex1, got1, dt1, w, w_other):
    v = pl.BlockSpec(memory_space=pltpu.VMEM)
    return pl.pallas_call(
        finish_last_kernel,
        out_shape=(SDS((DEVS, TOK + DX_ROWS, 128), bf16), SDS((160, 128), bf16), SDS((TXT, 64), bf16)),
        in_specs=[pl.BlockSpec(memory_space=pltpu.SMEM)] + [v] * 10,
        out_specs=(v, v, v),
        scratch_shapes=[
            pltpu.VMEM((TXT_PAD, 128), bf16),
            pltpu.VMEM((3, TXT_PAD, 128), bf16),
            pltpu.VMEM((3, TXT_PAD, 128), bf16),
        ],
        name="finish_last",
        cost_estimate=cost(5),
        compiler_params=params(),
    )(ids, dqo, own, ex0, got0, dt0, ex1, got1, dt1, w, w_other)


def unpack_kernel(z0_ref, z1_ref, o_ref, g_ref, dx_ref, acc):
    low = low_lanes()
    step = pl.program_id(0)
    for c in range(z0_ref.shape[0] // 2):
        cols = slice(128 * c, 128 * c + 128)
        for core in range(2):
            rows = slice(HALF * core, HALF * core + HALF)
            a, b = z0_ref[2 * c + core], z1_ref[2 * c + core]
            qo0, qo1, kv0, kv1 = a[:HALF], b[:HALF], a[HALF:TOK], b[HALF:TOK]
            g_ref[0, rows, cols] = jnp.where(low, qo0, swap(qo1))
            o_ref[rows, cols] = jnp.where(low, swap(qo0), qo1)
            g_ref[1, rows, cols] = jnp.where(low, kv0, swap(kv1))
            g_ref[2, rows, cols] = jnp.where(low, swap(kv0), kv1)
    for core in range(2):
        total = z1_ref[core, TOK:].astype(f32)
        for c in range(1, z0_ref.shape[0] // 2):
            total = total + z1_ref[2 * c + core, TOK:].astype(f32)
        rows = slice(DX_ROWS * core, DX_ROWS * core + DX_ROWS)

        @pl.when(step == 0)
        def _():
            acc[rows] = total

        @pl.when(step > 0)
        def _():
            acc[rows] += total

    dx_ref[...] = acc[: dx_ref.shape[0], : dx_ref.shape[1]]


def unpack(z0, z1, dx_cols):
    grid = 4
    cols = 2048 // grid
    return pl.pallas_call(
        unpack_kernel,
        grid=(grid,),
        out_shape=(SDS((TOK, 2048), bf16), SDS((3, TOK, 2048), bf16), SDS((TXT, dx_cols), f32)),
        in_specs=[
            pl.BlockSpec((DEVS // grid, TOK, 128), lambda i: (i, 0, 0)),
            pl.BlockSpec((DEVS // grid, TOK + DX_ROWS, 128), lambda i: (i, 0, 0)),
        ],
        out_specs=(
            pl.BlockSpec((TOK, cols), lambda i: (0, i)),
            pl.BlockSpec((3, TOK, cols), lambda i: (0, 0, i)),
            whole((TXT, dx_cols)),
        ),
        scratch_shapes=[pltpu.VMEM((2 * DX_ROWS, 128), f32)],
        name="unpack",
        cost_estimate=cost(4),
        compiler_params=params(),
    )(z0, z1)


def weight_grad_kernel(x_ref, tg_ref, out_ref):
    n = x_ref.shape[2]
    qk = jnp.zeros((n, 128), f32)
    v = jnp.zeros((n, 128), f32)
    for r in range(x_ref.shape[0]):
        qk += dot(x_ref[r], tg_ref[r, 0:TXT], 0, 0)
        v += dot(x_ref[r], tg_ref[r, 80 : 80 + TXT], 0, 0)
    out_ref[0] = qk[:, :64]
    out_ref[1] = qk[:, 64:]
    out_ref[2] = v[:, :64]


def weight_grad(x, tg):
    v = pl.BlockSpec(memory_space=pltpu.VMEM)
    return pl.pallas_call(
        weight_grad_kernel,
        out_shape=SDS((3, x.shape[2], 64), f32),
        in_specs=[v, v],
        out_specs=v,
        name="weight_grad",
        cost_estimate=cost(4),
        compiler_params=params(),
    )(x, tg)


def local(q_img, k_img, v_img, x_txt, w_txt, grad_img, grad_txt):
    seq, dp = lax.axis_index("seq"), lax.axis_index("dp")
    core = seq % 2
    dp_hi, dp_lo = dp // 4, dp % 4
    pair = [(i, i ^ 1) for i in range(DEVS)]
    across = [(i, i ^ 4) for i in range(8)]
    turns = [[(i, i // 4 * 4 + (i + k) % 4) for i in range(8)] for k in range(1, 4)]

    def gather_dp(x):
        both = jnp.stack([x, lax.ppermute(x, "dp", across)])
        return jnp.concatenate([both] + [lax.ppermute(both, "dp", t) for t in turns])

    order = jnp.stack(
        [(dp_hi ^ side) * 4 + (dp_lo + 4 - k) % 4 for k in range(4) for side in range(2)]
    ).astype(jnp.int32)

    x0, x1, w_own = pack(q_img[0], k_img[0], v_img[0], grad_img[0], w_txt)
    r0 = lax.all_to_all(x0, "seq", 0, 0, tiled=True)
    weights = gather_dp(w_own)
    x8 = x_txt[0].reshape(TXT, 8, -1).transpose(1, 0, 2)
    text = project(order, x8, weights, grad_txt[0])
    text_other = lax.ppermute(text, "seq", pair)
    weights_other = lax.ppermute(weights, "seq", pair)
    text0 = jnp.where(core == 0, text, text_other)
    text1 = jnp.where(core == 0, text_other, text)

    def phase(received, text_of_head, name):
        other = lax.ppermute(received[:, 1], "seq", pair)
        tq = lax.dynamic_slice_in_dim(text_of_head, TXT_HALF * core, TXT_HALF, 0)
        dqo, own, ex, dt = attend(received, tq, other, text_of_head[TXT_PAD:], name)
        return dqo, own, ex, dt, lax.ppermute(ex, "seq", pair)

    r1 = lax.all_to_all(x1, "seq", 0, 0, tiled=True)
    dqo0, own0, ex0, dt0, got0 = phase(r0, text0, "attend_first")
    z0 = lax.all_to_all(finish(dqo0, own0, got0), "seq", 0, 0, tiled=True)
    dqo1, own1, ex1, dt1, got1 = phase(r1, text1, "attend_second")

    xs = x8.reshape(2, 4, TXT, -1)
    kept = lax.dynamic_index_in_dim(xs, dp_hi, 0, keepdims=False)
    sent = lax.dynamic_index_in_dim(xs, 1 - dp_hi, 0, keepdims=False)
    both = jnp.stack([kept, lax.ppermute(sent, "dp", across)], axis=1)
    columns = [lax.dynamic_index_in_dim(both, (dp_lo + k) % 4, 0, keepdims=False) for k in range(4)]
    x_all = jnp.concatenate([columns[0]] + [lax.ppermute(c, "dp", t) for c, t in zip(columns[1:], turns)])

    ids = jnp.concatenate([core[None].astype(jnp.int32), order])
    y1, text_grads, o_txt = finish_last(
        ids, dqo1, own1, ex0, got0, dt0, ex1, got1, dt1, weights, weights_other
    )
    z1 = lax.all_to_all(y1, "seq", 0, 0, tiled=True)
    dw = weight_grad(x_all, gather_dp(text_grads))
    o_img, grads, dx = unpack(z0, z1, x_txt.shape[2] // DEVS)
    return o_img[None], o_txt[None], grads[:, None], dx[None], dw


def solution(mesh):
    in_specs = (
        P("dp", "seq", None),
        P("dp", "seq", None),
        P("dp", "seq", None),
        P("dp", None, None),
        P(None, "dp", "seq"),
        P("dp", "seq", None),
        P("dp", None, "seq"),
    )
    out_specs = (
        P("dp", "seq", None),
        P("dp", None, "seq"),
        P(None, "dp", "seq", None),
        P("dp", None, "seq"),
        P(None, "dp", "seq"),
    )
    return jax.shard_map(local, mesh=mesh, in_specs=in_specs, out_specs=out_specs, check_vma=False)
```

time: 709 us -> 264 us (0.37); the launches traced: 697 us -> 262 us
  other arithmetic: 164 us -> 1.04 us
  matrix products: 120 us -> 0 us
  Pallas kernels: 0 us -> 104 us
  waiting for transfers between devices: 165 us -> 80.2 us
  local copies, waits for them, and re-layouts: 102 us -> 18.9 us
  blocking collectives: 61.4 us -> 0 us
  between operations: 17.1 us -> 1.01 us
    unnamed x4 -> x0, waiting for transfers between devices: 157 us -> none
    unnamed x10 -> x0, other arithmetic: 137 us -> none
    dot_general x57 -> x0, matrix products: 120 us -> none  [the longest x9 27.6 us: block_pass(): jnp.einsum('gbd,gkd->gbk', cotangent, values, preferred_element_type=jnp....]
    pallas_call x0 -> x8, Pallas kernels: none -> 104 us  [the longest x2 81.9 us: attend(): pl.pallas_call(attend_kernel, grid=(STEPS,), out_shape=(SDS(half, bf16),...]
    ppermute x0 -> x18, waiting for transfers between devices: none -> 80.2 us  [the longest x1 34.8 us: local(): both = jnp.stack([kept, lax.ppermute(sent, 'dp', across)], axis=1)]
    all_gather x1 -> x0, blocking collectives: 61.4 us -> none  [local(): full_weights = lax.all_gather(w_txt, 'dp', axis=1, tiled=True)]
    unnamed x100 -> x47, local copies, waits for them, and re-layouts: 65.6 us -> 13.6 us
    all_to_all x8 -> x4, starting transfers between devices: 61.6 us -> 31.9 us  [the longest x1 8.89 us: local(): r0 = lax.all_to_all(x0, 'seq', 0, 0, tiled=True)]
  transfers between devices with their start and end apart: 10 -> 22, of which waited for: 4 -> 11; matrix products, arithmetic and copies ran while one was open for 28% -> 4% of each run, Pallas kernels for 0% -> 36%
where the time goes in v1:
time: 264 us; the launch traced here: 262 us
  Pallas kernels  104 us (39%)
  waiting for transfers between devices  80.2 us (30%)
  starting transfers between devices  56.9 us (22%)
  local copies, waits for them, and re-layouts  18.9 us (7%)
    pallas_call x2, Pallas kernels, attend(): pl.pallas_call(attend_kernel, grid=(STEPS,), out_shape=(SDS(half, bf16),...  81.9 us
    ppermute x1, waiting for transfers between devices, local(): both = jnp.stack([kept, lax.ppermute(sent, 'dp', across)], axis=1)  34.8 us
    ppermute x2, waiting for transfers between devices, gather_dp(): both = jnp.stack([x, lax.ppermute(x, 'dp', across)])  25.7 us
    unnamed x47, local copies, waits for them, and re-layouts  13.6 us
    ppermute x6, waiting for transfers between devices, gather_dp(): lax.ppermute(both, 'dp', t)  13 us
    ppermute x2, starting transfers between devices, gather_dp(): both = jnp.stack([x, lax.ppermute(x, 'dp', across)])  9.08 us
    all_to_all x1, starting transfers between devices, local(): r0 = lax.all_to_all(x0, 'seq', 0, 0, tiled=True)  8.89 us
    ppermute x6, starting transfers between devices, gather_dp(): lax.ppermute(both, 'dp', t)  8.89 us
  transfers between devices with their start and end apart: 22, of which 11 were waited for; matrix products, arithmetic and copies ran while one was open for 4% of the time, Pallas kernels for 36%

profile of v1, /device:TPU:8, one launch (start us, length us, event | category | flops | bytes accessed | tf_op | source)
XLA Modules:
  0.0 261.6 jit_solution(16789300553499267363)
XLA Ops:
  0.6 1.7 copy.37.w_ref
  2.4 4.4 %pack.1 = (bf16[32,2,64,128]{3,2,1,0:T(8,128)(2,1)}, bf16[32,2,64,128]{3,2,1,0:T(8,128)(2,1)}, bf16[456,128]{1,0:T(8,128)(2,1)}) custom-call(bf16[128,2048]{1,0:T(8,128)(2,1)} %bitcast.63, bf16[128,2048]{1,0:T(8,128)(2,1)} %bitcast.64, bf16[128,2048]{1,0:T(8,128)(2,1)} %bitcast.65, bf16[128,2048]{1,0:T(8,128)(2,1)} %bitcast.66, bf16[3,304,64]{2,1,0:T(8,128)(2,1)} %copy.37.w_ref), custom_call_target="tpu_custom_call" | custom-call | flops 4600000000 | bytes 1048576 | tf_op jit(solution)/shard_map/pack/pallas_call | solution.py:84
  6.9 8.9 %all-to-all-start = ((bf16[32,2,64,128]{3,2,1,0:T(8,128)(2,1)}), bf16[32,2,64,128]{3,2,1,0:T(8,128)(2,1)S(1)}, u32[]{:S(2)}, u32[]{:S(2)}) async-start(bf16[32,2,64,128]{3,2,1,0:T(8,128)(2,1)} %get-tuple-element.22), calls=%async_computation | async-start | bytes 2097152 | tf_op jit(solution)/shard_map/all_to_all | solution.py:409
  15.8 4.6 %collective-permute-start = (bf16[456,128]{1,0:T(8,128)(2,1)S(1)}, bf16[456,128]{1,0:T(8,128)(2,1)S(1)}, u32[]{:S(2)}, u32[]{:S(2)}) collective-permute-start(bf16[456,128]{1,0:T(8,128)(2,1)S(1)} %copy-done.5), channel_id=1, source_target_pairs={{0,128},{32,160},{64,192},{96,224},{128,0},{160,32},{192,64},{224,... | collective-permute-start | bytes 350216 | tf_op jit(solution)/shard_map/ppermute | solution.py:401
  20.4 23.0 %collective-permute-done = bf16[456,128]{1,0:T(8,128)(2,1)S(1)} collective-permute-done((bf16[456,128]{1,0:T(8,128)(2,1)S(1)}, bf16[456,128]{1,0:T(8,128)(2,1)S(1)}, u32[]{:S(2)}, u32[]{:S(2)}) %collective-permute-start) | collective-permute-done | bytes 116768 | tf_op jit(solution)/shard_map/ppermute | solution.py:401
  43.4 1.7 collective-permute-start.1
  45.0 0.7 copy.39
  46.3 0.8 copy.50
  48.2 2.3 collective-permute-start.2
  50.9 9.8 %collective-permute-done.2 = bf16[2,456,128]{2,1,0:T(8,128)(2,1)S(1)} collective-permute-done((bf16[2,456,128]{2,1,0:T(8,128)(2,1)S(1)}, bf16[2,456,128]{2,1,0:T(8,128)(2,1)S(1)}, u32[]{:S(2)}, u32[]{:S(2)}) %collective-permute-start.2) | collective-permute-done | bytes 233504 | tf_op jit(solution)/shard_map/ppermute | solution.py:402
  60.9 0.8 copy-done.11
  61.7 2.6 project.1
  64.3 7.7 %all-to-all-start.2 = ((bf16[32,2,64,128]{3,2,1,0:T(8,128)(2,1)}), bf16[32,2,64,128]{3,2,1,0:T(8,128)(2,1)S(1)}, u32[]{:S(2)}, u32[]{:S(2)}) async-start(bf16[32,2,64,128]{3,2,1,0:T(8,128)(2,1)} %get-tuple-element.27), calls=%async_computation.2 | async-start | bytes 2097152 | tf_op jit(solution)/shard_map/all_to_all | solution.py:424
  72.1 0.6 slice.17.tk_ref
  73.3 0.8 copy-done.15
  74.1 40.9 %attend_first.1 = (bf16[32,64,128]{2,1,0:T(8,128)(2,1)}, bf16[32,64,128]{2,1,0:T(8,128)(2,1)}, bf16[2240,128]{1,0:T(8,128)(2,1)}, f32[128,128]{1,0:T(8,128)}) custom-call(bf16[32,2,64,128]{3,2,1,0:T(8,128)(2,1)} %copy-done, bf16[64,128]{1,0:T(8,128)(2,1)} %constant_dynamic-slice_fusion.1.tq_ref, bf16[32,2,64,128]{3,2,1,0:T(8,128)(2,1)} %copy-done, ...), custom_call_target="tpu_custom_call" | custom-call | flops 49450000384 | bytes 1048576 | tf_op jit(solution)/shard_map/attend_first/pallas_call | solution.py:198
  115.9 0.6 slice.19.tk_ref
  117.3 0.8 copy-done.13
  118.1 2.5 finish_first.1
  120.6 7.8 %all-to-all-start.1 = ((bf16[32,128,128]{2,1,0:T(8,128)(2,1)}), bf16[32,128,128]{2,1,0:T(8,128)(2,1)S(1)}, u32[]{:S(2)}, u32[]{:S(2)}) async-start(bf16[32,128,128]{2,1,0:T(8,128)(2,1)} %finish_first.1), calls=%async_computation.1 | async-start | bytes 2097152 | tf_op jit(solution)/shard_map/all_to_all | solution.py:426
  128.4 0.8 copy-done.16
  129.2 40.9 %attend_second.1 = (bf16[32,64,128]{2,1,0:T(8,128)(2,1)}, bf16[32,64,128]{2,1,0:T(8,128)(2,1)}, bf16[2240,128]{1,0:T(8,128)(2,1)}, f32[128,128]{1,0:T(8,128)}) custom-call(bf16[32,2,64,128]{3,2,1,0:T(8,128)(2,1)} %copy-done.1, bf16[64,128]{1,0:T(8,128)(2,1)} %constant_dynamic-slice_fusion.tq_ref, bf16[32,2,64,128]{3,2,1,0:T(8,128)(2,1)} %copy-done.1, ...), custom_call_target="tpu_custom_call" | custom-call | flops 49450000384 | bytes 1048576 | tf_op jit(solution)/shard_map/attend_second/pallas_call | solution.py:198
  170.9 1.5 collective-permute-done.8.got1_ref
  172.4 0.8 copy-done.14
  173.3 5.1 %finish_last.1 = (bf16[32,176,128]{2,1,0:T(8,128)(2,1)}, bf16[160,128]{1,0:T(8,128)(2,1)}, bf16[77,64]{1,0:T(8,128)(2,1)}) custom-call(s32[9]{0:T(128)} %concatenate.16.ids_ref, bf16[32,64,128]{2,1,0:T(8,128)(2,1)} %get-tuple-element.28.dqo_ref, bf16[32,64,128]{2,1,0:T(8,128)(2,1)} %get-tuple-element.29.own_ref, ...), custom_call_target="tpu_custom_call" | custom-call | flops 5750000128 | bytes 1048576 | tf_op jit(solution)/shard_map/finish_last/pallas_call | solution.py:298
  178.4 1.0 copy-done.4
  179.4 7.5 %all-to-all-start.3 = ((bf16[32,176,128]{2,1,0:T(8,128)(2,1)}), bf16[32,176,128]{2,1,0:T(8,128)(2,1)S(1)}, u32[]{:S(2)}, u32[]{:S(2)}) async-start(bf16[32,176,128]{2,1,0:T(8,128)(2,1)} %get-tuple-element.33), calls=%async_computation.3 | async-start | bytes 2883584 | tf_op jit(solution)/shard_map/all_to_all | solution.py:440
  187.0 1.5 collective-permute-start.10
  188.6 34.8 %collective-permute-done.10 = bf16[4,77,304]{2,1,0:T(8,128)(2,1)S(1)} collective-permute-done((bf16[4,77,304]{2,1,0:T(8,128)(2,1)S(1)}, bf16[4,77,304]{2,1,0:T(8,128)(2,1)S(1)}, u32[]{:S(2)}, u32[]{:S(2)}) %collective-permute-start.10) | collective-permute-done | bytes 187296 | tf_op jit(solution)/shard_map/ppermute | solution.py:432
  223.9 1.6 collective-permute-start.12
  225.5 2.5 collective-permute-start.13
  228.0 1.7 collective-permute-done.11
  229.7 1.9 collective-permute-done.12
  231.7 1.2 collective-permute-done.13
  232.9 0.9 pad_maximum_fusion.x_ref
  233.8 4.5 %collective-permute-start.14 = (bf16[160,128]{1,0:T(8,128)(2,1)S(1)}, bf16[160,128]{1,0:T(8,128)(2,1)S(1)}, u32[]{:S(2)}, u32[]{:S(2)}) collective-permute-start(bf16[160,128]{1,0:T(8,128)(2,1)S(1)} %copy-done.7), channel_id=1, source_target_pairs={{0,128},{32,160},{64,192},{96,224},{128,0},{160,32},{192,64},{224,... | collective-permute-start | bytes 122888 | tf_op jit(solution)/shard_map/ppermute | solution.py:401
  238.3 0.7 copy.42
  239.0 2.7 %collective-permute-done.14 = bf16[160,128]{1,0:T(8,128)(2,1)S(1)} collective-permute-done((bf16[160,128]{1,0:T(8,128)(2,1)S(1)}, bf16[160,128]{1,0:T(8,128)(2,1)S(1)}, u32[]{:S(2)}, u32[]{:S(2)}) %collective-permute-start.14) | collective-permute-done | bytes 40992 | tf_op jit(solution)/shard_map/ppermute | solution.py:401
  241.7 0.9 collective-permute-start.17
  242.6 1.5 collective-permute-start.16
  244.1 2.1 collective-permute-start.15
  246.2 3.0 %collective-permute-done.15 = bf16[2,160,128]{2,1,0:T(8,128)(2,1)S(1)} collective-permute-done((bf16[2,160,128]{2,1,0:T(8,128)(2,1)S(1)}, bf16[2,160,128]{2,1,0:T(8,128)(2,1)S(1)}, u32[]{:S(2)}, u32[]{:S(2)}) %collective-permute-start.15) | collective-permute-done | bytes 81952 | tf_op jit(solution)/shard_map/ppermute | solution.py:402
  249.3 0.7 copy-done.12
  250.0 2.8 %weight_grad.1 = f32[3,304,64]{2,1,0:T(8,128)} custom-call(bf16[8,77,304]{2,1,0:T(8,128)(2,1)} %pad_maximum_fusion.x_ref, bf16[8,160,128]{2,1,0:T(8,128)(2,1)} %copy-done.12), custom_call_target="tpu_custom_call" | custom-call | flops 4600000000 | bytes 1048576 | tf_op jit(solution)/shard_map/weight_grad/pallas_call | solution.py:381
  252.8 2.0 copy.45
  254.7 1.1 copy-done.3
  255.9 4.2 %unpack.1 = (bf16[128,2048]{1,0:T(8,128)(2,1)}, bf16[3,128,2048]{2,1,0:T(8,128)(2,1)}, f32[77,76]{1,0:T(8,128)}) custom-call(bf16[32,128,128]{2,1,0:T(8,128)(2,1)} %copy-done.4, bf16[32,176,128]{2,1,0:T(8,128)(2,1)} %copy-done.3), custom_call_target="tpu_custom_call" | custom-call | flops 4600000000 | bytes 1048576 | tf_op jit(solution)/shard_map/unpack/pallas_call | solution.py:347
  260.1 1.5 copy.44
  (69 shorter events, 5.9 us)
Async XLA Ops:
  6.8 8.9 %copy-start.5 = (bf16[456,128]{1,0:T(8,128)(2,1)S(1)}, bf16[456,128]{1,0:T(8,128)(2,1)}, u32[]{:S(2)}) copy-start(bf16[456,128]{1,0:T(8,128)(2,1)} %get-tuple-element.23) | copy-start | bytes 350212
  6.8 38.2 %copy-start.10 = (bf16[1,77,64]{1,2,0:T(8,128)(2,1)S(1)}, bf16[1,77,64]{1,2,0:T(8,128)(2,1)}, u32[]{:S(2)}) copy-start(bf16[1,77,64]{1,2,0:T(8,128)(2,1)} %param.13) | copy-start | bytes 29572
  6.8 38.9 %copy-start.6 = (bf16[1,77,2432]{2,1,0:T(8,128)(2,1)S(1)}, bf16[1,77,2432]{2,1,0:T(8,128)(2,1)}, u32[]{:S(2)}) copy-start(bf16[1,77,2432]{2,1,0:T(8,128)(2,1)} %param.10) | copy-start | bytes 1123588
  6.9 53.9 %all-to-all-start = ((bf16[32,2,64,128]{3,2,1,0:T(8,128)(2,1)}), bf16[32,2,64,128]{3,2,1,0:T(8,128)(2,1)S(1)}, u32[]{:S(2)}, u32[]{:S(2)}) async-start(bf16[32,2,64,128]{3,2,1,0:T(8,128)(2,1)} %get-tuple-element.22), calls=%async_computation | async-start | bytes 2097152 | tf_op jit(solution)/shard_map/all_to_all | solution.py:409
  15.8 27.6 %collective-permute-start = (bf16[456,128]{1,0:T(8,128)(2,1)S(1)}, bf16[456,128]{1,0:T(8,128)(2,1)S(1)}, u32[]{:S(2)}, u32[]{:S(2)}) collective-permute-start(bf16[456,128]{1,0:T(8,128)(2,1)S(1)} %copy-done.5), channel_id=1, source_target_pairs={{0,128},{32,160},{64,192},{96,224},{128,0},{160,32},{192,64},{224,... | collective-permute-start | bytes 350216 | tf_op jit(solution)/shard_map/ppermute | solution.py:401
  43.4 7.5 %collective-permute-start.1 = (bf16[2,456,128]{2,1,0:T(8,128)(2,1)S(1)}, bf16[2,456,128]{2,1,0:T(8,128)(2,1)S(1)}, u32[]{:S(2)}, u32[]{:S(2)}) collective-permute-start(bf16[2,456,128]{2,1,0:T(8,128)(2,1)S(1)} %pad_maximum_fusion.1), channel_id=1, source_target_pairs={{0,32},{32,64},{64,96},{96,0},{128,160},{160,192},{192,224},{224,1... | collective-permute-start | bytes 700424 | tf_op jit(solution)/shard_map/ppermute | solution.py:402
  47.8 12.9 %collective-permute-start.3 = (bf16[2,456,128]{2,1,0:T(8,128)(2,1)S(1)}, bf16[2,456,128]{2,1,0:T(8,128)(2,1)S(1)}, u32[]{:S(2)}, u32[]{:S(2)}) collective-permute-start(bf16[2,456,128]{2,1,0:T(8,128)(2,1)S(1)} %pad_maximum_fusion.1), channel_id=1, source_target_pairs={{0,96},{32,0},{64,32},{96,64},{128,224},{160,128},{192,160},{224,1... | collective-permute-start | bytes 700424 | tf_op jit(solution)/shard_map/ppermute | solution.py:402
  48.2 12.4 %collective-permute-start.2 = (bf16[2,456,128]{2,1,0:T(8,128)(2,1)S(1)}, bf16[2,456,128]{2,1,0:T(8,128)(2,1)S(1)}, u32[]{:S(2)}, u32[]{:S(2)}) collective-permute-start(bf16[2,456,128]{2,1,0:T(8,128)(2,1)S(1)} %pad_maximum_fusion.1), channel_id=1, source_target_pairs={{0,64},{32,96},{64,0},{96,32},{128,192},{160,224},{192,128},{224,1... | collective-permute-start | bytes 700424 | tf_op jit(solution)/shard_map/ppermute | solution.py:402
  60.7 0.9 copy-start.11
  60.8 3.5 %copy-start = (bf16[32,2,64,128]{3,2,1,0:T(8,128)(2,1)}, bf16[32,2,64,128]{3,2,1,0:T(8,128)(2,1)S(1)}, u32[]{:S(2)}) copy-start(bf16[32,2,64,128]{3,2,1,0:T(8,128)(2,1)S(1)} %all-to-all-done.q_ref.k0_ref) | copy-start | bytes 3145732
  60.8 12.5 %collective-permute-start.5 = (bf16[32,64,128]{2,1,0:T(8,128)(2,1)S(1)}, bf16[32,64,128]{2,1,0:T(8,128)(2,1)S(1)}, u32[]{:S(2)}, u32[]{:S(2)}) collective-permute-start(bf16[32,64,128]{2,1,0:T(8,128)(2,1)S(1)} %slice_bitcast_fusion.1), channel_id=1, source_target_pairs={{0,1},{1,0},{2,3},{3,2},{4,5},{5,4},{6,7},{7,6},{8,9},{9,8},{10,11... | collective-permute-start | bytes 1572872 | tf_op jit(solution)/shard_map/ppermute | solution.py:419
  64.3 7.8 %copy-start.8 = (bf16[256,128]{1,0:T(8,128)(2,1)S(1)}, bf16[256,128]{1,0:T(8,128)(2,1)}, u32[]{:S(2)}) copy-start(bf16[256,128]{1,0:T(8,128)(2,1)} %project.1) | copy-start | bytes 196612
  64.3 7.8 %collective-permute-start.4 = (bf16[256,128]{1,0:T(8,128)(2,1)}, bf16[256,128]{1,0:T(8,128)(2,1)S(1)}, u32[]{:S(2)}, u32[]{:S(2)}) collective-permute-start(bf16[256,128]{1,0:T(8,128)(2,1)} %project.1), channel_id=1, source_target_pairs={{0,1},{1,0},{2,3},{3,2},{4,5},{5,4},{6,7},{7,6},{8,9},{9,8},{10,11... | collective-permute-start | bytes 196616 | tf_op jit(solution)/shard_map/ppermute | solution.py:413
  64.3 50.9 %all-to-all-start.2 = ((bf16[32,2,64,128]{3,2,1,0:T(8,128)(2,1)}), bf16[32,2,64,128]{3,2,1,0:T(8,128)(2,1)S(1)}, u32[]{:S(2)}, u32[]{:S(2)}) async-start(bf16[32,2,64,128]{3,2,1,0:T(8,128)(2,1)} %get-tuple-element.27), calls=%async_computation.2 | async-start | bytes 2097152 | tf_op jit(solution)/shard_map/all_to_all | solution.py:424
  73.3 0.8 copy-start.15
  115.0 2.3 collective-permute-start.6
  115.2 5.4 %copy-start.1 = (bf16[32,2,64,128]{3,2,1,0:T(8,128)(2,1)}, bf16[32,2,64,128]{3,2,1,0:T(8,128)(2,1)S(1)}, u32[]{:S(2)}) copy-start(bf16[32,2,64,128]{3,2,1,0:T(8,128)(2,1)S(1)} %all-to-all-done.2.q_ref.k0_ref) | copy-start | bytes 3145732
  115.3 13.2 %collective-permute-start.7 = (bf16[32,64,128]{2,1,0:T(8,128)(2,1)S(1)}, bf16[32,64,128]{2,1,0:T(8,128)(2,1)S(1)}, u32[]{:S(2)}, u32[]{:S(2)}) collective-permute-start(bf16[32,64,128]{2,1,0:T(8,128)(2,1)S(1)} %slice_bitcast_fusion), channel_id=1, source_target_pairs={{0,1},{1,0},{2,3},{3,2},{4,5},{5,4},{6,7},{7,6},{8,9},{9,8},{10,11... | collective-permute-start | bytes 1572872 | tf_op jit(solution)/shard_map/ppermute | solution.py:419
  115.8 55.2 %collective-permute-start.9 = (bf16[8,456,128]{2,1,0:T(8,128)(2,1)}, bf16[8,456,128]{2,1,0:T(8,128)(2,1)}, u32[]{:S(2)}, u32[]{:S(2)}) collective-permute-start(bf16[8,456,128]{2,1,0:T(8,128)(2,1)} %copy-done.11), channel_id=1, source_target_pairs={{0,1},{1,0},{2,3},{3,2},{4,5},{5,4},{6,7},{7,6},{8,9},{9,8},{10,11... | collective-permute-start | bytes 2801672 | tf_op jit(solution)/shard_map/ppermute | solution.py:414
  117.3 0.8 copy-start.13
  120.6 57.8 %all-to-all-start.1 = ((bf16[32,128,128]{2,1,0:T(8,128)(2,1)}), bf16[32,128,128]{2,1,0:T(8,128)(2,1)S(1)}, u32[]{:S(2)}, u32[]{:S(2)}) async-start(bf16[32,128,128]{2,1,0:T(8,128)(2,1)} %finish_first.1), calls=%async_computation.1 | async-start | bytes 2097152 | tf_op jit(solution)/shard_map/all_to_all | solution.py:426
  128.4 0.8 copy-start.16
  170.2 2.3 collective-permute-start.8
  172.4 0.8 copy-start.14
  178.4 1.0 copy-start.4
  178.4 8.5 %copy-start.2 = (bf16[77,8,304]{2,0,1:T(8,128)(2,1)S(1)}, bf16[77,8,304]{2,0,1:T(8,128)(2,1)}, u32[]{:S(2)}) copy-start(bf16[77,8,304]{2,0,1:T(8,128)(2,1)} %copy.50) | copy-start | bytes 1123588
  179.4 75.3 %all-to-all-start.3 = ((bf16[32,176,128]{2,1,0:T(8,128)(2,1)}), bf16[32,176,128]{2,1,0:T(8,128)(2,1)S(1)}, u32[]{:S(2)}, u32[]{:S(2)}) async-start(bf16[32,176,128]{2,1,0:T(8,128)(2,1)} %get-tuple-element.33), calls=%async_computation.3 | async-start | bytes 2883584 | tf_op jit(solution)/shard_map/all_to_all | solution.py:440
  187.0 46.8 %copy-start.7 = (bf16[160,128]{1,0:T(8,128)(2,1)S(1)}, bf16[160,128]{1,0:T(8,128)(2,1)}, u32[]{:S(2)}) copy-start(bf16[160,128]{1,0:T(8,128)(2,1)} %get-tuple-element.38) | copy-start | bytes 122884
  187.0 51.3 %copy-start.9 = (bf16[77,64]{1,0:T(8,128)(2,1)S(1)}, bf16[77,64]{1,0:T(8,128)(2,1)}, u32[]{:S(2)}) copy-start(bf16[77,64]{1,0:T(8,128)(2,1)} %get-tuple-element.35) | copy-start | bytes 29572
  187.0 36.4 %collective-permute-start.10 = (bf16[4,77,304]{2,1,0:T(8,128)(2,1)S(1)}, bf16[4,77,304]{2,1,0:T(8,128)(2,1)S(1)}, u32[]{:S(2)}, u32[]{:S(2)}) collective-permute-start(bf16[4,77,304]{2,1,0:T(8,128)(2,1)S(1)} %get-tuple-element.58), channel_id=1, source_target_pairs={{0,128},{32,160},{64,192},{96,224},{128,0},{160,32},{192,64},{224,... | collective-permute-start | bytes 561800 | tf_op jit(solution)/shard_map/ppermute | solution.py:432
  223.5 6.2 %collective-permute-start.11 = (bf16[2,77,304]{2,1,0:T(8,128)(2,1)S(1)}, bf16[2,77,304]{2,1,0:T(8,128)(2,1)S(1)}, u32[]{:S(2)}, u32[]{:S(2)}) collective-permute-start(bf16[2,77,304]{2,1,0:T(8,128)(2,1)S(1)} %get-tuple-element.55), channel_id=1, source_target_pairs={{0,32},{32,64},{64,96},{96,0},{128,160},{160,192},{192,224},{224,1... | collective-permute-start | bytes 280904 | tf_op jit(solution)/shard_map/ppermute | solution.py:434
  223.9 7.8 %collective-permute-start.12 = (bf16[2,77,304]{2,1,0:T(8,128)(2,1)S(1)}, bf16[2,77,304]{2,1,0:T(8,128)(2,1)S(1)}, u32[]{:S(2)}, u32[]{:S(2)}) collective-permute-start(bf16[2,77,304]{2,1,0:T(8,128)(2,1)S(1)} %get-tuple-element.56), channel_id=1, source_target_pairs={{0,64},{32,96},{64,0},{96,32},{128,192},{160,224},{192,128},{224,1... | collective-permute-start | bytes 280904 | tf_op jit(solution)/shard_map/ppermute | solution.py:434
  225.5 7.4 %collective-permute-start.13 = (bf16[2,77,304]{2,1,0:T(8,128)(2,1)S(1)}, bf16[2,77,304]{2,1,0:T(8,128)(2,1)S(1)}, u32[]{:S(2)}, u32[]{:S(2)}) collective-permute-start(bf16[2,77,304]{2,1,0:T(8,128)(2,1)S(1)} %get-tuple-element.57), channel_id=1, source_target_pairs={{0,96},{32,0},{64,32},{96,64},{128,224},{160,128},{192,160},{224,1... | collective-permute-start | bytes 280904 | tf_op jit(solution)/shard_map/ppermute | solution.py:434
  233.8 7.9 %collective-permute-start.14 = (bf16[160,128]{1,0:T(8,128)(2,1)S(1)}, bf16[160,128]{1,0:T(8,128)(2,1)S(1)}, u32[]{:S(2)}, u32[]{:S(2)}) collective-permute-start(bf16[160,128]{1,0:T(8,128)(2,1)S(1)} %copy-done.7), channel_id=1, source_target_pairs={{0,128},{32,160},{64,192},{96,224},{128,0},{160,32},{192,64},{224,... | collective-permute-start | bytes 122888 | tf_op jit(solution)/shard_map/ppermute | solution.py:401
  241.7 7.5 %collective-permute-start.17 = (bf16[2,160,128]{2,1,0:T(8,128)(2,1)S(1)}, bf16[2,160,128]{2,1,0:T(8,128)(2,1)S(1)}, u32[]{:S(2)}, u32[]{:S(2)}) collective-permute-start(bf16[2,160,128]{2,1,0:T(8,128)(2,1)S(1)} %pad_maximum_fusion.2), channel_id=1, source_target_pairs={{0,96},{32,0},{64,32},{96,64},{128,224},{160,128},{192,160},{224,1... | collective-permute-start | bytes 245768 | tf_op jit(solution)/shard_map/ppermute | solution.py:402
  242.6 6.6 %collective-permute-start.16 = (bf16[2,160,128]{2,1,0:T(8,128)(2,1)S(1)}, bf16[2,160,128]{2,1,0:T(8,128)(2,1)S(1)}, u32[]{:S(2)}, u32[]{:S(2)}) collective-permute-start(bf16[2,160,128]{2,1,0:T(8,128)(2,1)S(1)} %pad_maximum_fusion.2), channel_id=1, source_target_pairs={{0,64},{32,96},{64,0},{96,32},{128,192},{160,224},{192,128},{224,1... | collective-permute-start | bytes 245768 | tf_op jit(solution)/shard_map/ppermute | solution.py:402
  244.1 5.1 %collective-permute-start.15 = (bf16[2,160,128]{2,1,0:T(8,128)(2,1)S(1)}, bf16[2,160,128]{2,1,0:T(8,128)(2,1)S(1)}, u32[]{:S(2)}, u32[]{:S(2)}) collective-permute-start(bf16[2,160,128]{2,1,0:T(8,128)(2,1)S(1)} %pad_maximum_fusion.2), channel_id=1, source_target_pairs={{0,32},{32,64},{64,96},{96,0},{128,160},{160,192},{192,224},{224,1... | collective-permute-start | bytes 245768 | tf_op jit(solution)/shard_map/ppermute | solution.py:402
  249.2 0.7 copy-start.12
  254.7 1.1 copy-start.3

commit v2 on v0

v2 whole, which is shorter than its diff:
```python
import functools

import jax
import jax.numpy as jnp
from jax import lax
from jax.experimental import pallas as pl
from jax.experimental.pallas import tpu as pltpu
from jax.sharding import PartitionSpec as P

bf16, f32 = jnp.bfloat16, jnp.float32
SDS = jax.ShapeDtypeStruct
LOG2E = 1.4426950408889634
CHIPS = 16
TOK = 128
MINE = CHIPS * TOK
IMG = 2 * MINE
TXT = 77
TXT_ROWS = 80
TXT_PAD = 128
TXT_HALF = TXT_PAD // 2
KEYS = IMG + TXT_PAD
STEPS = 4
SRC_STEP = CHIPS // STEPS
ROWS = SRC_STEP * TOK
TAIL = TXT_HALF + TXT_PAD
CHUNK = 1024
VMEM = 40 << 20
IN_VMEM = pl.BlockSpec(memory_space=pltpu.VMEM)
IN_SMEM = pl.BlockSpec(memory_space=pltpu.SMEM)


def dot(a, b, ca, cb):
    return lax.dot_general(a, b, (((ca,), (cb,)), ((), ())), preferred_element_type=f32)


def low_lanes():
    return lax.broadcasted_iota(jnp.int32, (1, 128), 1) < 64


def swap(x):
    return jnp.concatenate([x[..., 64:], x[..., :64]], axis=-1)


def params():
    return pltpu.CompilerParams(vmem_limit_bytes=VMEM)


def whole(shape):
    return pl.BlockSpec(shape, lambda *i: (0,) * len(shape))


def cost(us):
    return pl.CostEstimate(flops=int(us * 1.15e9), bytes_accessed=1 << 20, transcendentals=0)


def pack_kernel(phase, q_ref, k_ref, v_ref, g_ref, x_ref):
    low = low_lanes()
    for c in range(q_ref.shape[1] // 128):
        cols = slice(128 * c, 128 * c + 128)
        q = q_ref[:, cols] * jnp.asarray(0.125, bf16)
        k, v, g = k_ref[:, cols], v_ref[:, cols], g_ref[:, cols]
        for which, (a, b) in enumerate(((q, g), (k, v))):
            if phase == 0:
                x_ref[c, which] = jnp.where(low, a, swap(b))
            else:
                x_ref[c, which] = jnp.where(low, swap(a), b)


def pack(phase, q, k, v, g, grid):
    part = pl.BlockSpec((TOK, q.shape[1] // grid), lambda i: (0, i))
    return pl.pallas_call(
        functools.partial(pack_kernel, phase),
        grid=(grid,),
        out_shape=SDS((CHIPS, 2, TOK, 128), bf16),
        in_specs=[part] * 4,
        out_specs=pl.BlockSpec((CHIPS // grid, 2, TOK, 128), lambda i: (i, 0, 0, 0)),
        name=("pack_first", "pack_second")[phase],
        cost_estimate=cost(3),
        compiler_params=params(),
    )(q, k, v, g)


def project_kernel(ids_ref, x_ref, w_ref, g_ref, out_ref):
    total = jnp.zeros((TXT, w_ref.shape[1]), f32)
    for r in range(w_ref.shape[0]):
        total += dot(x_ref[ids_ref[1 + r]], w_ref[r], 1, 1)
    total = total.astype(bf16)
    q = total[:, :64] * jnp.asarray(0.125, bf16)
    out_ref[...] = jnp.zeros_like(out_ref)
    out_ref[0:TXT] = jnp.concatenate([q, g_ref[...]], axis=1)
    out_ref[TXT_PAD : TXT_PAD + TXT] = total[:, 64:]


def project(ids, x8, w, g):
    return pl.pallas_call(
        project_kernel,
        out_shape=SDS((2 * TXT_PAD, 128), bf16),
        in_specs=[IN_SMEM] + [IN_VMEM] * 3,
        out_specs=IN_VMEM,
        name="project",
        cost_estimate=cost(3),
        compiler_params=params(),
    )(ids, x8, w, g)


def key_chunks():
    return [(j, min(CHUNK, IMG - j)) for j in range(0, IMG, CHUNK)] + [(IMG, TXT_PAD)]


def attend_kernel(
    phase, ids_ref, q_ref, own_kv_ref, other_kv_ref, text_ref, text_other_ref, y_ref, ex_ref, dt_ref,
    keys, values, kvt, s_ref, e_ref, acc,
):
    step = pl.program_id(0)
    core = ids_ref[0]
    mine = core == phase

    @pl.when(step == 0)
    def _():
        text = jnp.where(mine, text_ref[TXT_PAD:], text_other_ref[TXT_PAD:])
        for j, n, x in ((0, MINE, own_kv_ref), (MINE, MINE, other_kv_ref), (IMG, TXT_PAD, None)):
            t = (text if x is None else x[...].reshape(n, 128)).T
            cols = slice(j, j + n)
            kvt[0:128, cols] = t
            keys[0:64, cols] = t[:64]
            keys[64:128, cols] = t[:64]
            minus = lax.broadcasted_iota(jnp.int32, (64, n), 0) < 2
            values[0:64, cols] = jnp.where(minus, -1.0, 0.0).astype(bf16)
            values[64:128, cols] = t[64:]
        kvt[128:144] = jnp.ones((16, KEYS), bf16)
        acc[...] = jnp.zeros_like(acc)

    padding = lax.broadcasted_iota(jnp.int32, (1, TXT_PAD), 1) >= TXT

    def block(qg):
        rows = qg.shape[0]
        qgt = qg.T
        q = qg[:, :64].astype(f32) * LOG2E
        q_high = q.astype(bf16)
        left = jnp.concatenate([q_high, (q - q_high.astype(f32)).astype(bf16)], axis=1)
        top = jnp.full((rows, 128), -jnp.inf, f32)
        for j, n in key_chunks():
            s = dot(left, keys[:, j : j + n], 1, 0)
            if j == IMG:
                s = jnp.where(padding, -jnp.inf, s)
            s_ref[:rows, j : j + n] = s
            for i in range(0, n, 128):
                top = jnp.maximum(top, s[:, i : i + 128])
        top = jnp.max(top, axis=1, keepdims=True)
        ot = jnp.zeros((80, rows), f32)
        for j, n in key_chunks():
            e = jnp.exp2(s_ref[:rows, j : j + n] - top).astype(bf16)
            e_ref[:rows, j : j + n] = e
            ot = ot + dot(kvt[64:144, j : j + n], e, 1, 1)
        inv = 1.0 / ot[64:65]
        ot = (ot[:64] * inv).astype(bf16).astype(f32)
        gt = qgt[64:].astype(f32)
        row_term = jnp.sum(gt * ot, axis=0, keepdims=True) * inv
        gt = (gt * inv).astype(bf16)
        high = row_term.astype(bf16).astype(f32)
        left = jnp.concatenate([high, row_term - high, jnp.zeros((62, rows), f32), gt.astype(f32)], axis=0)
        left = left.astype(bf16).T
        dqt = jnp.zeros((64, rows), f32)
        for j, n in key_chunks():
            e = e_ref[:rows, j : j + n]
            ds = e * dot(left, values[:, j : j + n], 1, 0).astype(bf16)
            dqt = dqt + dot(kvt[0:64, j : j + n], ds, 1, 1)
            acc[0:64, j : j + n] += dot(qgt[0:64], ds, 1, 0)
            acc[64:128, j : j + n] += dot(gt, e, 1, 0)
        return jnp.concatenate([dqt * 0.125, ot], axis=0).T.astype(bf16)

    y_ref[pl.ds(SRC_STEP * step, SRC_STEP), :TOK] = block(q_ref[...].reshape(ROWS, 128)).reshape(SRC_STEP, TOK, 128)

    @pl.when(step == STEPS - 1)
    def _():
        rows = pl.ds(pl.multiple_of(TXT_HALF * core, TXT_HALF), TXT_HALF)
        ex_ref[:TXT_HALF] = block(jnp.where(mine, text_ref[rows], text_other_ref[rows]))
        dt = acc[:, IMG:].T
        dt_ref[...] = dt
        ex_ref[TXT_HALF:TAIL] = dt.astype(bf16)
        ex_ref[TAIL:] = acc[:, MINE:IMG].T.astype(bf16)
        y_ref[:, TOK : 2 * TOK] = acc[:, :MINE].T.astype(bf16).reshape(CHIPS, TOK, 128)


def attend(phase, ids, received, other, text, text_other, y_rows):
    half = (CHIPS, TOK, 128)
    text_shape = (2 * TXT_PAD, 128)
    return pl.pallas_call(
        functools.partial(attend_kernel, phase),
        grid=(STEPS,),
        out_shape=(
            SDS((CHIPS, y_rows, 128), bf16),
            SDS((TAIL + MINE, 128), bf16),
            SDS((TXT_PAD, 128), f32),
        ),
        in_specs=[
            IN_SMEM,
            pl.BlockSpec((SRC_STEP, None, TOK, 128), lambda i: (i, 0, 0, 0)),
            pl.BlockSpec((CHIPS, None, TOK, 128), lambda i: (0, 1, 0, 0)),
            whole(half),
            whole(text_shape),
            whole(text_shape),
        ],
        out_specs=(whole((CHIPS, y_rows, 128)), whole((TAIL + MINE, 128)), whole((TXT_PAD, 128))),
        scratch_shapes=[
            pltpu.VMEM((128, KEYS), bf16),
            pltpu.VMEM((128, KEYS), bf16),
            pltpu.VMEM((144, KEYS), bf16),
            pltpu.VMEM((ROWS, KEYS), f32),
            pltpu.VMEM((ROWS, KEYS), bf16),
            pltpu.VMEM((128, KEYS), f32),
        ],
        name=("attend_first", "attend_second")[phase],
        cost_estimate=cost(34),
        compiler_params=params(),
    )(ids, received, received, other, text, text_other)


def add_shares(y_in, got_ref, y_ref):
    for i in range(CHIPS):
        got = got_ref[TAIL + TOK * i : TAIL + TOK * i + TOK].astype(f32)
        y_ref[i] = (y_in[i].astype(f32) + got).astype(bf16)


def finish_first(y, got):
    part = pl.BlockSpec((CHIPS, TOK, 128), lambda i: (0, 1, 0))
    return pl.pallas_call(
        add_shares,
        grid=(1,),
        out_shape=SDS(y.shape, bf16),
        in_specs=[part, whole(got.shape)],
        out_specs=part,
        input_output_aliases={0: 0},
        name="finish_first",
        cost_estimate=cost(2),
        compiler_params=params(),
    )(y, got)


def text_kernel(ids_ref, ex0_ref, got0_ref, dt0_ref, ex1_ref, got1_ref, dt1_ref, own_ref, other_ref, o_ref, rows_ref):
    core = ids_ref[0]
    low = low_lanes()
    heads = []
    for ex, got, dt in ((ex0_ref, got0_ref, dt0_ref), (ex1_ref, got1_ref, dt1_ref)):
        rows_ref[pl.ds(pl.multiple_of(TXT_HALF * core, TXT_HALF), TXT_HALF)] = ex[:TXT_HALF]
        rows_ref[pl.ds(pl.multiple_of(TXT_HALF * (1 - core), TXT_HALF), TXT_HALF)] = got[:TXT_HALF]
        qo = rows_ref[0:TXT_ROWS]
        kv = (dt[...] + got[TXT_HALF:TAIL].astype(f32)).astype(bf16)[:TXT_ROWS]
        heads.append((qo, kv))
    for target, which in ((own_ref, core == 0), (other_ref, core == 1)):
        qo, kv = (jnp.where(which, a, b) for a, b in zip(*heads))
        vk = swap(kv)
        target[:, :128] = jnp.where(low, qo, vk)
        target[:, 128:] = jnp.where(low, vk, jnp.zeros_like(vk))
        if target is own_ref:
            o_ref[...] = qo[:TXT, 64:]


def text_grads(ids, shares):
    tail = whole((TAIL, 128))
    return pl.pallas_call(
        text_kernel,
        grid=(1,),
        out_shape=(SDS((TXT_ROWS, 256), bf16), SDS((TXT_ROWS, 256), bf16), SDS((TXT, 64), bf16)),
        in_specs=[IN_SMEM] + [tail, tail, whole((TXT_PAD, 128))] * 2,
        out_specs=(whole((TXT_ROWS, 256)), whole((TXT_ROWS, 256)), whole((TXT, 64))),
        scratch_shapes=[pltpu.VMEM((TXT_PAD, 128), bf16)],
        name="text_grads",
        cost_estimate=cost(2),
        compiler_params=params(),
    )(ids, *shares)


def finish_last_kernel(ids_ref, y_in, got_ref, own_ref, other_ref, w_ref, w_other_ref, y_ref):
    y_ref[:, :TOK] = y_in[:, :TOK]
    add_shares(y_in.at[:, TOK : 2 * TOK], got_ref, y_ref.at[:, TOK : 2 * TOK])
    first = ids_ref[0] == 0
    n = w_ref.shape[2] // 4
    for r in range(w_ref.shape[0]):
        total = dot(own_ref[:, :192], w_ref[r], 1, 0) + dot(other_ref[:, :192], w_other_ref[r], 1, 0)
        for i in range(2):
            at = 2 * n * i
            piece = jnp.where(first, total[:, at : at + n], total[:, at + n : at + 2 * n])
            piece = jnp.concatenate([piece, jnp.zeros((TXT_ROWS, 128 - n), f32)], axis=1)
            y_ref[2 * ids_ref[1 + r] + i, 2 * TOK :] = piece.astype(bf16)


def finish_last(ids, y, got, own, other, w, w_other):
    return pl.pallas_call(
        finish_last_kernel,
        out_shape=SDS(y.shape, bf16),
        in_specs=[IN_SMEM] + [IN_VMEM] * 6,
        out_specs=IN_VMEM,
        name="finish_last",
        cost_estimate=cost(5),
        compiler_params=params(),
    )(ids, y, got, own, other, w, w_other)


def unpack_kernel(z0_ref, z1_ref, o_ref, g_ref, dx_ref, acc):
    low = low_lanes()
    step = pl.program_id(0)
    total = jnp.zeros((TXT_ROWS, 128), f32)
    for c in range(z0_ref.shape[0]):
        cols = slice(128 * c, 128 * c + 128)
        qo0, qo1 = z0_ref[c, :TOK], z1_ref[c, :TOK]
        kv0, kv1 = z0_ref[c, TOK : 2 * TOK], z1_ref[c, TOK : 2 * TOK]
        g_ref[0, :, cols] = jnp.where(low, qo0, swap(qo1))
        o_ref[:, cols] = jnp.where(low, swap(qo0), qo1)
        g_ref[1, :, cols] = jnp.where(low, kv0, swap(kv1))
        g_ref[2, :, cols] = jnp.where(low, swap(kv0), kv1)
        total += z1_ref[c, 2 * TOK :].astype(f32)

    @pl.when(step == 0)
    def _():
        acc[...] = total

    @pl.when(step > 0)
    def _():
        acc[...] += total

    @pl.when(step == pl.num_programs(0) - 1)
    def _():
        dx_ref[...] = acc[...].T[: dx_ref.shape[0], :TXT].reshape(dx_ref.shape)


def unpack(z0, z1, dx_cols):
    grid = 4
    width = 128 * CHIPS
    return pl.pallas_call(
        unpack_kernel,
        grid=(grid,),
        out_shape=(SDS((TOK, width), bf16), SDS((3, TOK, width), bf16), SDS((dx_cols, 1, TXT), f32)),
        in_specs=[pl.BlockSpec((CHIPS // grid, z.shape[1], 128), lambda i: (i, 0, 0)) for z in (z0, z1)],
        out_specs=(
            pl.BlockSpec((TOK, width // grid), lambda i: (0, i)),
            pl.BlockSpec((3, TOK, width // grid), lambda i: (0, 0, i)),
            whole((dx_cols, 1, TXT)),
        ),
        scratch_shapes=[pltpu.VMEM((TXT_ROWS, 128), f32)],
        name="unpack",
        cost_estimate=cost(4),
        compiler_params=params(),
    )(z0, z1)


def weight_grad_kernel(x_ref, tg_ref, out_ref):
    total = jnp.zeros(out_ref.shape, f32)
    for r in range(x_ref.shape[0]):
        total += dot(tg_ref[r, :TXT, :192], x_ref[r], 0, 0)
    out_ref[...] = total


def weight_grad(x, tg):
    return pl.pallas_call(
        weight_grad_kernel,
        out_shape=SDS((192, x.shape[2]), f32),
        in_specs=[IN_VMEM] * 2,
        out_specs=IN_VMEM,
        name="weight_grad",
        cost_estimate=cost(4),
        compiler_params=params(),
    )(x, tg)


def local(q_img, k_img, v_img, x_txt, w_txt, grad_img, grad_txt):
    seq, dp = lax.axis_index("seq"), lax.axis_index("dp")
    core = seq % 2
    dp_hi, dp_lo = dp // 4, dp % 4
    pair = [(i, i ^ 1) for i in range(2 * CHIPS)]
    parity = [list(range(j, 2 * CHIPS, 2)) for j in range(2)]
    across = [(i, i ^ 4) for i in range(8)]
    turns = [[(i, i // 4 * 4 + (i + k) % 4) for i in range(8)] for k in range(1, 4)]

    def exchange(x):
        return lax.all_to_all(x, "seq", 0, 0, axis_index_groups=parity, tiled=True)

    def around(x, got):
        both = jnp.stack([x, got])
        return jnp.concatenate([both] + [lax.ppermute(both, "dp", t) for t in turns])

    order = [(dp_hi ^ side) * 4 + (dp_lo + 4 - k) % 4 for k in range(4) for side in range(2)]
    ids = jnp.stack([core] + order).astype(jnp.int32)
    image = (q_img[0], k_img[0], v_img[0], grad_img[0])

    w_own = jnp.swapaxes(w_txt, 1, 2).reshape(192, -1)
    w_across = lax.ppermute(w_own, "dp", across)

    x8 = x_txt[0].reshape(TXT, 8, -1).transpose(1, 0, 2)
    halves = x8.reshape(4, 2, TXT, -1)
    half = lax.dynamic_index_in_dim(halves, 2 * (1 - dp_hi) + core, 0, keepdims=False)
    packed = pack(0, *image, 4)
    packed, w_across = lax.optimization_barrier((packed, w_across))
    r0 = exchange(packed)
    weights = around(w_own, w_across)
    text = project(ids, x8, weights, grad_txt[0])
    text_other = lax.ppermute(text, "seq", pair)
    weights_other = lax.ppermute(weights, "seq", pair)
    second = pack(1, *image, 4)
    r0, second, text_other, weights_other, half = lax.optimization_barrier(
        (r0, second, text_other, weights_other, half)
    )

    kv0 = lax.ppermute(r0[:, 1], "seq", pair)
    r1 = exchange(second)
    x_half = lax.ppermute(half, "dp", across)
    y0, ex0, dt0 = attend(0, ids, r0, kv0, text, text_other, 2 * TOK)
    ex0, x_half = lax.optimization_barrier((ex0, x_half))
    got0 = lax.ppermute(ex0, "seq", pair)
    kv1 = lax.ppermute(r1[:, 1], "seq", pair)
    z0 = exchange(finish_first(y0, got0))
    y1, ex1, dt1 = attend(1, ids, r1, kv1, text, text_other, 2 * TOK + TXT_ROWS)
    got1 = lax.ppermute(ex1, "seq", pair)

    grads_own, grads_other, o_txt = text_grads(ids, (ex0, got0, dt0, ex1, got1, dt1))
    grads_across = lax.ppermute(grads_own, "dp", across)
    y1 = finish_last(ids, y1, got1, grads_own, grads_other, weights, weights_other)
    y1, grads_across, x_half = lax.optimization_barrier((y1, grads_across, x_half))
    z1 = exchange(y1)
    x_other = lax.ppermute(x_half, "seq", pair)
    x_across = jnp.where(core == 0, jnp.concatenate([x_half, x_other]), jnp.concatenate([x_other, x_half]))
    kept = lax.dynamic_slice_in_dim(x8, 4 * dp_hi, 4, 0)
    both = jnp.stack([kept, x_across], axis=1)
    columns = [lax.dynamic_index_in_dim(both, (dp_lo + k) % 4, 0, keepdims=False) for k in range(4)]
    x_all = jnp.concatenate([columns[0]] + [lax.ppermute(c, "dp", t) for c, t in zip(columns[1:], turns)])
    dw = weight_grad(x_all, around(grads_own, grads_across))
    dw = jnp.swapaxes(dw.reshape(3, 64, -1), 1, 2)
    o_img, grads, dx = unpack(z0, z1, x_txt.shape[2] // (2 * CHIPS))
    return o_img[None], o_txt[None], grads[:, None], dx.transpose(1, 2, 0), dw


def solution(mesh):
    in_specs = (
        P("dp", "seq", None),
        P("dp", "seq", None),
        P("dp", "seq", None),
        P("dp", None, None),
        P(None, "dp", "seq"),
        P("dp", "seq", None),
        P("dp", None, "seq"),
    )
    out_specs = (
        P("dp", "seq", None),
        P("dp", None, "seq"),
        P(None, "dp", "seq", None),
        P("dp", None, "seq"),
        P(None, "dp", "seq"),
    )
    return jax.shard_map(local, mesh=mesh, in_specs=in_specs, out_specs=out_specs, check_vma=False)
```

time: 709 us -> 192 us (0.27); the launches traced: 697 us -> 188 us
  other arithmetic: 164 us -> 1.97 us
  waiting for transfers between devices: 165 us -> 35.9 us
  matrix products: 120 us -> 0 us
  local copies, waits for them, and re-layouts: 102 us -> 14.6 us
  Pallas kernels: 0 us -> 78.8 us
  blocking collectives: 61.4 us -> 0 us
  between operations: 17.1 us -> 1.09 us
    unnamed x4 -> x0, waiting for transfers between devices: 157 us -> none
    unnamed x10 -> x0, other arithmetic: 137 us -> none
    dot_general x57 -> x0, matrix products: 120 us -> none  [the longest x9 27.6 us: block_pass(): jnp.einsum('gbd,gkd->gbk', cotangent, values, preferred_element_type=jnp....]
    pallas_call x0 -> x10, Pallas kernels: none -> 78.8 us  [the longest x2 64 us: attend(): pl.pallas_call(functools.partial(attend_kernel, phase), grid=(STEPS,), ou...]
    all_gather x1 -> x0, blocking collectives: 61.4 us -> none  [local(): full_weights = lax.all_gather(w_txt, 'dp', axis=1, tiled=True)]
    unnamed x100 -> x48, local copies, waits for them, and re-layouts: 65.6 us -> 9.01 us
    all_to_all x8 -> x4, starting transfers between devices: 61.6 us -> 28.4 us  [exchange(): return lax.all_to_all(x, 'seq', 0, 0, axis_index_groups=parity, tiled=True)]
    ppermute x0 -> x19, starting transfers between devices: none -> 27.5 us  [the longest x6 8.63 us: around(): lax.ppermute(both, 'dp', t)]
  transfers between devices with their start and end apart: 10 -> 23, of which waited for: 4 -> 10; matrix products, arithmetic and copies ran while one was open for 28% -> 5% of each run, Pallas kernels for 0% -> 41%
where the time goes in v2:
time: 192 us; the launch traced here: 188 us
  Pallas kernels  78.8 us (41%)
  starting transfers between devices  56 us (29%)
  waiting for transfers between devices  35.9 us (19%)
  local copies, waits for them, and re-layouts  14.6 us (8%)
  other arithmetic  1.97 us (1%)
    pallas_call x2, Pallas kernels, attend(): pl.pallas_call(functools.partial(attend_kernel, phase), grid=(STEPS,), ou...  64 us
    all_to_all x4, starting transfers between devices, exchange(): return lax.all_to_all(x, 'seq', 0, 0, axis_index_groups=parity, tiled=True)  28.4 us
    ppermute x6, waiting for transfers between devices, around(): lax.ppermute(both, 'dp', t)  15 us
    all_to_all x4, waiting for transfers between devices, exchange(): return lax.all_to_all(x, 'seq', 0, 0, axis_index_groups=parity, tiled=True)  9.04 us
    unnamed x48, local copies, waits for them, and re-layouts  9.01 us
    ppermute x6, starting transfers between devices, around(): lax.ppermute(both, 'dp', t)  8.63 us
    ppermute x1, starting transfers between devices, local(): w_across = lax.ppermute(w_own, 'dp', across)  7.28 us
    ppermute x1, starting transfers between devices, local(): x_half = lax.ppermute(half, 'dp', across)  5.33 us
  transfers between devices with their start and end apart: 23, of which 10 were waited for; matrix products, arithmetic and copies ran while one was open for 5% of the time, Pallas kernels for 41%

profile of v2, /device:TPU:8, one launch (start us, length us, event | category | flops | bytes accessed | tf_op | source)
XLA Modules:
  0.0 188.3 jit_solution(12732890791831739036)
XLA Ops:
  0.6 7.3 %collective-permute-start = (bf16[192,304]{1,0:T(8,128)(2,1)}, bf16[192,304]{1,0:T(8,128)(2,1)S(1)}, u32[]{:S(2)}, u32[]{:S(2)}) collective-permute-start(bf16[192,304]{1,0:T(8,128)(2,1)} %bitcast.78), channel_id=1, source_target_pairs={{0,128},{32,160},{64,192},{96,224},{128,0},{160,32},{192,64},{224,... | collective-permute-start | bytes 350216 | tf_op jit(solution)/shard_map/ppermute | solution.py:387
  7.9 1.0 copy-done.4
  9.0 1.0 copy-done.6
  10.0 1.0 copy-done.8
  11.0 1.0 copy-done.10
  12.1 2.0 %pack_first.1 = bf16[16,2,128,128]{3,2,1,0:T(8,128)(2,1)} custom-call(bf16[128,2048]{1,0:T(8,128)(2,1)S(1)} %bitcast.70, bf16[128,2048]{1,0:T(8,128)(2,1)S(1)} %bitcast.72, bf16[128,2048]{1,0:T(8,128)(2,1)S(1)} %bitcast.74, bf16[128,2048]{1,0:T(8,128)(2,1)S(1)} %bitcast.76), custom_call_target="tpu_custom_call" | custom-call | flops 3449999872 | bytes 1048576 | tf_op jit(solution)/shard_map/pack_first/pallas_call | solution.py:71
  14.1 6.9 %all-to-all-start = ((bf16[16,2,128,128]{3,2,1,0:T(8,128)(2,1)}), bf16[16,2,128,128]{3,2,1,0:T(8,128)(2,1)S(1)}, u32[]{:S(2)}, u32[]{:S(2)}) async-start(bf16[16,2,128,128]{3,2,1,0:T(8,128)(2,1)} %pack_first.1), calls=%async_computation | async-start | bytes 2097152 | tf_op jit(solution)/shard_map/all_to_all | solution.py:376
  21.0 1.7 collective-permute-start.1
  23.2 2.3 %collective-permute-start.2 = (bf16[2,192,304]{2,1,0:T(8,128)(2,1)S(1)}, bf16[2,192,304]{2,1,0:T(8,128)(2,1)S(1)}, u32[]{:S(2)}, u32[]{:S(2)}) collective-permute-start(bf16[2,192,304]{2,1,0:T(8,128)(2,1)S(1)} %pad_maximum_fusion.1), channel_id=1, source_target_pairs={{0,64},{32,96},{64,0},{96,32},{128,192},{160,224},{192,128},{224,1... | collective-permute-start | bytes 700424 | tf_op jit(solution)/shard_map/ppermute | solution.py:380
  25.5 5.5 %collective-permute-done.1 = bf16[2,192,304]{2,1,0:T(8,128)(2,1)S(1)} collective-permute-done((bf16[2,192,304]{2,1,0:T(8,128)(2,1)S(1)}, bf16[2,192,304]{2,1,0:T(8,128)(2,1)S(1)}, u32[]{:S(2)}, u32[]{:S(2)}) %collective-permute-start.1) | collective-permute-done | bytes 233504 | tf_op jit(solution)/shard_map/ppermute | solution.py:380
  31.1 6.2 %collective-permute-done.2 = bf16[2,192,304]{2,1,0:T(8,128)(2,1)S(1)} collective-permute-done((bf16[2,192,304]{2,1,0:T(8,128)(2,1)S(1)}, bf16[2,192,304]{2,1,0:T(8,128)(2,1)S(1)}, u32[]{:S(2)}, u32[]{:S(2)}) %collective-permute-start.2) | collective-permute-done | bytes 233504 | tf_op jit(solution)/shard_map/ppermute | solution.py:380
  37.7 2.6 %reshape_squeeze.3 = bf16[77,8,304]{2,1,0:T(8,128)(2,1)} reshape(bf16[1,77,2432]{2,1,0:T(8,128)(2,1)} %param.10) | data formatting | bytes 749056 | tf_op jit(solution)/shard_map/reshape;squeeze | solution.py:389
  40.4 1.1 copy.70
  41.6 1.0 copy-done.7
  42.6 1.0 copy-done.9
  43.6 1.0 copy-done.11
  44.7 2.0 %pack_second.1 = bf16[16,2,128,128]{3,2,1,0:T(8,128)(2,1)} custom-call(bf16[128,2048]{1,0:T(8,128)(2,1)S(1)} %bitcast.71, bf16[128,2048]{1,0:T(8,128)(2,1)S(1)} %bitcast.73, bf16[128,2048]{1,0:T(8,128)(2,1)S(1)} %bitcast.75, bf16[128,2048]{1,0:T(8,128)(2,1)S(1)} %bitcast.77), custom_call_target="tpu_custom_call" | custom-call | flops 3449999872 | bytes 1048576 | tf_op jit(solution)/shard_map/pack_second/pallas_call | solution.py:71
  46.7 1.2 project.1.text_ref
  48.1 0.7 copy.69
  49.5 7.2 %all-to-all-start.2 = ((bf16[16,2,128,128]{3,2,1,0:T(8,128)(2,1)}), bf16[16,2,128,128]{3,2,1,0:T(8,128)(2,1)S(1)}, u32[]{:S(2)}, u32[]{:S(2)}) async-start(bf16[16,2,128,128]{3,2,1,0:T(8,128)(2,1)} %pack_second.1), calls=%async_computation.2 | async-start | bytes 2097152 | tf_op jit(solution)/shard_map/all_to_all | solution.py:376
  56.8 5.3 %collective-permute-start.7 = (bf16[2,77,304]{2,0,1:T(2,128)(2,1)}, bf16[2,77,304]{2,0,1:T(2,128)(2,1)S(1)}, u32[]{:S(2)}, u32[]{:S(2)}) collective-permute-start(bf16[2,77,304]{2,0,1:T(2,128)(2,1)} %bitcast.64), channel_id=1, source_target_pairs={{0,128},{32,160},{64,192},{96,224},{128,0},{160,32},{192,64},{224,... | collective-permute-start | bytes 280904 | tf_op jit(solution)/shard_map/ppermute | solution.py:406
  62.1 32.2 %attend_first.1 = (bf16[16,256,128]{2,1,0:T(8,128)(2,1)}, bf16[2240,128]{1,0:T(8,128)(2,1)S(1)}, f32[128,128]{1,0:T(8,128)S(1)}) custom-call(s32[9]{0:T(128)S(1)} %stack.61.ids_ref, bf16[16,2,128,128]{3,2,1,0:T(8,128)(2,1)S(1)} %all-to-all-done.q_ref.own_kv_ref, bf16[16,2,128,128]{3,2,1,0:T(8,128)(2,1)S(1)} %all-to-all-done.q_ref.own_kv_ref, ...), custom_call_target="tpu_custom_call" | custom-call | flops 39099998208 | bytes 1048576 | tf_op jit(solution)/shard_map/attend_first/pallas_call | solution.py:188
  94.3 0.6 copy-done.14
  95.0 0.8 slice_bitcast_fusion
  96.3 0.6 collective-permute-done.8.got_ref.got0_ref
  96.9 2.2 %finish_first.1 = bf16[16,256,128]{2,1,0:T(8,128)(2,1)} custom-call(bf16[16,256,128]{2,1,0:T(8,128)(2,1)} %get-tuple-element.33.y_in, bf16[2240,128]{1,0:T(8,128)(2,1)S(1)} %collective-permute-done.8.got_ref.got0_ref), custom_call_target="tpu_custom_call", output_to_operand_aliasing={{}: (0, {})} | custom-call | flops 2300000000 | bytes 1048576 | tf_op jit(solution)/shard_map/finish_first/pallas_call | solution.py:227
  99.2 7.3 %all-to-all-start.1 = ((bf16[16,256,128]{2,1,0:T(8,128)(2,1)}), bf16[16,256,128]{2,1,0:T(8,128)(2,1)S(1)}, u32[]{:S(2)}, u32[]{:S(2)}) async-start(bf16[16,256,128]{2,1,0:T(8,128)(2,1)} %finish_first.1), calls=%async_computation.1 | async-start | bytes 2097152 | tf_op jit(solution)/shard_map/all_to_all | solution.py:376
  106.4 31.8 %attend_second.1 = (bf16[16,336,128]{2,1,0:T(8,128)(2,1)S(1)}, bf16[2240,128]{1,0:T(8,128)(2,1)S(1)}, f32[128,128]{1,0:T(8,128)S(1)}) custom-call(s32[9]{0:T(128)S(1)} %stack.61.ids_ref, bf16[16,2,128,128]{3,2,1,0:T(8,128)(2,1)S(1)} %all-to-all-done.2.q_ref.own_kv_ref, bf16[16,2,128,128]{3,2,1,0:T(8,128)(2,1)S(1)} %all-to-all-done.2.q_ref.own_kv_ref, ...), custom_call_target="tpu_custom_call" | custom-call | flops 39099998208 | bytes 1048576 | tf_op jit(solution)/shard_map/attend_second/pallas_call | solution.py:188
  138.4 2.0 %collective-permute-done.10.got1_ref.got_ref = bf16[2240,128]{1,0:T(8,128)(2,1)S(1)} collective-permute-done((bf16[2240,128]{1,0:T(8,128)(2,1)S(1)}, bf16[2240,128]{1,0:T(8,128)(2,1)S(1)}, u32[]{:S(2)}, u32[]{:S(2)}) %collective-permute-start.10) | collective-permute-done | bytes 573472 | tf_op jit(solution)/shard_map/ppermute | solution.py:413
  140.3 0.6 text_grads.1
  141.0 1.0 collective-permute-start.11
  141.9 3.2 %finish_last.1 = bf16[16,336,128]{2,1,0:T(8,128)(2,1)} custom-call(s32[9]{0:T(128)S(1)} %stack.61.ids_ref, bf16[16,336,128]{2,1,0:T(8,128)(2,1)S(1)} %get-tuple-element.38.y_in, bf16[2240,128]{1,0:T(8,128)(2,1)S(1)} %collective-permute-done.10.got1_ref.got_ref, bf16[80,256]{1,0:T(8,128)(2,1)S(1)} %get-tuple-element.42.own_ref, ...), custom_call_target="tpu_custom_call" | custom-call | flops 5750000128 | bytes 1048576 | tf_op jit(solution)/shard_map/finish_last/pallas_call | solution.py:289
  145.1 4.3 %collective-permute-done.11 = bf16[80,256]{1,0:T(8,128)(2,1)S(1)} collective-permute-done((bf16[80,256]{1,0:T(8,128)(2,1)S(1)}, bf16[80,256]{1,0:T(8,128)(2,1)S(1)}, u32[]{:S(2)}, u32[]{:S(2)}) %collective-permute-start.11) | collective-permute-done | bytes 40992 | tf_op jit(solution)/shard_map/ppermute | solution.py:416
  149.4 7.1 %all-to-all-start.3 = ((bf16[16,336,128]{2,1,0:T(8,128)(2,1)}), bf16[16,336,128]{2,1,0:T(8,128)(2,1)S(1)}, u32[]{:S(2)}, u32[]{:S(2)}) async-start(bf16[16,336,128]{2,1,0:T(8,128)(2,1)} %finish_last.1), calls=%async_computation.3 | async-start | bytes 2752512 | tf_op jit(solution)/shard_map/all_to_all | solution.py:376
  156.7 0.7 copy.49
  157.4 0.9 collective-permute-start.18
  158.3 0.8 collective-permute-start.17
  159.0 2.5 %collective-permute-start.16 = (bf16[2,80,256]{2,1,0:T(8,128)(2,1)S(1)}, bf16[2,80,256]{2,1,0:T(8,128)(2,1)S(1)}, u32[]{:S(2)}, u32[]{:S(2)}) collective-permute-start(bf16[2,80,256]{2,1,0:T(8,128)(2,1)S(1)} %pad_maximum_fusion.2), channel_id=1, source_target_pairs={{0,32},{32,64},{64,96},{96,0},{128,160},{160,192},{192,224},{224,1... | collective-permute-start | bytes 245768 | tf_op jit(solution)/shard_map/ppermute | solution.py:380
  161.6 3.3 %collective-permute-done.16 = bf16[2,80,256]{2,1,0:T(8,128)(2,1)S(1)} collective-permute-done((bf16[2,80,256]{2,1,0:T(8,128)(2,1)S(1)}, bf16[2,80,256]{2,1,0:T(8,128)(2,1)S(1)}, u32[]{:S(2)}, u32[]{:S(2)}) %collective-permute-start.16) | collective-permute-done | bytes 81952 | tf_op jit(solution)/shard_map/ppermute | solution.py:380
  165.4 1.3 fusion.1
  166.8 2.4 %collective-permute-start.15 = (bf16[2,77,304]{2,1,0:T(8,128)(2,1)S(1)}, bf16[2,77,304]{2,1,0:T(8,128)(2,1)S(1)}, u32[]{:S(2)}, u32[]{:S(2)}) collective-permute-start(bf16[2,77,304]{2,1,0:T(8,128)(2,1)S(1)} %bitcast.86), channel_id=1, source_target_pairs={{0,96},{32,0},{64,32},{96,64},{128,224},{160,128},{192,160},{224,1... | collective-permute-start | bytes 280904 | tf_op jit(solution)/shard_map/ppermute | solution.py:425
  169.2 0.6 collective-permute-start.14
  169.8 1.2 collective-permute-start.13
  171.0 2.0 %collective-permute-done.15 = bf16[2,77,304]{2,1,0:T(8,128)(2,1)S(1)} collective-permute-done((bf16[2,77,304]{2,1,0:T(8,128)(2,1)S(1)}, bf16[2,77,304]{2,1,0:T(8,128)(2,1)S(1)}, u32[]{:S(2)}, u32[]{:S(2)}) %collective-permute-start.15) | collective-permute-done | bytes 93664 | tf_op jit(solution)/shard_map/ppermute | solution.py:425
  173.0 2.6 %collective-permute-done.14 = bf16[2,77,304]{2,1,0:T(8,128)(2,1)S(1)} collective-permute-done((bf16[2,77,304]{2,1,0:T(8,128)(2,1)S(1)}, bf16[2,77,304]{2,1,0:T(8,128)(2,1)S(1)}, u32[]{:S(2)}, u32[]{:S(2)}) %collective-permute-start.14) | collective-permute-done | bytes 93664 | tf_op jit(solution)/shard_map/ppermute | solution.py:425
  175.7 1.2 weight_grad.1
  177.0 9.0 %all-to-all-done.3.z1_ref = bf16[16,336,128]{2,1,0:T(8,128)(2,1)S(1)} async-done(((bf16[16,336,128]{2,1,0:T(8,128)(2,1)}), bf16[16,336,128]{2,1,0:T(8,128)(2,1)S(1)}, u32[]{:S(2)}, u32[]{:S(2)}) %all-to-all-start.3) | async-done | bytes 1376288 | tf_op jit(solution)/shard_map/all_to_all | solution.py:376
  186.0 2.3 %unpack.1 = (bf16[128,2048]{1,0:T(8,128)(2,1)}, bf16[3,128,2048]{2,1,0:T(8,128)(2,1)}, f32[76,1,77]{2,1,0:T(1,128)}) custom-call(bf16[16,256,128]{2,1,0:T(8,128)(2,1)S(1)} %all-to-all-done.1.z0_ref, bf16[16,336,128]{2,1,0:T(8,128)(2,1)S(1)} %all-to-all-done.3.z1_ref), custom_call_target="tpu_custom_call" | custom-call | flops 4600000000 | bytes 1048576 | tf_op jit(solution)/shard_map/unpack/pallas_call | solution.py:330
  (71 shorter events, 3.5 us)
Async XLA Ops:
  0.6 13.4 %collective-permute-start = (bf16[192,304]{1,0:T(8,128)(2,1)}, bf16[192,304]{1,0:T(8,128)(2,1)S(1)}, u32[]{:S(2)}, u32[]{:S(2)}) collective-permute-start(bf16[192,304]{1,0:T(8,128)(2,1)} %bitcast.78), channel_id=1, source_target_pairs={{0,128},{32,160},{64,192},{96,224},{128,0},{160,32},{192,64},{224,... | collective-permute-start | bytes 350216 | tf_op jit(solution)/shard_map/ppermute | solution.py:387
  7.9 1.0 copy-start.4
  8.9 1.0 copy-start.6
  10.0 1.0 copy-start.8
  11.0 1.0 copy-start.10
  14.1 6.9 %copy-start.13 = (bf16[3,304,64]{1,2,0:T(8,128)(2,1)S(1)}, bf16[3,304,64]{1,2,0:T(8,128)(2,1)}, u32[]{:S(2)}) copy-start(bf16[3,304,64]{1,2,0:T(8,128)(2,1)} %param.11) | copy-start | bytes 350212
  14.1 35.2 %all-to-all-start = ((bf16[16,2,128,128]{3,2,1,0:T(8,128)(2,1)}), bf16[16,2,128,128]{3,2,1,0:T(8,128)(2,1)S(1)}, u32[]{:S(2)}, u32[]{:S(2)}) async-start(bf16[16,2,128,128]{3,2,1,0:T(8,128)(2,1)} %pack_first.1), calls=%async_computation | async-start | bytes 2097152 | tf_op jit(solution)/shard_map/all_to_all | solution.py:376
  21.0 10.0 %collective-permute-start.1 = (bf16[2,192,304]{2,1,0:T(8,128)(2,1)S(1)}, bf16[2,192,304]{2,1,0:T(8,128)(2,1)S(1)}, u32[]{:S(2)}, u32[]{:S(2)}) collective-permute-start(bf16[2,192,304]{2,1,0:T(8,128)(2,1)S(1)} %pad_maximum_fusion.1), channel_id=1, source_target_pairs={{0,32},{32,64},{64,96},{96,0},{128,160},{160,192},{192,224},{224,1... | collective-permute-start | bytes 700424 | tf_op jit(solution)/shard_map/ppermute | solution.py:380
  22.7 15.0 %copy-start.16 = (bf16[1,77,64]{1,2,0:T(8,128)(2,1)S(1)}, bf16[1,77,64]{1,2,0:T(8,128)(2,1)}, u32[]{:S(2)}) copy-start(bf16[1,77,64]{1,2,0:T(8,128)(2,1)} %param.13) | copy-start | bytes 29572
  22.7 14.7 %collective-permute-start.3 = (bf16[2,192,304]{2,1,0:T(8,128)(2,1)S(1)}, bf16[2,192,304]{2,1,0:T(8,128)(2,1)S(1)}, u32[]{:S(2)}, u32[]{:S(2)}) collective-permute-start(bf16[2,192,304]{2,1,0:T(8,128)(2,1)S(1)} %pad_maximum_fusion.1), channel_id=1, source_target_pairs={{0,96},{32,0},{64,32},{96,64},{128,224},{160,128},{192,160},{224,1... | collective-permute-start | bytes 700424 | tf_op jit(solution)/shard_map/ppermute | solution.py:380
  23.2 14.1 %collective-permute-start.2 = (bf16[2,192,304]{2,1,0:T(8,128)(2,1)S(1)}, bf16[2,192,304]{2,1,0:T(8,128)(2,1)S(1)}, u32[]{:S(2)}, u32[]{:S(2)}) collective-permute-start(bf16[2,192,304]{2,1,0:T(8,128)(2,1)S(1)} %pad_maximum_fusion.1), channel_id=1, source_target_pairs={{0,64},{32,96},{64,0},{96,32},{128,192},{160,224},{192,128},{224,1... | collective-permute-start | bytes 700424 | tf_op jit(solution)/shard_map/ppermute | solution.py:380
  37.4 9.2 %copy-start = (bf16[8,192,304]{2,1,0:T(8,128)(2,1)}, bf16[8,192,304]{2,1,0:T(8,128)(2,1)S(1)}, u32[]{:S(2)}) copy-start(bf16[8,192,304]{2,1,0:T(8,128)(2,1)S(1)} %constant_dynamic-update-slice_fusion.w_ref) | copy-start | bytes 2801668
  37.4 4.1 %copy-start.5 = (bf16[1,128,2048]{2,1,0:T(8,128)(2,1)S(1)}, bf16[1,128,2048]{2,1,0:T(8,128)(2,1)}, u32[]{:S(2)}) copy-start(bf16[1,128,2048]{2,1,0:T(8,128)(2,1)} %param.7) | copy-start | bytes 1572868
  37.4 11.8 %collective-permute-start.5 = (bf16[8,192,304]{2,1,0:T(8,128)(2,1)S(1)}, bf16[8,192,304]{2,1,0:T(8,128)(2,1)}, u32[]{:S(2)}, u32[]{:S(2)}) collective-permute-start(bf16[8,192,304]{2,1,0:T(8,128)(2,1)S(1)} %constant_dynamic-update-slice_fusion.w_ref), channel_id=1, source_target_pairs={{0,1},{1,0},{2,3},{3,2},{4,5},{5,4},{6,7},{7,6},{8,9},{9,8},{10,11... | collective-permute-start | bytes 2801672 | tf_op jit(solution)/shard_map/ppermute | solution.py:398
  41.6 1.0 copy-start.7
  42.6 1.0 copy-start.9
  43.6 1.0 copy-start.11
  47.9 1.3 collective-permute-start.4
  49.3 12.8 %collective-permute-start.6 = (bf16[16,128,128]{2,1,0:T(8,128)(2,1)S(1)}, bf16[16,128,128]{2,1,0:T(8,128)(2,1)S(1)}, u32[]{:S(2)}, u32[]{:S(2)}) collective-permute-start(bf16[16,128,128]{2,1,0:T(8,128)(2,1)S(1)} %slice_bitcast_fusion.1), channel_id=1, source_target_pairs={{0,1},{1,0},{2,3},{3,2},{4,5},{5,4},{6,7},{7,6},{8,9},{9,8},{10,11... | collective-permute-start | bytes 1572872 | tf_op jit(solution)/shard_map/ppermute | solution.py:404
  49.5 45.4 %all-to-all-start.2 = ((bf16[16,2,128,128]{3,2,1,0:T(8,128)(2,1)}), bf16[16,2,128,128]{3,2,1,0:T(8,128)(2,1)S(1)}, u32[]{:S(2)}, u32[]{:S(2)}) async-start(bf16[16,2,128,128]{3,2,1,0:T(8,128)(2,1)} %pack_second.1), calls=%async_computation.2 | async-start | bytes 2097152 | tf_op jit(solution)/shard_map/all_to_all | solution.py:376
  56.8 37.5 %collective-permute-start.7 = (bf16[2,77,304]{2,0,1:T(2,128)(2,1)}, bf16[2,77,304]{2,0,1:T(2,128)(2,1)S(1)}, u32[]{:S(2)}, u32[]{:S(2)}) collective-permute-start(bf16[2,77,304]{2,0,1:T(2,128)(2,1)} %bitcast.64), channel_id=1, source_target_pairs={{0,128},{32,160},{64,192},{96,224},{128,0},{160,32},{192,64},{224,... | collective-permute-start | bytes 280904 | tf_op jit(solution)/shard_map/ppermute | solution.py:406
  94.3 0.6 copy-start.14
  94.9 2.0 %collective-permute-start.8 = (bf16[2240,128]{1,0:T(8,128)(2,1)S(1)}, bf16[2240,128]{1,0:T(8,128)(2,1)S(1)}, u32[]{:S(2)}, u32[]{:S(2)}) collective-permute-start(bf16[2240,128]{1,0:T(8,128)(2,1)S(1)} %get-tuple-element.36.ex0_ref), channel_id=1, source_target_pairs={{0,1},{1,0},{2,3},{3,2},{4,5},{5,4},{6,7},{7,6},{8,9},{9,8},{10,11... | collective-permute-start | bytes 1720328 | tf_op jit(solution)/shard_map/ppermute | solution.py:409
  95.8 10.6 %collective-permute-start.9 = (bf16[16,128,128]{2,1,0:T(8,128)(2,1)}, bf16[16,128,128]{2,1,0:T(8,128)(2,1)}, u32[]{:S(2)}, u32[]{:S(2)}) collective-permute-start(bf16[16,128,128]{2,1,0:T(8,128)(2,1)} %slice_bitcast_fusion), channel_id=1, source_target_pairs={{0,1},{1,0},{2,3},{3,2},{4,5},{5,4},{6,7},{7,6},{8,9},{9,8},{10,11... | collective-permute-start | bytes 1572872 | tf_op jit(solution)/shard_map/ppermute | solution.py:410
  96.9 2.2 %copy-start.2 = (bf16[2240,128]{1,0:T(8,128)(2,1)}, bf16[2240,128]{1,0:T(8,128)(2,1)S(1)}, u32[]{:S(2)}) copy-start(bf16[2240,128]{1,0:T(8,128)(2,1)S(1)} %collective-permute-done.8.got_ref.got0_ref) | copy-start | bytes 1720324
  99.2 50.2 %all-to-all-start.1 = ((bf16[16,256,128]{2,1,0:T(8,128)(2,1)}), bf16[16,256,128]{2,1,0:T(8,128)(2,1)S(1)}, u32[]{:S(2)}, u32[]{:S(2)}) async-start(bf16[16,256,128]{2,1,0:T(8,128)(2,1)} %finish_first.1), calls=%async_computation.1 | async-start | bytes 2097152 | tf_op jit(solution)/shard_map/all_to_all | solution.py:376
  106.4 33.9 %copy-start.3 = (bf16[2240,128]{1,0:T(8,128)(2,1)S(1)}, bf16[2240,128]{1,0:T(8,128)(2,1)}, u32[]{:S(2)}) copy-start(bf16[2240,128]{1,0:T(8,128)(2,1)} %copy-done.2) | copy-start | bytes 1720324
  138.3 2.1 %collective-permute-start.10 = (bf16[2240,128]{1,0:T(8,128)(2,1)S(1)}, bf16[2240,128]{1,0:T(8,128)(2,1)S(1)}, u32[]{:S(2)}, u32[]{:S(2)}) collective-permute-start(bf16[2240,128]{1,0:T(8,128)(2,1)S(1)} %get-tuple-element.39.ex1_ref), channel_id=1, source_target_pairs={{0,1},{1,0},{2,3},{3,2},{4,5},{5,4},{6,7},{7,6},{8,9},{9,8},{10,11... | collective-permute-start | bytes 1720328 | tf_op jit(solution)/shard_map/ppermute | solution.py:413
  140.3 1.6 copy-start.1
  141.0 8.4 %collective-permute-start.11 = (bf16[80,256]{1,0:T(8,128)(2,1)S(1)}, bf16[80,256]{1,0:T(8,128)(2,1)S(1)}, u32[]{:S(2)}, u32[]{:S(2)}) collective-permute-start(bf16[80,256]{1,0:T(8,128)(2,1)S(1)} %get-tuple-element.42.own_ref), channel_id=1, source_target_pairs={{0,128},{32,160},{64,192},{96,224},{128,0},{160,32},{192,64},{224,... | collective-permute-start | bytes 122888 | tf_op jit(solution)/shard_map/ppermute | solution.py:416
  145.1 11.4 %copy-start.12 = (bf16[77,8,304]{2,1,0:T(8,128)(2,1)S(1)}, bf16[77,8,304]{2,1,0:T(8,128)(2,1)}, u32[]{:S(2)}) copy-start(bf16[77,8,304]{2,1,0:T(8,128)(2,1)} %reshape_squeeze.3) | copy-start | bytes 1123588
  145.1 16.4 %copy-start.15 = (bf16[2,77,304]{2,0,1:T(2,128)(2,1)S(1)}, bf16[2,77,304]{2,0,1:T(2,128)(2,1)}, u32[]{:S(2)}) copy-start(bf16[2,77,304]{2,0,1:T(2,128)(2,1)} %copy-done.14) | copy-start | bytes 280900
  149.4 36.6 %all-to-all-start.3 = ((bf16[16,336,128]{2,1,0:T(8,128)(2,1)}), bf16[16,336,128]{2,1,0:T(8,128)(2,1)S(1)}, u32[]{:S(2)}, u32[]{:S(2)}) async-start(bf16[16,336,128]{2,1,0:T(8,128)(2,1)} %finish_last.1), calls=%async_computation.3 | async-start | bytes 2752512 | tf_op jit(solution)/shard_map/all_to_all | solution.py:376
  157.4 13.5 %collective-permute-start.18 = (bf16[2,80,256]{2,1,0:T(8,128)(2,1)S(1)}, bf16[2,80,256]{2,1,0:T(8,128)(2,1)S(1)}, u32[]{:S(2)}, u32[]{:S(2)}) collective-permute-start(bf16[2,80,256]{2,1,0:T(8,128)(2,1)S(1)} %pad_maximum_fusion.2), channel_id=1, source_target_pairs={{0,96},{32,0},{64,32},{96,64},{128,224},{160,128},{192,160},{224,1... | collective-permute-start | bytes 245768 | tf_op jit(solution)/shard_map/ppermute | solution.py:380
  158.3 6.6 %collective-permute-start.17 = (bf16[2,80,256]{2,1,0:T(8,128)(2,1)S(1)}, bf16[2,80,256]{2,1,0:T(8,128)(2,1)S(1)}, u32[]{:S(2)}, u32[]{:S(2)}) collective-permute-start(bf16[2,80,256]{2,1,0:T(8,128)(2,1)S(1)} %pad_maximum_fusion.2), channel_id=1, source_target_pairs={{0,64},{32,96},{64,0},{96,32},{128,192},{160,224},{192,128},{224,1... | collective-permute-start | bytes 245768 | tf_op jit(solution)/shard_map/ppermute | solution.py:380
  159.0 5.8 %collective-permute-start.16 = (bf16[2,80,256]{2,1,0:T(8,128)(2,1)S(1)}, bf16[2,80,256]{2,1,0:T(8,128)(2,1)S(1)}, u32[]{:S(2)}, u32[]{:S(2)}) collective-permute-start(bf16[2,80,256]{2,1,0:T(8,128)(2,1)S(1)} %pad_maximum_fusion.2), channel_id=1, source_target_pairs={{0,32},{32,64},{64,96},{96,0},{128,160},{160,192},{192,224},{224,1... | collective-permute-start | bytes 245768 | tf_op jit(solution)/shard_map/ppermute | solution.py:380
  161.6 3.3 %collective-permute-start.12 = (bf16[2,77,304]{2,0,1:T(2,128)(2,1)S(1)}, bf16[2,77,304]{2,0,1:T(2,128)(2,1)S(1)}, u32[]{:S(2)}, u32[]{:S(2)}) collective-permute-start(bf16[2,77,304]{2,0,1:T(2,128)(2,1)S(1)} %copy-done.15), channel_id=1, source_target_pairs={{0,1},{1,0},{2,3},{3,2},{4,5},{5,4},{6,7},{7,6},{8,9},{9,8},{10,11... | collective-permute-start | bytes 280904 | tf_op jit(solution)/shard_map/ppermute | solution.py:420
  166.8 6.2 %collective-permute-start.15 = (bf16[2,77,304]{2,1,0:T(8,128)(2,1)S(1)}, bf16[2,77,304]{2,1,0:T(8,128)(2,1)S(1)}, u32[]{:S(2)}, u32[]{:S(2)}) collective-permute-start(bf16[2,77,304]{2,1,0:T(8,128)(2,1)S(1)} %bitcast.86), channel_id=1, source_target_pairs={{0,96},{32,0},{64,32},{96,64},{128,224},{160,128},{192,160},{224,1... | collective-permute-start | bytes 280904 | tf_op jit(solution)/shard_map/ppermute | solution.py:425
  169.2 6.4 %collective-permute-start.14 = (bf16[2,77,304]{2,1,0:T(8,128)(2,1)S(1)}, bf16[2,77,304]{2,1,0:T(8,128)(2,1)S(1)}, u32[]{:S(2)}, u32[]{:S(2)}) collective-permute-start(bf16[2,77,304]{2,1,0:T(8,128)(2,1)S(1)} %bitcast.85), channel_id=1, source_target_pairs={{0,64},{32,96},{64,0},{96,32},{128,192},{160,224},{192,128},{224,1... | collective-permute-start | bytes 280904 | tf_op jit(solution)/shard_map/ppermute | solution.py:425
  169.8 5.8 %collective-permute-start.13 = (bf16[2,77,304]{2,1,0:T(8,128)(2,1)S(1)}, bf16[2,77,304]{2,1,0:T(8,128)(2,1)S(1)}, u32[]{:S(2)}, u32[]{:S(2)}) collective-permute-start(bf16[2,77,304]{2,1,0:T(8,128)(2,1)S(1)} %bitcast.84), channel_id=1, source_target_pairs={{0,32},{32,64},{64,96},{96,0},{128,160},{160,192},{192,224},{224,1... | collective-permute-start | bytes 280904 | tf_op jit(solution)/shard_map/ppermute | solution.py:425

commit v3 on v2

--- a/solution.py
+++ b/solution.py
@@ -17,6 +17,7 @@
 TXT = 77
 TXT_ROWS = 80
 TXT_PAD = 128
+DX_ROWS = 48
 TXT_HALF = TXT_PAD // 2
 KEYS = IMG + TXT_PAD
 STEPS = 4
@@ -41,8 +42,8 @@
     return jnp.concatenate([x[..., 64:], x[..., :64]], axis=-1)
 
 
-def params():
-    return pltpu.CompilerParams(vmem_limit_bytes=VMEM)
+def params(limit=VMEM):
+    return pltpu.CompilerParams(vmem_limit_bytes=limit)
 
 
 def whole(shape):
@@ -76,14 +77,19 @@
         out_specs=pl.BlockSpec((CHIPS // grid, 2, TOK, 128), lambda i: (i, 0, 0, 0)),
         name=("pack_first", "pack_second")[phase],
         cost_estimate=cost(3),
-        compiler_params=params(),
+        compiler_params=params(60 << 20),
     )(q, k, v, g)
 
 
-def project_kernel(ids_ref, x_ref, w_ref, g_ref, out_ref):
+def project_kernel(ids_ref, x_ref, w_ref, g_ref, out_ref, x8_ref, half_ref):
     total = jnp.zeros((TXT, w_ref.shape[1]), f32)
-    for r in range(w_ref.shape[0]):
-        total += dot(x_ref[ids_ref[1 + r]], w_ref[r], 1, 1)
+    n = w_ref.shape[2]
+    for d in range(w_ref.shape[0]):
+        x = x_ref[:, n * d : n * d + n]
+        x8_ref[d] = x
+        total += dot(x, w_ref[ids_ref[9 + d]], 1, 1)
+    for i in range(half_ref.shape[0]):
+        half_ref[i] = x8_ref[ids_ref[17] + i]
     total = total.astype(bf16)
     q = total[:, :64] * jnp.asarray(0.125, bf16)
     out_ref[...] = jnp.zeros_like(out_ref)
@@ -91,16 +97,20 @@
     out_ref[TXT_PAD : TXT_PAD + TXT] = total[:, 64:]
 
 
-def project(ids, x8, w, g):
+def project(ids, x, w, g):
     return pl.pallas_call(
         project_kernel,
-        out_shape=SDS((2 * TXT_PAD, 128), bf16),
+        out_shape=(
+            SDS((2 * TXT_PAD, 128), bf16),
+            SDS((w.shape[0], TXT, w.shape[2]), bf16),
+            SDS((2, TXT, w.shape[2]), bf16),
+        ),
         in_specs=[IN_SMEM] + [IN_VMEM] * 3,
-        out_specs=IN_VMEM,
+        out_specs=(IN_VMEM,) * 3,
         name="project",
         cost_estimate=cost(3),
         compiler_params=params(),
-    )(ids, x8, w, g)
+    )(ids, x, w, g)
 
 
 def key_chunks():
@@ -161,9 +171,17 @@
         left = jnp.concatenate([high, row_term - high, jnp.zeros((62, rows), f32), gt.astype(f32)], axis=0)
         left = left.astype(bf16).T
         dqt = jnp.zeros((64, rows), f32)
-        for j, n in key_chunks():
+        chunks = key_chunks()
+
+        def prob_grads(k):
+            return dot(left, values[:, chunks[k][0] : chunks[k][0] + chunks[k][1]], 1, 0)
+
+        dp = prob_grads(0)
+        for k, (j, n) in enumerate(chunks):
             e = e_ref[:rows, j : j + n]
-            ds = e * dot(left, values[:, j : j + n], 1, 0).astype(bf16)
+            ds = e * dp.astype(bf16)
+            if k + 1 < len(chunks):
+                dp = prob_grads(k + 1)
             dqt = dqt + dot(kvt[0:64, j : j + n], ds, 1, 1)
             acc[0:64, j : j + n] += dot(qgt[0:64], ds, 1, 0)
             acc[64:128, j : j + n] += dot(gt, e, 1, 0)
@@ -271,6 +289,21 @@
     )(ids, *shares)
 
 
+def fold(x, n):
+    lane = lax.broadcasted_iota(jnp.int32, (1, 128), 1)
+    m = 2 * n - 128
+    tail = jnp.where(lane < n + m, pltpu.roll(x[48:64], m, 1), pltpu.roll(x[64:80], 2 * m, 1))
+    beside = jnp.concatenate([pltpu.roll(x[48:80], n, 1), tail], axis=0)
+    return jnp.where(lane < n, x[:48], beside)
+
+
+def unfold(x, n):
+    lane = lax.broadcasted_iota(jnp.int32, (1, 128), 1)
+    m = 2 * n - 128
+    tail = jnp.concatenate([pltpu.roll(x[32:48], 128 - m, 1), pltpu.roll(x[32:48], 128 - 2 * m, 1)], axis=0)
+    return jnp.concatenate([x, jnp.where(lane < 128 - n, pltpu.roll(x[:32], 128 - n, 1), tail)], axis=0)
+
+
 def finish_last_kernel(ids_ref, y_in, got_ref, own_ref, other_ref, w_ref, w_other_ref, y_ref):
     y_ref[:, :TOK] = y_in[:, :TOK]
     add_shares(y_in.at[:, TOK : 2 * TOK], got_ref, y_ref.at[:, TOK : 2 * TOK])
@@ -282,7 +315,7 @@
             at = 2 * n * i
             piece = jnp.where(first, total[:, at : at + n], total[:, at + n : at + 2 * n])
             piece = jnp.concatenate([piece, jnp.zeros((TXT_ROWS, 128 - n), f32)], axis=1)
-            y_ref[2 * ids_ref[1 + r] + i, 2 * TOK :] = piece.astype(bf16)
+            y_ref[2 * ids_ref[1 + r] + i, 2 * TOK :] = fold(piece, n).astype(bf16)
 
 
 def finish_last(ids, y, got, own, other, w, w_other):
@@ -300,7 +333,7 @@
 def unpack_kernel(z0_ref, z1_ref, o_ref, g_ref, dx_ref, acc):
     low = low_lanes()
     step = pl.program_id(0)
-    total = jnp.zeros((TXT_ROWS, 128), f32)
+    total = jnp.zeros((DX_ROWS, 128), f32)
     for c in range(z0_ref.shape[0]):
         cols = slice(128 * c, 128 * c + 128)
         qo0, qo1 = z0_ref[c, :TOK], z1_ref[c, :TOK]
@@ -321,7 +354,7 @@
 
     @pl.when(step == pl.num_programs(0) - 1)
     def _():
-        dx_ref[...] = acc[...].T[: dx_ref.shape[0], :TXT].reshape(dx_ref.shape)
+        dx_ref[...] = unfold(acc[...], dx_ref.shape[0]).T[: dx_ref.shape[0], :TXT].reshape(dx_ref.shape)
 
 
 def unpack(z0, z1, dx_cols):
@@ -337,7 +370,7 @@
             pl.BlockSpec((3, TOK, width // grid), lambda i: (0, 0, i)),
             whole((dx_cols, 1, TXT)),
         ),
-        scratch_shapes=[pltpu.VMEM((TXT_ROWS, 128), f32)],
+        scratch_shapes=[pltpu.VMEM((DX_ROWS, 128), f32)],
         name="unpack",
         cost_estimate=cost(4),
         compiler_params=params(),
@@ -380,20 +413,18 @@
         return jnp.concatenate([both] + [lax.ppermute(both, "dp", t) for t in turns])
 
     order = [(dp_hi ^ side) * 4 + (dp_lo + 4 - k) % 4 for k in range(4) for side in range(2)]
-    ids = jnp.stack([core] + order).astype(jnp.int32)
+    place = [2 * ((dp_lo + 4 - d % 4) % 4) + (dp_hi ^ (d // 4)) for d in range(8)]
+    ids = jnp.stack([core] + order + place + [4 * (1 - dp_hi) + 2 * core]).astype(jnp.int32)
     image = (q_img[0], k_img[0], v_img[0], grad_img[0])
 
     w_own = jnp.swapaxes(w_txt, 1, 2).reshape(192, -1)
     w_across = lax.ppermute(w_own, "dp", across)
 
-    x8 = x_txt[0].reshape(TXT, 8, -1).transpose(1, 0, 2)
-    halves = x8.reshape(4, 2, TXT, -1)
-    half = lax.dynamic_index_in_dim(halves, 2 * (1 - dp_hi) + core, 0, keepdims=False)
     packed = pack(0, *image, 4)
     packed, w_across = lax.optimization_barrier((packed, w_across))
     r0 = exchange(packed)
     weights = around(w_own, w_across)
-    text = project(ids, x8, weights, grad_txt[0])
+    text, x8, half = project(ids, x_txt[0], weights, grad_txt[0])
     text_other = lax.ppermute(text, "seq", pair)
     weights_other = lax.ppermute(weights, "seq", pair)
     second = pack(1, *image, 4)
@@ -409,7 +440,7 @@
     got0 = lax.ppermute(ex0, "seq", pair)
     kv1 = lax.ppermute(r1[:, 1], "seq", pair)
     z0 = exchange(finish_first(y0, got0))
-    y1, ex1, dt1 = attend(1, ids, r1, kv1, text, text_other, 2 * TOK + TXT_ROWS)
+    y1, ex1, dt1 = attend(1, ids, r1, kv1, text, text_other, 2 * TOK + DX_ROWS)
     got1 = lax.ppermute(ex1, "seq", pair)
 
     grads_own, grads_other, o_txt = text_grads(ids, (ex0, got0, dt0, ex1, got1, dt1))

time: 192 us -> 186 us (0.969)
  local copies, waits for them, and re-layouts: 14.6 us -> 7.85 us
  starting transfers between devices: 56 us -> 58.5 us
    pallas_call x2, Pallas kernels: 3.95 us -> 7.73 us  [pack(): pl.pallas_call(functools.partial(pack_kernel, phase), grid=(grid,), out_s...]
    another operation x3 -> x1, local copies, waits for them, and re-layouts: 3.8 us -> 0.1 us  [local(): jnp.stack([core] + order + place + [4 * (1 - dp_hi) + 2 * core])]
    unnamed x48 -> x38, local copies, waits for them, and re-layouts: 9.01 us -> 5.99 us
    pallas_call x2, Pallas kernels: 64 us -> 61.6 us  [attend(): pl.pallas_call(functools.partial(attend_kernel, phase), grid=(STEPS,), ou...]
  transfers between devices with their start and end apart: 23 -> 23, of which waited for: 10 -> 12; matrix products, arithmetic and copies ran while one was open for 5% -> 1% of each run, Pallas kernels for 41% -> 42%
where the time goes in v3:
time: 186 us; the launch traced here: 183 us
  Pallas kernels  80 us (43%)
  starting transfers between devices  58.5 us (31%)
  waiting for transfers between devices  35 us (19%)
  local copies, waits for them, and re-layouts  7.85 us (4%)
    pallas_call x2, Pallas kernels, attend(): pl.pallas_call(functools.partial(attend_kernel, phase), grid=(STEPS,), ou...  61.6 us
    all_to_all x4, starting transfers between devices, exchange(): return lax.all_to_all(x, 'seq', 0, 0, axis_index_groups=parity, tiled=True)  29.8 us
    ppermute x6, waiting for transfers between devices, around(): lax.ppermute(both, 'dp', t)  14.4 us
    ppermute x6, starting transfers between devices, around(): lax.ppermute(both, 'dp', t)  9.19 us
    all_to_all x4, waiting for transfers between devices, exchange(): return lax.all_to_all(x, 'seq', 0, 0, axis_index_groups=parity, tiled=True)  8.53 us
    pallas_call x2, Pallas kernels, pack(): pl.pallas_call(functools.partial(pack_kernel, phase), grid=(grid,), out_s...  7.73 us
    ppermute x1, starting transfers between devices, local(): w_across = lax.ppermute(w_own, 'dp', across)  7.28 us
    unnamed x38, local copies, waits for them, and re-layouts  5.99 us
  transfers between devices with their start and end apart: 23, of which 12 were waited for; matrix products, arithmetic and copies ran while one was open for 1% of the time, Pallas kernels for 42%

profile of v3, /device:TPU:8, one launch (start us, length us, event | category | flops | bytes accessed | tf_op | source)
XLA Modules:
  0.0 182.8 jit_solution(6214924692976970190)
XLA Ops:
  0.6 7.3 %collective-permute-start = (bf16[192,304]{1,0:T(8,128)(2,1)}, bf16[192,304]{1,0:T(8,128)(2,1)S(1)}, u32[]{:S(2)}, u32[]{:S(2)}) collective-permute-start(bf16[192,304]{1,0:T(8,128)(2,1)} %bitcast.66), channel_id=1, source_target_pairs={{0,128},{32,160},{64,192},{96,224},{128,0},{160,32},{192,64},{224,... | collective-permute-start | bytes 350216 | tf_op jit(solution)/shard_map/ppermute | solution.py:421
  7.9 3.9 %pack_first.1 = bf16[16,2,128,128]{3,2,1,0:T(8,128)(2,1)} custom-call(bf16[128,2048]{1,0:T(8,128)(2,1)} %bitcast.73, bf16[128,2048]{1,0:T(8,128)(2,1)} %bitcast.75, bf16[128,2048]{1,0:T(8,128)(2,1)} %bitcast.77, bf16[128,2048]{1,0:T(8,128)(2,1)} %bitcast.79), custom_call_target="tpu_custom_call" | custom-call | flops 3449999872 | bytes 1048576 | tf_op jit(solution)/shard_map/pack_first/pallas_call | solution.py:72
  11.8 0.3 collective-permute-done
  12.1 8.9 %all-to-all-start = ((bf16[16,2,128,128]{3,2,1,0:T(8,128)(2,1)}), bf16[16,2,128,128]{3,2,1,0:T(8,128)(2,1)S(1)}, u32[]{:S(2)}, u32[]{:S(2)}) async-start(bf16[16,2,128,128]{3,2,1,0:T(8,128)(2,1)} %pack_first.1), calls=%async_computation | async-start | bytes 2097152 | tf_op jit(solution)/shard_map/all_to_all | solution.py:409
  21.0 1.7 collective-permute-start.1
  22.7 0.5 collective-permute-start.3
  23.2 2.3 %collective-permute-start.2 = (bf16[2,192,304]{2,1,0:T(8,128)(2,1)S(1)}, bf16[2,192,304]{2,1,0:T(8,128)(2,1)S(1)}, u32[]{:S(2)}, u32[]{:S(2)}) collective-permute-start(bf16[2,192,304]{2,1,0:T(8,128)(2,1)S(1)} %pad_maximum_fusion.1), channel_id=1, source_target_pairs={{0,64},{32,96},{64,0},{96,32},{128,192},{160,224},{192,128},{224,1... | collective-permute-start | bytes 700424 | tf_op jit(solution)/shard_map/ppermute | solution.py:413
  25.5 5.5 %collective-permute-done.1 = bf16[2,192,304]{2,1,0:T(8,128)(2,1)S(1)} collective-permute-done((bf16[2,192,304]{2,1,0:T(8,128)(2,1)S(1)}, bf16[2,192,304]{2,1,0:T(8,128)(2,1)S(1)}, u32[]{:S(2)}, u32[]{:S(2)}) %collective-permute-start.1) | collective-permute-done | bytes 233504 | tf_op jit(solution)/shard_map/ppermute | solution.py:413
  31.1 6.2 %collective-permute-done.2 = bf16[2,192,304]{2,1,0:T(8,128)(2,1)S(1)} collective-permute-done((bf16[2,192,304]{2,1,0:T(8,128)(2,1)S(1)}, bf16[2,192,304]{2,1,0:T(8,128)(2,1)S(1)}, u32[]{:S(2)}, u32[]{:S(2)}) %collective-permute-start.2) | collective-permute-done | bytes 233504 | tf_op jit(solution)/shard_map/ppermute | solution.py:413
  37.9 1.3 project.1
  39.2 0.5 collective-permute-start.4
  39.6 3.9 %pack_second.1 = bf16[16,2,128,128]{3,2,1,0:T(8,128)(2,1)} custom-call(bf16[128,2048]{1,0:T(8,128)(2,1)} %bitcast.74, bf16[128,2048]{1,0:T(8,128)(2,1)} %bitcast.76, bf16[128,2048]{1,0:T(8,128)(2,1)} %bitcast.78, bf16[128,2048]{1,0:T(8,128)(2,1)} %bitcast.80), custom_call_target="tpu_custom_call" | custom-call | flops 3449999872 | bytes 1048576 | tf_op jit(solution)/shard_map/pack_second/pallas_call | solution.py:72
  43.5 0.6 copy-done.8
  44.2 0.8 all-to-all-done.q_ref.own_kv_ref
  44.9 0.8 slice_bitcast_fusion.1
  45.8 6.6 %all-to-all-start.2 = ((bf16[16,2,128,128]{3,2,1,0:T(8,128)(2,1)}), bf16[16,2,128,128]{3,2,1,0:T(8,128)(2,1)S(1)}, u32[]{:S(2)}, u32[]{:S(2)}) async-start(bf16[16,2,128,128]{3,2,1,0:T(8,128)(2,1)} %pack_second.1), calls=%async_computation.2 | async-start | bytes 2097152 | tf_op jit(solution)/shard_map/all_to_all | solution.py:409
  52.4 5.3 %collective-permute-start.7 = (bf16[2,77,304]{2,1,0:T(8,128)(2,1)S(1)}, bf16[2,77,304]{2,1,0:T(8,128)(2,1)S(1)}, u32[]{:S(2)}, u32[]{:S(2)}) collective-permute-start(bf16[2,77,304]{2,1,0:T(8,128)(2,1)S(1)} %get-tuple-element.40), channel_id=1, source_target_pairs={{0,128},{32,160},{64,192},{96,224},{128,0},{160,32},{192,64},{224,... | collective-permute-start | bytes 280904 | tf_op jit(solution)/shard_map/ppermute | solution.py:437
  57.7 0.8 copy-done.5
  58.5 1.0 copy-done.6
  59.6 31.0 %attend_first.1 = (bf16[16,256,128]{2,1,0:T(8,128)(2,1)}, bf16[2240,128]{1,0:T(8,128)(2,1)S(1)}, f32[128,128]{1,0:T(8,128)S(1)}) custom-call(s32[18]{0:T(128)S(1)} %stack.97.ids_ref, bf16[16,2,128,128]{3,2,1,0:T(8,128)(2,1)S(1)} %all-to-all-done.q_ref.own_kv_ref, bf16[16,2,128,128]{3,2,1,0:T(8,128)(2,1)S(1)} %all-to-all-done.q_ref.own_kv_ref, ...), custom_call_target="tpu_custom_call" | custom-call | flops 39099998208 | bytes 1048576 | tf_op jit(solution)/shard_map/attend_first/pallas_call | solution.py:206
  90.5 0.6 copy-done.11
  91.2 0.8 slice_bitcast_fusion
  92.0 0.5 collective-permute-start.9
  92.5 0.6 collective-permute-done.8.got_ref.got0_ref
  93.2 0.8 copy-done.2
  94.0 1.1 copy-done.3
  95.0 2.0 %finish_first.1 = bf16[16,256,128]{2,1,0:T(8,128)(2,1)} custom-call(bf16[16,256,128]{2,1,0:T(8,128)(2,1)} %get-tuple-element.38.y_in, bf16[2240,128]{1,0:T(8,128)(2,1)S(1)} %copy-done.3), custom_call_target="tpu_custom_call", output_to_operand_aliasing={{}: (0, {})} | custom-call | flops 2300000000 | bytes 1048576 | tf_op jit(solution)/shard_map/finish_first/pallas_call | solution.py:245
  97.0 7.3 %all-to-all-start.1 = ((bf16[16,256,128]{2,1,0:T(8,128)(2,1)}), bf16[16,256,128]{2,1,0:T(8,128)(2,1)S(1)}, u32[]{:S(2)}, u32[]{:S(2)}) async-start(bf16[16,256,128]{2,1,0:T(8,128)(2,1)} %finish_first.1), calls=%async_computation.1 | async-start | bytes 2097152 | tf_op jit(solution)/shard_map/all_to_all | solution.py:409
  104.3 30.6 %attend_second.1 = (bf16[16,304,128]{2,1,0:T(8,128)(2,1)S(1)}, bf16[2240,128]{1,0:T(8,128)(2,1)S(1)}, f32[128,128]{1,0:T(8,128)S(1)}) custom-call(s32[18]{0:T(128)S(1)} %stack.97.ids_ref, bf16[16,2,128,128]{3,2,1,0:T(8,128)(2,1)S(1)} %all-to-all-done.2.q_ref.own_kv_ref, bf16[16,2,128,128]{3,2,1,0:T(8,128)(2,1)S(1)} %all-to-all-done.2.q_ref.own_kv_ref, ...), custom_call_target="tpu_custom_call" | custom-call | flops 39099998208 | bytes 1048576 | tf_op jit(solution)/shard_map/attend_second/pallas_call | solution.py:206
  135.0 2.0 %collective-permute-done.10.got1_ref.got_ref = bf16[2240,128]{1,0:T(8,128)(2,1)S(1)} collective-permute-done((bf16[2240,128]{1,0:T(8,128)(2,1)S(1)}, bf16[2240,128]{1,0:T(8,128)(2,1)S(1)}, u32[]{:S(2)}, u32[]{:S(2)}) %collective-permute-start.10) | collective-permute-done | bytes 573472 | tf_op jit(solution)/shard_map/ppermute | solution.py:444
  137.0 0.6 text_grads.1
  137.6 1.0 collective-permute-start.11
  138.6 3.2 %finish_last.1 = bf16[16,304,128]{2,1,0:T(8,128)(2,1)} custom-call(s32[18]{0:T(128)S(1)} %stack.97.ids_ref, bf16[16,304,128]{2,1,0:T(8,128)(2,1)S(1)} %get-tuple-element.43.y_in, bf16[2240,128]{1,0:T(8,128)(2,1)S(1)} %collective-permute-done.10.got1_ref.got_ref, bf16[80,256]{1,0:T(8,128)(2,1)S(1)} %get-tuple-element.47.own_ref, ...), custom_call_target="tpu_custom_call" | custom-call | flops 5750000128 | bytes 1048576 | tf_op jit(solution)/shard_map/finish_last/pallas_call | solution.py:322
  141.8 4.2 %collective-permute-done.11 = bf16[80,256]{1,0:T(8,128)(2,1)S(1)} collective-permute-done((bf16[80,256]{1,0:T(8,128)(2,1)S(1)}, bf16[80,256]{1,0:T(8,128)(2,1)S(1)}, u32[]{:S(2)}, u32[]{:S(2)}) %collective-permute-start.11) | collective-permute-done | bytes 40992 | tf_op jit(solution)/shard_map/ppermute | solution.py:447
  146.0 7.1 %all-to-all-start.3 = ((bf16[16,304,128]{2,1,0:T(8,128)(2,1)}), bf16[16,304,128]{2,1,0:T(8,128)(2,1)S(1)}, u32[]{:S(2)}, u32[]{:S(2)}) async-start(bf16[16,304,128]{2,1,0:T(8,128)(2,1)} %finish_last.1), calls=%async_computation.3 | async-start | bytes 2490368 | tf_op jit(solution)/shard_map/all_to_all | solution.py:409
  153.3 0.7 copy.25
  154.0 0.8 collective-permute-start.18
  154.8 2.0 %collective-permute-start.17 = (bf16[2,80,256]{2,1,0:T(8,128)(2,1)S(1)}, bf16[2,80,256]{2,1,0:T(8,128)(2,1)S(1)}, u32[]{:S(2)}, u32[]{:S(2)}) collective-permute-start(bf16[2,80,256]{2,1,0:T(8,128)(2,1)S(1)} %pad_maximum_fusion.2), channel_id=1, source_target_pairs={{0,64},{32,96},{64,0},{96,32},{128,192},{160,224},{192,128},{224,1... | collective-permute-start | bytes 245768 | tf_op jit(solution)/shard_map/ppermute | solution.py:413
  156.8 1.9 %collective-permute-start.16 = (bf16[2,80,256]{2,1,0:T(8,128)(2,1)S(1)}, bf16[2,80,256]{2,1,0:T(8,128)(2,1)S(1)}, u32[]{:S(2)}, u32[]{:S(2)}) collective-permute-start(bf16[2,80,256]{2,1,0:T(8,128)(2,1)S(1)} %pad_maximum_fusion.2), channel_id=1, source_target_pairs={{0,32},{32,64},{64,96},{96,0},{128,160},{160,192},{192,224},{224,1... | collective-permute-start | bytes 245768 | tf_op jit(solution)/shard_map/ppermute | solution.py:413
  158.7 2.7 %collective-permute-done.16 = bf16[2,80,256]{2,1,0:T(8,128)(2,1)S(1)} collective-permute-done((bf16[2,80,256]{2,1,0:T(8,128)(2,1)S(1)}, bf16[2,80,256]{2,1,0:T(8,128)(2,1)S(1)}, u32[]{:S(2)}, u32[]{:S(2)}) %collective-permute-start.16) | collective-permute-done | bytes 81952 | tf_op jit(solution)/shard_map/ppermute | solution.py:413
  161.7 1.8 collective-permute-start.13
  163.4 3.0 %collective-permute-start.14 = (bf16[2,77,304]{2,1,0:T(8,128)(2,1)S(1)}, bf16[2,77,304]{2,1,0:T(8,128)(2,1)S(1)}, u32[]{:S(2)}, u32[]{:S(2)}) collective-permute-start(bf16[2,77,304]{2,1,0:T(8,128)(2,1)S(1)} %get-tuple-element.71), channel_id=1, source_target_pairs={{0,64},{32,96},{64,0},{96,32},{128,192},{160,224},{192,128},{224,1... | collective-permute-start | bytes 280904 | tf_op jit(solution)/shard_map/ppermute | solution.py:456
  166.4 1.1 collective-permute-done.13
  167.5 2.3 %collective-permute-done.14 = bf16[2,77,304]{2,1,0:T(8,128)(2,1)S(1)} collective-permute-done((bf16[2,77,304]{2,1,0:T(8,128)(2,1)S(1)}, bf16[2,77,304]{2,1,0:T(8,128)(2,1)S(1)}, u32[]{:S(2)}, u32[]{:S(2)}) %collective-permute-start.14) | collective-permute-done | bytes 93664 | tf_op jit(solution)/shard_map/ppermute | solution.py:456
  169.8 1.5 collective-permute-done.15
  171.4 1.2 weight_grad.1
  172.6 7.8 %all-to-all-done.3.z1_ref = bf16[16,304,128]{2,1,0:T(8,128)(2,1)S(1)} async-done(((bf16[16,304,128]{2,1,0:T(8,128)(2,1)}), bf16[16,304,128]{2,1,0:T(8,128)(2,1)S(1)}, u32[]{:S(2)}, u32[]{:S(2)}) %all-to-all-start.3) | async-done | bytes 1245216 | tf_op jit(solution)/shard_map/all_to_all | solution.py:409
  180.4 2.4 %unpack.1 = (bf16[128,2048]{1,0:T(8,128)(2,1)}, bf16[3,128,2048]{2,1,0:T(8,128)(2,1)}, f32[76,1,77]{2,1,0:T(1,128)}) custom-call(bf16[16,256,128]{2,1,0:T(8,128)(2,1)S(1)} %all-to-all-done.1.z0_ref, bf16[16,304,128]{2,1,0:T(8,128)(2,1)S(1)} %all-to-all-done.3.z1_ref), custom_call_target="tpu_custom_call" | custom-call | flops 4600000000 | bytes 1048576 | tf_op jit(solution)/shard_map/unpack/pallas_call | solution.py:363
  (57 shorter events, 1.1 us)
Async XLA Ops:
  0.6 11.4 %collective-permute-start = (bf16[192,304]{1,0:T(8,128)(2,1)}, bf16[192,304]{1,0:T(8,128)(2,1)S(1)}, u32[]{:S(2)}, u32[]{:S(2)}) collective-permute-start(bf16[192,304]{1,0:T(8,128)(2,1)} %bitcast.66), channel_id=1, source_target_pairs={{0,128},{32,160},{64,192},{96,224},{128,0},{160,32},{192,64},{224,... | collective-permute-start | bytes 350216 | tf_op jit(solution)/shard_map/ppermute | solution.py:421
  11.8 9.2 %copy-start.10 = (bf16[3,304,64]{1,2,0:T(8,128)(2,1)S(1)}, bf16[3,304,64]{1,2,0:T(8,128)(2,1)}, u32[]{:S(2)}) copy-start(bf16[3,304,64]{1,2,0:T(8,128)(2,1)} %param.11) | copy-start | bytes 350212
  12.1 32.8 %all-to-all-start = ((bf16[16,2,128,128]{3,2,1,0:T(8,128)(2,1)}), bf16[16,2,128,128]{3,2,1,0:T(8,128)(2,1)S(1)}, u32[]{:S(2)}, u32[]{:S(2)}) async-start(bf16[16,2,128,128]{3,2,1,0:T(8,128)(2,1)} %pack_first.1), calls=%async_computation | async-start | bytes 2097152 | tf_op jit(solution)/shard_map/all_to_all | solution.py:409
  21.0 10.0 %collective-permute-start.1 = (bf16[2,192,304]{2,1,0:T(8,128)(2,1)S(1)}, bf16[2,192,304]{2,1,0:T(8,128)(2,1)S(1)}, u32[]{:S(2)}, u32[]{:S(2)}) collective-permute-start(bf16[2,192,304]{2,1,0:T(8,128)(2,1)S(1)} %pad_maximum_fusion.1), channel_id=1, source_target_pairs={{0,32},{32,64},{64,96},{96,0},{128,160},{160,192},{192,224},{224,1... | collective-permute-start | bytes 700424 | tf_op jit(solution)/shard_map/ppermute | solution.py:413
  22.7 15.0 %copy-start.13 = (bf16[1,77,64]{1,2,0:T(8,128)(2,1)S(1)}, bf16[1,77,64]{1,2,0:T(8,128)(2,1)}, u32[]{:S(2)}) copy-start(bf16[1,77,64]{1,2,0:T(8,128)(2,1)} %param.13) | copy-start | bytes 29572
  22.7 15.2 %copy-start.7 = (bf16[1,77,2432]{2,1,0:T(8,128)(2,1)S(1)}, bf16[1,77,2432]{2,1,0:T(8,128)(2,1)}, u32[]{:S(2)}) copy-start(bf16[1,77,2432]{2,1,0:T(8,128)(2,1)} %param.10) | copy-start | bytes 1123588
  22.7 14.7 %collective-permute-start.3 = (bf16[2,192,304]{2,1,0:T(8,128)(2,1)S(1)}, bf16[2,192,304]{2,1,0:T(8,128)(2,1)S(1)}, u32[]{:S(2)}, u32[]{:S(2)}) collective-permute-start(bf16[2,192,304]{2,1,0:T(8,128)(2,1)S(1)} %pad_maximum_fusion.1), channel_id=1, source_target_pairs={{0,96},{32,0},{64,32},{96,64},{128,224},{160,128},{192,160},{224,1... | collective-permute-start | bytes 700424 | tf_op jit(solution)/shard_map/ppermute | solution.py:413
  23.2 14.1 %collective-permute-start.2 = (bf16[2,192,304]{2,1,0:T(8,128)(2,1)S(1)}, bf16[2,192,304]{2,1,0:T(8,128)(2,1)S(1)}, u32[]{:S(2)}, u32[]{:S(2)}) collective-permute-start(bf16[2,192,304]{2,1,0:T(8,128)(2,1)S(1)} %pad_maximum_fusion.1), channel_id=1, source_target_pairs={{0,64},{32,96},{64,0},{96,32},{128,192},{160,224},{192,128},{224,1... | collective-permute-start | bytes 700424 | tf_op jit(solution)/shard_map/ppermute | solution.py:413
  37.4 1.7 copy-start
  37.4 6.7 %collective-permute-start.5 = (bf16[8,192,304]{2,1,0:T(8,128)(2,1)S(1)}, bf16[8,192,304]{2,1,0:T(8,128)(2,1)}, u32[]{:S(2)}, u32[]{:S(2)}) collective-permute-start(bf16[8,192,304]{2,1,0:T(8,128)(2,1)S(1)} %constant_dynamic-update-slice_fusion.w_ref), channel_id=1, source_target_pairs={{0,1},{1,0},{2,3},{3,2},{4,5},{5,4},{6,7},{7,6},{8,9},{9,8},{10,11... | collective-permute-start | bytes 2801672 | tf_op jit(solution)/shard_map/ppermute | solution.py:429
  39.2 4.4 %collective-permute-start.4 = (bf16[256,128]{1,0:T(8,128)(2,1)S(1)}, bf16[256,128]{1,0:T(8,128)(2,1)S(1)}, u32[]{:S(2)}, u32[]{:S(2)}) collective-permute-start(bf16[256,128]{1,0:T(8,128)(2,1)S(1)} %get-tuple-element.34.text_ref), channel_id=1, source_target_pairs={{0,1},{1,0},{2,3},{3,2},{4,5},{5,4},{6,7},{7,6},{8,9},{9,8},{10,11... | collective-permute-start | bytes 196616 | tf_op jit(solution)/shard_map/ppermute | solution.py:428
  43.5 0.6 copy-start.8
  45.8 12.8 %copy-start.9 = (bf16[256,128]{1,0:T(8,128)(2,1)S(1)}, bf16[256,128]{1,0:T(8,128)(2,1)}, u32[]{:S(2)}) copy-start(bf16[256,128]{1,0:T(8,128)(2,1)} %copy-done.8) | copy-start | bytes 196612
  45.8 12.0 %collective-permute-start.6 = (bf16[16,128,128]{2,1,0:T(8,128)(2,1)}, bf16[16,128,128]{2,1,0:T(8,128)(2,1)S(1)}, u32[]{:S(2)}, u32[]{:S(2)}) collective-permute-start(bf16[16,128,128]{2,1,0:T(8,128)(2,1)} %slice_bitcast_fusion.1), channel_id=1, source_target_pairs={{0,1},{1,0},{2,3},{3,2},{4,5},{5,4},{6,7},{7,6},{8,9},{9,8},{10,11... | collective-permute-start | bytes 1572872 | tf_op jit(solution)/shard_map/ppermute | solution.py:435
  45.8 45.4 %all-to-all-start.2 = ((bf16[16,2,128,128]{3,2,1,0:T(8,128)(2,1)}), bf16[16,2,128,128]{3,2,1,0:T(8,128)(2,1)S(1)}, u32[]{:S(2)}, u32[]{:S(2)}) async-start(bf16[16,2,128,128]{3,2,1,0:T(8,128)(2,1)} %pack_second.1), calls=%async_computation.2 | async-start | bytes 2097152 | tf_op jit(solution)/shard_map/all_to_all | solution.py:409
  52.4 38.1 %collective-permute-start.7 = (bf16[2,77,304]{2,1,0:T(8,128)(2,1)S(1)}, bf16[2,77,304]{2,1,0:T(8,128)(2,1)S(1)}, u32[]{:S(2)}, u32[]{:S(2)}) collective-permute-start(bf16[2,77,304]{2,1,0:T(8,128)(2,1)S(1)} %get-tuple-element.40), channel_id=1, source_target_pairs={{0,128},{32,160},{64,192},{96,224},{128,0},{160,32},{192,64},{224,... | collective-permute-start | bytes 280904 | tf_op jit(solution)/shard_map/ppermute | solution.py:437
  57.7 0.8 copy-start.5
  58.5 1.0 copy-start.6
  90.5 0.6 copy-start.11
  91.2 2.0 %collective-permute-start.8 = (bf16[2240,128]{1,0:T(8,128)(2,1)S(1)}, bf16[2240,128]{1,0:T(8,128)(2,1)S(1)}, u32[]{:S(2)}, u32[]{:S(2)}) collective-permute-start(bf16[2240,128]{1,0:T(8,128)(2,1)S(1)} %get-tuple-element.41.ex0_ref), channel_id=1, source_target_pairs={{0,1},{1,0},{2,3},{3,2},{4,5},{5,4},{6,7},{7,6},{8,9},{9,8},{10,11... | collective-permute-start | bytes 1720328 | tf_op jit(solution)/shard_map/ppermute | solution.py:440
  92.0 12.3 %collective-permute-start.9 = (bf16[16,128,128]{2,1,0:T(8,128)(2,1)}, bf16[16,128,128]{2,1,0:T(8,128)(2,1)}, u32[]{:S(2)}, u32[]{:S(2)}) collective-permute-start(bf16[16,128,128]{2,1,0:T(8,128)(2,1)} %slice_bitcast_fusion), channel_id=1, source_target_pairs={{0,1},{1,0},{2,3},{3,2},{4,5},{5,4},{6,7},{7,6},{8,9},{9,8},{10,11... | collective-permute-start | bytes 1572872 | tf_op jit(solution)/shard_map/ppermute | solution.py:441
  93.2 0.8 copy-start.2
  94.0 1.1 copy-start.3
  97.0 49.0 %all-to-all-start.1 = ((bf16[16,256,128]{2,1,0:T(8,128)(2,1)}), bf16[16,256,128]{2,1,0:T(8,128)(2,1)S(1)}, u32[]{:S(2)}, u32[]{:S(2)}) async-start(bf16[16,256,128]{2,1,0:T(8,128)(2,1)} %finish_first.1), calls=%async_computation.1 | async-start | bytes 2097152 | tf_op jit(solution)/shard_map/all_to_all | solution.py:409
  104.3 32.7 %copy-start.4 = (bf16[2240,128]{1,0:T(8,128)(2,1)S(1)}, bf16[2240,128]{1,0:T(8,128)(2,1)}, u32[]{:S(2)}) copy-start(bf16[2240,128]{1,0:T(8,128)(2,1)} %copy-done.2) | copy-start | bytes 1720324
  134.9 2.1 %collective-permute-start.10 = (bf16[2240,128]{1,0:T(8,128)(2,1)S(1)}, bf16[2240,128]{1,0:T(8,128)(2,1)S(1)}, u32[]{:S(2)}, u32[]{:S(2)}) collective-permute-start(bf16[2240,128]{1,0:T(8,128)(2,1)S(1)} %get-tuple-element.44.ex1_ref), channel_id=1, source_target_pairs={{0,1},{1,0},{2,3},{3,2},{4,5},{5,4},{6,7},{7,6},{8,9},{9,8},{10,11... | collective-permute-start | bytes 1720328 | tf_op jit(solution)/shard_map/ppermute | solution.py:444
  137.0 1.6 copy-start.1
  137.6 8.4 %collective-permute-start.11 = (bf16[80,256]{1,0:T(8,128)(2,1)S(1)}, bf16[80,256]{1,0:T(8,128)(2,1)S(1)}, u32[]{:S(2)}, u32[]{:S(2)}) collective-permute-start(bf16[80,256]{1,0:T(8,128)(2,1)S(1)} %get-tuple-element.47.own_ref), channel_id=1, source_target_pairs={{0,128},{32,160},{64,192},{96,224},{128,0},{160,32},{192,64},{224,... | collective-permute-start | bytes 122888 | tf_op jit(solution)/shard_map/ppermute | solution.py:447
  141.8 16.8 %copy-start.12 = (bf16[2,77,304]{2,1,0:T(8,128)(2,1)S(1)}, bf16[2,77,304]{2,1,0:T(8,128)(2,1)}, u32[]{:S(2)}) copy-start(bf16[2,77,304]{2,1,0:T(8,128)(2,1)} %copy-done.11) | copy-start | bytes 280900
  146.0 34.4 %all-to-all-start.3 = ((bf16[16,304,128]{2,1,0:T(8,128)(2,1)}), bf16[16,304,128]{2,1,0:T(8,128)(2,1)S(1)}, u32[]{:S(2)}, u32[]{:S(2)}) async-start(bf16[16,304,128]{2,1,0:T(8,128)(2,1)} %finish_last.1), calls=%async_computation.3 | async-start | bytes 2490368 | tf_op jit(solution)/shard_map/all_to_all | solution.py:409
  154.0 12.5 %collective-permute-start.18 = (bf16[2,80,256]{2,1,0:T(8,128)(2,1)S(1)}, bf16[2,80,256]{2,1,0:T(8,128)(2,1)S(1)}, u32[]{:S(2)}, u32[]{:S(2)}) collective-permute-start(bf16[2,80,256]{2,1,0:T(8,128)(2,1)S(1)} %pad_maximum_fusion.2), channel_id=1, source_target_pairs={{0,96},{32,0},{64,32},{96,64},{128,224},{160,128},{192,160},{224,1... | collective-permute-start | bytes 245768 | tf_op jit(solution)/shard_map/ppermute | solution.py:413
  154.8 6.6 %collective-permute-start.17 = (bf16[2,80,256]{2,1,0:T(8,128)(2,1)S(1)}, bf16[2,80,256]{2,1,0:T(8,128)(2,1)S(1)}, u32[]{:S(2)}, u32[]{:S(2)}) collective-permute-start(bf16[2,80,256]{2,1,0:T(8,128)(2,1)S(1)} %pad_maximum_fusion.2), channel_id=1, source_target_pairs={{0,64},{32,96},{64,0},{96,32},{128,192},{160,224},{192,128},{224,1... | collective-permute-start | bytes 245768 | tf_op jit(solution)/shard_map/ppermute | solution.py:413
  156.8 4.6 %collective-permute-start.16 = (bf16[2,80,256]{2,1,0:T(8,128)(2,1)S(1)}, bf16[2,80,256]{2,1,0:T(8,128)(2,1)S(1)}, u32[]{:S(2)}, u32[]{:S(2)}) collective-permute-start(bf16[2,80,256]{2,1,0:T(8,128)(2,1)S(1)} %pad_maximum_fusion.2), channel_id=1, source_target_pairs={{0,32},{32,64},{64,96},{96,0},{128,160},{160,192},{192,224},{224,1... | collective-permute-start | bytes 245768 | tf_op jit(solution)/shard_map/ppermute | solution.py:413
  158.7 2.8 %collective-permute-start.12 = (bf16[2,77,304]{2,1,0:T(8,128)(2,1)S(1)}, bf16[2,77,304]{2,1,0:T(8,128)(2,1)S(1)}, u32[]{:S(2)}, u32[]{:S(2)}) collective-permute-start(bf16[2,77,304]{2,1,0:T(8,128)(2,1)S(1)} %copy-done.12), channel_id=1, source_target_pairs={{0,1},{1,0},{2,3},{3,2},{4,5},{5,4},{6,7},{7,6},{8,9},{9,8},{10,11... | collective-permute-start | bytes 280904 | tf_op jit(solution)/shard_map/ppermute | solution.py:451
  161.7 5.9 %collective-permute-start.13 = (bf16[2,77,304]{2,1,0:T(8,128)(2,1)S(1)}, bf16[2,77,304]{2,1,0:T(8,128)(2,1)S(1)}, u32[]{:S(2)}, u32[]{:S(2)}) collective-permute-start(bf16[2,77,304]{2,1,0:T(8,128)(2,1)S(1)} %get-tuple-element.70), channel_id=1, source_target_pairs={{0,32},{32,64},{64,96},{96,0},{128,160},{160,192},{192,224},{224,1... | collective-permute-start | bytes 280904 | tf_op jit(solution)/shard_map/ppermute | solution.py:456
  163.4 6.4 %collective-permute-start.14 = (bf16[2,77,304]{2,1,0:T(8,128)(2,1)S(1)}, bf16[2,77,304]{2,1,0:T(8,128)(2,1)S(1)}, u32[]{:S(2)}, u32[]{:S(2)}) collective-permute-start(bf16[2,77,304]{2,1,0:T(8,128)(2,1)S(1)} %get-tuple-element.71), channel_id=1, source_target_pairs={{0,64},{32,96},{64,0},{96,32},{128,192},{160,224},{192,128},{224,1... | collective-permute-start | bytes 280904 | tf_op jit(solution)/shard_map/ppermute | solution.py:456
  166.4 4.9 %collective-permute-start.15 = (bf16[2,77,304]{2,1,0:T(8,128)(2,1)S(1)}, bf16[2,77,304]{2,1,0:T(8,128)(2,1)S(1)}, u32[]{:S(2)}, u32[]{:S(2)}) collective-permute-start(bf16[2,77,304]{2,1,0:T(8,128)(2,1)S(1)} %get-tuple-element.72), channel_id=1, source_target_pairs={{0,96},{32,0},{64,32},{96,64},{128,224},{160,128},{192,160},{224,1... | collective-permute-start | bytes 280904 | tf_op jit(solution)/shard_map/ppermute | solution.py:456

commit v4 on v3

--- a/solution.py
+++ b/solution.py
@@ -201,8 +201,6 @@
 
 
 def attend(phase, ids, received, other, text, text_other, y_rows):
-    half = (CHIPS, TOK, 128)
-    text_shape = (2 * TXT_PAD, 128)
     return pl.pallas_call(
         functools.partial(attend_kernel, phase),
         grid=(STEPS,),
@@ -215,9 +213,9 @@
             IN_SMEM,
             pl.BlockSpec((SRC_STEP, None, TOK, 128), lambda i: (i, 0, 0, 0)),
             pl.BlockSpec((CHIPS, None, TOK, 128), lambda i: (0, 1, 0, 0)),
-            whole(half),
-            whole(text_shape),
-            whole(text_shape),
+            IN_VMEM,
+            IN_VMEM,
+            IN_VMEM,
         ],
         out_specs=(whole((CHIPS, y_rows, 128)), whole((TAIL + MINE, 128)), whole((TXT_PAD, 128))),
         scratch_shapes=[
@@ -240,15 +238,17 @@
         y_ref[i] = (y_in[i].astype(f32) + got).astype(bf16)
 
 
+def finish_first_kernel(y_in, got_ref, y_ref):
+    y_ref[:, :TOK] = y_in[:, :TOK]
+    add_shares(y_in.at[:, TOK:], got_ref, y_ref.at[:, TOK:])
+
+
 def finish_first(y, got):
-    part = pl.BlockSpec((CHIPS, TOK, 128), lambda i: (0, 1, 0))
-    return pl.pallas_call(
-        add_shares,
-        grid=(1,),
+    return pl.pallas_call(
+        finish_first_kernel,
         out_shape=SDS(y.shape, bf16),
-        in_specs=[part, whole(got.shape)],
-        out_specs=part,
-        input_output_aliases={0: 0},
+        in_specs=[IN_VMEM] * 2,
+        out_specs=IN_VMEM,
         name="finish_first",
         cost_estimate=cost(2),
         compiler_params=params(),

time: 186 us -> 183 us (0.984)
    unnamed x38 -> x36, local copies, waits for them, and re-layouts: 5.99 us -> 5.82 us
where the time goes in v4:
time: 183 us; the launch traced here: 181 us
  Pallas kernels  78.2 us (43%)
  starting transfers between devices  58 us (32%)
  waiting for transfers between devices  35.3 us (19%)
  local copies, waits for them, and re-layouts  7.74 us (4%)
    pallas_call x2, Pallas kernels, attend(): pl.pallas_call(functools.partial(attend_kernel, phase), grid=(STEPS,), ou...  60.6 us
    all_to_all x4, starting transfers between devices, exchange(): return lax.all_to_all(x, 'seq', 0, 0, axis_index_groups=parity, tiled=True)  29.9 us
    ppermute x6, waiting for transfers between devices, around(): lax.ppermute(both, 'dp', t)  14.7 us
    ppermute x6, starting transfers between devices, around(): lax.ppermute(both, 'dp', t)  8.99 us
    all_to_all x4, waiting for transfers between devices, exchange(): return lax.all_to_all(x, 'seq', 0, 0, axis_index_groups=parity, tiled=True)  8.68 us
    pallas_call x2, Pallas kernels, pack(): pl.pallas_call(functools.partial(pack_kernel, phase), grid=(grid,), out_s...  7.7 us
    ppermute x1, starting transfers between devices, local(): w_across = lax.ppermute(w_own, 'dp', across)  7.28 us
    unnamed x36, local copies, waits for them, and re-layouts  5.82 us
  transfers between devices with their start and end apart: 23, of which 12 were waited for; matrix products, arithmetic and copies ran while one was open for 1% of the time, Pallas kernels for 42%

profile of v4, /device:TPU:8, one launch (start us, length us, event | category | flops | bytes accessed | tf_op | source)
XLA Modules:
  0.0 180.7 jit_solution(17882460109594561188)
XLA Ops:
  0.6 7.3 %collective-permute-start = (bf16[192,304]{1,0:T(8,128)(2,1)}, bf16[192,304]{1,0:T(8,128)(2,1)S(1)}, u32[]{:S(2)}, u32[]{:S(2)}) collective-permute-start(bf16[192,304]{1,0:T(8,128)(2,1)} %bitcast.66), channel_id=1, source_target_pairs={{0,128},{32,160},{64,192},{96,224},{128,0},{160,32},{192,64},{224,... | collective-permute-start | bytes 350216 | tf_op jit(solution)/shard_map/ppermute | solution.py:421
  7.9 3.8 %pack_first.1 = bf16[16,2,128,128]{3,2,1,0:T(8,128)(2,1)} custom-call(bf16[128,2048]{1,0:T(8,128)(2,1)} %bitcast.73, bf16[128,2048]{1,0:T(8,128)(2,1)} %bitcast.75, bf16[128,2048]{1,0:T(8,128)(2,1)} %bitcast.77, bf16[128,2048]{1,0:T(8,128)(2,1)} %bitcast.79), custom_call_target="tpu_custom_call" | custom-call | flops 3449999872 | bytes 1048576 | tf_op jit(solution)/shard_map/pack_first/pallas_call | solution.py:72
  11.8 0.3 collective-permute-done
  12.1 8.9 %all-to-all-start = ((bf16[16,2,128,128]{3,2,1,0:T(8,128)(2,1)}), bf16[16,2,128,128]{3,2,1,0:T(8,128)(2,1)S(1)}, u32[]{:S(2)}, u32[]{:S(2)}) async-start(bf16[16,2,128,128]{3,2,1,0:T(8,128)(2,1)} %pack_first.1), calls=%async_computation | async-start | bytes 2097152 | tf_op jit(solution)/shard_map/all_to_all | solution.py:409
  21.0 1.7 collective-permute-start.1
  22.7 0.5 collective-permute-start.3
  23.2 2.3 %collective-permute-start.2 = (bf16[2,192,304]{2,1,0:T(8,128)(2,1)S(1)}, bf16[2,192,304]{2,1,0:T(8,128)(2,1)S(1)}, u32[]{:S(2)}, u32[]{:S(2)}) collective-permute-start(bf16[2,192,304]{2,1,0:T(8,128)(2,1)S(1)} %pad_maximum_fusion.1), channel_id=1, source_target_pairs={{0,64},{32,96},{64,0},{96,32},{128,192},{160,224},{192,128},{224,1... | collective-permute-start | bytes 700424 | tf_op jit(solution)/shard_map/ppermute | solution.py:413
  25.5 5.5 %collective-permute-done.1 = bf16[2,192,304]{2,1,0:T(8,128)(2,1)S(1)} collective-permute-done((bf16[2,192,304]{2,1,0:T(8,128)(2,1)S(1)}, bf16[2,192,304]{2,1,0:T(8,128)(2,1)S(1)}, u32[]{:S(2)}, u32[]{:S(2)}) %collective-permute-start.1) | collective-permute-done | bytes 233504 | tf_op jit(solution)/shard_map/ppermute | solution.py:413
  31.1 6.2 %collective-permute-done.2 = bf16[2,192,304]{2,1,0:T(8,128)(2,1)S(1)} collective-permute-done((bf16[2,192,304]{2,1,0:T(8,128)(2,1)S(1)}, bf16[2,192,304]{2,1,0:T(8,128)(2,1)S(1)}, u32[]{:S(2)}, u32[]{:S(2)}) %collective-permute-start.2) | collective-permute-done | bytes 233504 | tf_op jit(solution)/shard_map/ppermute | solution.py:413
  37.9 1.3 project.1
  39.2 0.8 copy-done
  39.9 0.4 collective-permute-start.4
  40.3 3.9 %pack_second.1 = bf16[16,2,128,128]{3,2,1,0:T(8,128)(2,1)} custom-call(bf16[128,2048]{1,0:T(8,128)(2,1)} %bitcast.74, bf16[128,2048]{1,0:T(8,128)(2,1)} %bitcast.76, bf16[128,2048]{1,0:T(8,128)(2,1)} %bitcast.78, bf16[128,2048]{1,0:T(8,128)(2,1)} %bitcast.80), custom_call_target="tpu_custom_call" | custom-call | flops 3449999872 | bytes 1048576 | tf_op jit(solution)/shard_map/pack_second/pallas_call | solution.py:72
  44.2 0.7 all-to-all-done.q_ref.own_kv_ref
  44.9 0.8 slice_bitcast_fusion.1
  45.7 6.7 %all-to-all-start.2 = ((bf16[16,2,128,128]{3,2,1,0:T(8,128)(2,1)}), bf16[16,2,128,128]{3,2,1,0:T(8,128)(2,1)S(1)}, u32[]{:S(2)}, u32[]{:S(2)}) async-start(bf16[16,2,128,128]{3,2,1,0:T(8,128)(2,1)} %pack_second.1), calls=%async_computation.2 | async-start | bytes 2097152 | tf_op jit(solution)/shard_map/all_to_all | solution.py:409
  52.4 5.3 %collective-permute-start.7 = (bf16[2,77,304]{2,1,0:T(8,128)(2,1)S(1)}, bf16[2,77,304]{2,1,0:T(8,128)(2,1)S(1)}, u32[]{:S(2)}, u32[]{:S(2)}) collective-permute-start(bf16[2,77,304]{2,1,0:T(8,128)(2,1)S(1)} %get-tuple-element.40), channel_id=1, source_target_pairs={{0,128},{32,160},{64,192},{96,224},{128,0},{160,32},{192,64},{224,... | collective-permute-start | bytes 280904 | tf_op jit(solution)/shard_map/ppermute | solution.py:437
  57.8 0.8 copy-done.6
  58.6 1.0 copy-done.7
  59.6 30.0 %attend_first.1 = (bf16[16,256,128]{2,1,0:T(8,128)(2,1)S(1)}, bf16[2240,128]{1,0:T(8,128)(2,1)S(1)}, f32[128,128]{1,0:T(8,128)S(1)}) custom-call(s32[18]{0:T(128)S(1)} %stack.97.ids_ref, bf16[16,2,128,128]{3,2,1,0:T(8,128)(2,1)S(1)} %all-to-all-done.q_ref.own_kv_ref, bf16[16,2,128,128]{3,2,1,0:T(8,128)(2,1)S(1)} %all-to-all-done.q_ref.own_kv_ref, ...), custom_call_target="tpu_custom_call" | custom-call | flops 39099998208 | bytes 1048576 | tf_op jit(solution)/shard_map/attend_first/pallas_call | solution.py:204
  89.6 1.0 copy-done.9
  90.6 0.9 slice_bitcast_fusion
  91.5 0.4 collective-permute-start.9
  91.9 0.6 collective-permute-done.8.got_ref.got0_ref
  92.6 1.2 copy-done.10
  93.8 1.1 finish_first.1
  94.9 7.3 %all-to-all-start.1 = ((bf16[16,256,128]{2,1,0:T(8,128)(2,1)}), bf16[16,256,128]{2,1,0:T(8,128)(2,1)S(1)}, u32[]{:S(2)}, u32[]{:S(2)}) async-start(bf16[16,256,128]{2,1,0:T(8,128)(2,1)} %finish_first.1), calls=%async_computation.1 | async-start | bytes 2097152 | tf_op jit(solution)/shard_map/all_to_all | solution.py:409
  102.2 30.6 %attend_second.1 = (bf16[16,304,128]{2,1,0:T(8,128)(2,1)S(1)}, bf16[2240,128]{1,0:T(8,128)(2,1)S(1)}, f32[128,128]{1,0:T(8,128)S(1)}) custom-call(s32[18]{0:T(128)S(1)} %stack.97.ids_ref, bf16[16,2,128,128]{3,2,1,0:T(8,128)(2,1)S(1)} %all-to-all-done.2.q_ref.own_kv_ref, bf16[16,2,128,128]{3,2,1,0:T(8,128)(2,1)S(1)} %all-to-all-done.2.q_ref.own_kv_ref, ...), custom_call_target="tpu_custom_call" | custom-call | flops 39099998208 | bytes 1048576 | tf_op jit(solution)/shard_map/attend_second/pallas_call | solution.py:204
  132.9 2.0 %collective-permute-done.10.got1_ref.got_ref = bf16[2240,128]{1,0:T(8,128)(2,1)S(1)} collective-permute-done((bf16[2240,128]{1,0:T(8,128)(2,1)S(1)}, bf16[2240,128]{1,0:T(8,128)(2,1)S(1)}, u32[]{:S(2)}, u32[]{:S(2)}) %collective-permute-start.10) | collective-permute-done | bytes 573472 | tf_op jit(solution)/shard_map/ppermute | solution.py:444
  134.9 0.6 text_grads.1
  135.5 0.9 collective-permute-start.11
  136.5 3.2 %finish_last.1 = bf16[16,304,128]{2,1,0:T(8,128)(2,1)} custom-call(s32[18]{0:T(128)S(1)} %stack.97.ids_ref, bf16[16,304,128]{2,1,0:T(8,128)(2,1)S(1)} %get-tuple-element.43.y_in, bf16[2240,128]{1,0:T(8,128)(2,1)S(1)} %collective-permute-done.10.got1_ref.got_ref, bf16[80,256]{1,0:T(8,128)(2,1)S(1)} %get-tuple-element.47.own_ref, ...), custom_call_target="tpu_custom_call" | custom-call | flops 5750000128 | bytes 1048576 | tf_op jit(solution)/shard_map/finish_last/pallas_call | solution.py:322
  139.7 4.2 %collective-permute-done.11 = bf16[80,256]{1,0:T(8,128)(2,1)S(1)} collective-permute-done((bf16[80,256]{1,0:T(8,128)(2,1)S(1)}, bf16[80,256]{1,0:T(8,128)(2,1)S(1)}, u32[]{:S(2)}, u32[]{:S(2)}) %collective-permute-start.11) | collective-permute-done | bytes 40992 | tf_op jit(solution)/shard_map/ppermute | solution.py:447
  143.9 7.1 %all-to-all-start.3 = ((bf16[16,304,128]{2,1,0:T(8,128)(2,1)}), bf16[16,304,128]{2,1,0:T(8,128)(2,1)S(1)}, u32[]{:S(2)}, u32[]{:S(2)}) async-start(bf16[16,304,128]{2,1,0:T(8,128)(2,1)} %finish_last.1), calls=%async_computation.3 | async-start | bytes 2490368 | tf_op jit(solution)/shard_map/all_to_all | solution.py:409
  151.2 0.7 copy.24
  151.9 0.8 collective-permute-start.18
  152.7 1.8 collective-permute-start.17
  154.5 1.9 %collective-permute-start.16 = (bf16[2,80,256]{2,1,0:T(8,128)(2,1)S(1)}, bf16[2,80,256]{2,1,0:T(8,128)(2,1)S(1)}, u32[]{:S(2)}, u32[]{:S(2)}) collective-permute-start(bf16[2,80,256]{2,1,0:T(8,128)(2,1)S(1)} %pad_maximum_fusion.2), channel_id=1, source_target_pairs={{0,32},{32,64},{64,96},{96,0},{128,160},{160,192},{192,224},{224,1... | collective-permute-start | bytes 245768 | tf_op jit(solution)/shard_map/ppermute | solution.py:413
  156.4 2.9 %collective-permute-done.16 = bf16[2,80,256]{2,1,0:T(8,128)(2,1)S(1)} collective-permute-done((bf16[2,80,256]{2,1,0:T(8,128)(2,1)S(1)}, bf16[2,80,256]{2,1,0:T(8,128)(2,1)S(1)}, u32[]{:S(2)}, u32[]{:S(2)}) %collective-permute-start.16) | collective-permute-done | bytes 81952 | tf_op jit(solution)/shard_map/ppermute | solution.py:413
  159.6 1.6 collective-permute-start.13
  161.2 3.0 %collective-permute-start.14 = (bf16[2,77,304]{2,1,0:T(8,128)(2,1)S(1)}, bf16[2,77,304]{2,1,0:T(8,128)(2,1)S(1)}, u32[]{:S(2)}, u32[]{:S(2)}) collective-permute-start(bf16[2,77,304]{2,1,0:T(8,128)(2,1)S(1)} %get-tuple-element.71), channel_id=1, source_target_pairs={{0,64},{32,96},{64,0},{96,32},{128,192},{160,224},{192,128},{224,1... | collective-permute-start | bytes 280904 | tf_op jit(solution)/shard_map/ppermute | solution.py:456
  164.2 1.3 collective-permute-done.13
  165.4 2.1 %collective-permute-done.14 = bf16[2,77,304]{2,1,0:T(8,128)(2,1)S(1)} collective-permute-done((bf16[2,77,304]{2,1,0:T(8,128)(2,1)S(1)}, bf16[2,77,304]{2,1,0:T(8,128)(2,1)S(1)}, u32[]{:S(2)}, u32[]{:S(2)}) %collective-permute-start.14) | collective-permute-done | bytes 93664 | tf_op jit(solution)/shard_map/ppermute | solution.py:456
  167.5 1.5 collective-permute-done.15
  169.0 0.1 pad_maximum_fusion.x_ref
  169.1 1.2 weight_grad.1
  170.3 8.0 %all-to-all-done.3.z1_ref = bf16[16,304,128]{2,1,0:T(8,128)(2,1)S(1)} async-done(((bf16[16,304,128]{2,1,0:T(8,128)(2,1)}), bf16[16,304,128]{2,1,0:T(8,128)(2,1)S(1)}, u32[]{:S(2)}, u32[]{:S(2)}) %all-to-all-start.3) | async-done | bytes 1245216 | tf_op jit(solution)/shard_map/all_to_all | solution.py:409
  178.3 2.4 %unpack.1 = (bf16[128,2048]{1,0:T(8,128)(2,1)}, bf16[3,128,2048]{2,1,0:T(8,128)(2,1)}, f32[76,1,77]{2,1,0:T(1,128)}) custom-call(bf16[16,256,128]{2,1,0:T(8,128)(2,1)S(1)} %all-to-all-done.1.z0_ref, bf16[16,304,128]{2,1,0:T(8,128)(2,1)S(1)} %all-to-all-done.3.z1_ref), custom_call_target="tpu_custom_call" | custom-call | flops 4600000000 | bytes 1048576 | tf_op jit(solution)/shard_map/unpack/pallas_call | solution.py:363
  (55 shorter events, 1.0 us)
Async XLA Ops:
  0.6 11.4 %collective-permute-start = (bf16[192,304]{1,0:T(8,128)(2,1)}, bf16[192,304]{1,0:T(8,128)(2,1)S(1)}, u32[]{:S(2)}, u32[]{:S(2)}) collective-permute-start(bf16[192,304]{1,0:T(8,128)(2,1)} %bitcast.66), channel_id=1, source_target_pairs={{0,128},{32,160},{64,192},{96,224},{128,0},{160,32},{192,64},{224,... | collective-permute-start | bytes 350216 | tf_op jit(solution)/shard_map/ppermute | solution.py:421
  11.8 9.2 %copy-start.11 = (bf16[3,304,64]{1,2,0:T(8,128)(2,1)S(1)}, bf16[3,304,64]{1,2,0:T(8,128)(2,1)}, u32[]{:S(2)}) copy-start(bf16[3,304,64]{1,2,0:T(8,128)(2,1)} %param.11) | copy-start | bytes 350212
  12.1 32.8 %all-to-all-start = ((bf16[16,2,128,128]{3,2,1,0:T(8,128)(2,1)}), bf16[16,2,128,128]{3,2,1,0:T(8,128)(2,1)S(1)}, u32[]{:S(2)}, u32[]{:S(2)}) async-start(bf16[16,2,128,128]{3,2,1,0:T(8,128)(2,1)} %pack_first.1), calls=%async_computation | async-start | bytes 2097152 | tf_op jit(solution)/shard_map/all_to_all | solution.py:409
  21.0 10.0 %collective-permute-start.1 = (bf16[2,192,304]{2,1,0:T(8,128)(2,1)S(1)}, bf16[2,192,304]{2,1,0:T(8,128)(2,1)S(1)}, u32[]{:S(2)}, u32[]{:S(2)}) collective-permute-start(bf16[2,192,304]{2,1,0:T(8,128)(2,1)S(1)} %pad_maximum_fusion.1), channel_id=1, source_target_pairs={{0,32},{32,64},{64,96},{96,0},{128,160},{160,192},{192,224},{224,1... | collective-permute-start | bytes 700424 | tf_op jit(solution)/shard_map/ppermute | solution.py:413
  22.7 15.0 %copy-start.12 = (bf16[1,77,64]{1,2,0:T(8,128)(2,1)S(1)}, bf16[1,77,64]{1,2,0:T(8,128)(2,1)}, u32[]{:S(2)}) copy-start(bf16[1,77,64]{1,2,0:T(8,128)(2,1)} %param.13) | copy-start | bytes 29572
  22.7 15.2 %copy-start.8 = (bf16[1,77,2432]{2,1,0:T(8,128)(2,1)S(1)}, bf16[1,77,2432]{2,1,0:T(8,128)(2,1)}, u32[]{:S(2)}) copy-start(bf16[1,77,2432]{2,1,0:T(8,128)(2,1)} %param.10) | copy-start | bytes 1123588
  22.7 14.7 %collective-permute-start.3 = (bf16[2,192,304]{2,1,0:T(8,128)(2,1)S(1)}, bf16[2,192,304]{2,1,0:T(8,128)(2,1)S(1)}, u32[]{:S(2)}, u32[]{:S(2)}) collective-permute-start(bf16[2,192,304]{2,1,0:T(8,128)(2,1)S(1)} %pad_maximum_fusion.1), channel_id=1, source_target_pairs={{0,96},{32,0},{64,32},{96,64},{128,224},{160,128},{192,160},{224,1... | collective-permute-start | bytes 700424 | tf_op jit(solution)/shard_map/ppermute | solution.py:413
  23.2 14.1 %collective-permute-start.2 = (bf16[2,192,304]{2,1,0:T(8,128)(2,1)S(1)}, bf16[2,192,304]{2,1,0:T(8,128)(2,1)S(1)}, u32[]{:S(2)}, u32[]{:S(2)}) collective-permute-start(bf16[2,192,304]{2,1,0:T(8,128)(2,1)S(1)} %pad_maximum_fusion.1), channel_id=1, source_target_pairs={{0,64},{32,96},{64,0},{96,32},{128,192},{160,224},{192,128},{224,1... | collective-permute-start | bytes 700424 | tf_op jit(solution)/shard_map/ppermute | solution.py:413
  37.4 1.7 copy-start.2
  37.4 6.8 %collective-permute-start.5 = (bf16[8,192,304]{2,1,0:T(8,128)(2,1)S(1)}, bf16[8,192,304]{2,1,0:T(8,128)(2,1)}, u32[]{:S(2)}, u32[]{:S(2)}) collective-permute-start(bf16[8,192,304]{2,1,0:T(8,128)(2,1)S(1)} %constant_dynamic-update-slice_fusion.w_ref), channel_id=1, source_target_pairs={{0,1},{1,0},{2,3},{3,2},{4,5},{5,4},{6,7},{7,6},{8,9},{9,8},{10,11... | collective-permute-start | bytes 2801672 | tf_op jit(solution)/shard_map/ppermute | solution.py:429
  39.1 0.8 copy-start
  39.9 4.2 %collective-permute-start.4 = (bf16[256,128]{1,0:T(8,128)(2,1)S(1)}, bf16[256,128]{1,0:T(8,128)(2,1)S(1)}, u32[]{:S(2)}, u32[]{:S(2)}) collective-permute-start(bf16[256,128]{1,0:T(8,128)(2,1)S(1)} %get-tuple-element.34.text_ref), channel_id=1, source_target_pairs={{0,1},{1,0},{2,3},{3,2},{4,5},{5,4},{6,7},{7,6},{8,9},{9,8},{10,11... | collective-permute-start | bytes 196616 | tf_op jit(solution)/shard_map/ppermute | solution.py:428
  45.7 12.0 %collective-permute-start.6 = (bf16[16,128,128]{2,1,0:T(8,128)(2,1)}, bf16[16,128,128]{2,1,0:T(8,128)(2,1)S(1)}, u32[]{:S(2)}, u32[]{:S(2)}) collective-permute-start(bf16[16,128,128]{2,1,0:T(8,128)(2,1)} %slice_bitcast_fusion.1), channel_id=1, source_target_pairs={{0,1},{1,0},{2,3},{3,2},{4,5},{5,4},{6,7},{7,6},{8,9},{9,8},{10,11... | collective-permute-start | bytes 1572872 | tf_op jit(solution)/shard_map/ppermute | solution.py:435
  45.7 44.9 %all-to-all-start.2 = ((bf16[16,2,128,128]{3,2,1,0:T(8,128)(2,1)}), bf16[16,2,128,128]{3,2,1,0:T(8,128)(2,1)S(1)}, u32[]{:S(2)}, u32[]{:S(2)}) async-start(bf16[16,2,128,128]{3,2,1,0:T(8,128)(2,1)} %pack_second.1), calls=%async_computation.2 | async-start | bytes 2097152 | tf_op jit(solution)/shard_map/all_to_all | solution.py:409
  52.4 38.2 %collective-permute-start.7 = (bf16[2,77,304]{2,1,0:T(8,128)(2,1)S(1)}, bf16[2,77,304]{2,1,0:T(8,128)(2,1)S(1)}, u32[]{:S(2)}, u32[]{:S(2)}) collective-permute-start(bf16[2,77,304]{2,1,0:T(8,128)(2,1)S(1)} %get-tuple-element.40), channel_id=1, source_target_pairs={{0,128},{32,160},{64,192},{96,224},{128,0},{160,32},{192,64},{224,... | collective-permute-start | bytes 280904 | tf_op jit(solution)/shard_map/ppermute | solution.py:437
  57.8 0.8 copy-start.6
  58.6 1.0 copy-start.7
  89.6 1.0 copy-start.9
  90.6 4.3 %copy-start.4 = (bf16[2240,128]{1,0:T(8,128)(2,1)}, bf16[2240,128]{1,0:T(8,128)(2,1)S(1)}, u32[]{:S(2)}) copy-start(bf16[2240,128]{1,0:T(8,128)(2,1)S(1)} %get-tuple-element.41.ex0_ref) | copy-start | bytes 1720324
  90.6 2.0 %collective-permute-start.8 = (bf16[2240,128]{1,0:T(8,128)(2,1)S(1)}, bf16[2240,128]{1,0:T(8,128)(2,1)S(1)}, u32[]{:S(2)}, u32[]{:S(2)}) collective-permute-start(bf16[2240,128]{1,0:T(8,128)(2,1)S(1)} %get-tuple-element.41.ex0_ref), channel_id=1, source_target_pairs={{0,1},{1,0},{2,3},{3,2},{4,5},{5,4},{6,7},{7,6},{8,9},{9,8},{10,11... | collective-permute-start | bytes 1720328 | tf_op jit(solution)/shard_map/ppermute | solution.py:440
  91.5 10.7 %collective-permute-start.9 = (bf16[16,128,128]{2,1,0:T(8,128)(2,1)}, bf16[16,128,128]{2,1,0:T(8,128)(2,1)}, u32[]{:S(2)}, u32[]{:S(2)}) collective-permute-start(bf16[16,128,128]{2,1,0:T(8,128)(2,1)} %slice_bitcast_fusion), channel_id=1, source_target_pairs={{0,1},{1,0},{2,3},{3,2},{4,5},{5,4},{6,7},{7,6},{8,9},{9,8},{10,11... | collective-permute-start | bytes 1572872 | tf_op jit(solution)/shard_map/ppermute | solution.py:441
  92.6 1.2 copy-start.10
  94.9 49.0 %all-to-all-start.1 = ((bf16[16,256,128]{2,1,0:T(8,128)(2,1)}), bf16[16,256,128]{2,1,0:T(8,128)(2,1)S(1)}, u32[]{:S(2)}, u32[]{:S(2)}) async-start(bf16[16,256,128]{2,1,0:T(8,128)(2,1)} %finish_first.1), calls=%async_computation.1 | async-start | bytes 2097152 | tf_op jit(solution)/shard_map/all_to_all | solution.py:409
  102.2 32.7 %copy-start.5 = (bf16[2240,128]{1,0:T(8,128)(2,1)S(1)}, bf16[2240,128]{1,0:T(8,128)(2,1)}, u32[]{:S(2)}) copy-start(bf16[2240,128]{1,0:T(8,128)(2,1)} %copy-done.4) | copy-start | bytes 1720324
  132.8 2.1 %collective-permute-start.10 = (bf16[2240,128]{1,0:T(8,128)(2,1)S(1)}, bf16[2240,128]{1,0:T(8,128)(2,1)S(1)}, u32[]{:S(2)}, u32[]{:S(2)}) collective-permute-start(bf16[2240,128]{1,0:T(8,128)(2,1)S(1)} %get-tuple-element.44.ex1_ref), channel_id=1, source_target_pairs={{0,1},{1,0},{2,3},{3,2},{4,5},{5,4},{6,7},{7,6},{8,9},{9,8},{10,11... | collective-permute-start | bytes 1720328 | tf_op jit(solution)/shard_map/ppermute | solution.py:444
  134.9 1.6 copy-start.3
  135.5 8.4 %collective-permute-start.11 = (bf16[80,256]{1,0:T(8,128)(2,1)S(1)}, bf16[80,256]{1,0:T(8,128)(2,1)S(1)}, u32[]{:S(2)}, u32[]{:S(2)}) collective-permute-start(bf16[80,256]{1,0:T(8,128)(2,1)S(1)} %get-tuple-element.47.own_ref), channel_id=1, source_target_pairs={{0,128},{32,160},{64,192},{96,224},{128,0},{160,32},{192,64},{224,... | collective-permute-start | bytes 122888 | tf_op jit(solution)/shard_map/ppermute | solution.py:447
  139.7 11.4 %copy-start.1 = (bf16[8,77,304]{2,1,0:T(8,128)(2,1)S(1)}, bf16[8,77,304]{2,1,0:T(8,128)(2,1)}, u32[]{:S(2)}) copy-start(bf16[8,77,304]{2,1,0:T(8,128)(2,1)} %copy-done) | copy-start | bytes 1123588
  143.9 34.4 %all-to-all-start.3 = ((bf16[16,304,128]{2,1,0:T(8,128)(2,1)}), bf16[16,304,128]{2,1,0:T(8,128)(2,1)S(1)}, u32[]{:S(2)}, u32[]{:S(2)}) async-start(bf16[16,304,128]{2,1,0:T(8,128)(2,1)} %finish_last.1), calls=%async_computation.3 | async-start | bytes 2490368 | tf_op jit(solution)/shard_map/all_to_all | solution.py:409
  151.9 12.3 %collective-permute-start.18 = (bf16[2,80,256]{2,1,0:T(8,128)(2,1)S(1)}, bf16[2,80,256]{2,1,0:T(8,128)(2,1)S(1)}, u32[]{:S(2)}, u32[]{:S(2)}) collective-permute-start(bf16[2,80,256]{2,1,0:T(8,128)(2,1)S(1)} %pad_maximum_fusion.2), channel_id=1, source_target_pairs={{0,96},{32,0},{64,32},{96,64},{128,224},{160,128},{192,160},{224,1... | collective-permute-start | bytes 245768 | tf_op jit(solution)/shard_map/ppermute | solution.py:413
  152.7 6.6 %collective-permute-start.17 = (bf16[2,80,256]{2,1,0:T(8,128)(2,1)S(1)}, bf16[2,80,256]{2,1,0:T(8,128)(2,1)S(1)}, u32[]{:S(2)}, u32[]{:S(2)}) collective-permute-start(bf16[2,80,256]{2,1,0:T(8,128)(2,1)S(1)} %pad_maximum_fusion.2), channel_id=1, source_target_pairs={{0,64},{32,96},{64,0},{96,32},{128,192},{160,224},{192,128},{224,1... | collective-permute-start | bytes 245768 | tf_op jit(solution)/shard_map/ppermute | solution.py:413
  154.5 4.8 %collective-permute-start.16 = (bf16[2,80,256]{2,1,0:T(8,128)(2,1)S(1)}, bf16[2,80,256]{2,1,0:T(8,128)(2,1)S(1)}, u32[]{:S(2)}, u32[]{:S(2)}) collective-permute-start(bf16[2,80,256]{2,1,0:T(8,128)(2,1)S(1)} %pad_maximum_fusion.2), channel_id=1, source_target_pairs={{0,32},{32,64},{64,96},{96,0},{128,160},{160,192},{192,224},{224,1... | collective-permute-start | bytes 245768 | tf_op jit(solution)/shard_map/ppermute | solution.py:413
  156.4 3.0 %collective-permute-start.12 = (bf16[2,77,304]{2,1,0:T(8,128)(2,1)S(1)}, bf16[2,77,304]{2,1,0:T(8,128)(2,1)S(1)}, u32[]{:S(2)}, u32[]{:S(2)}) collective-permute-start(bf16[2,77,304]{2,1,0:T(8,128)(2,1)S(1)} %collective-permute-done.7), channel_id=1, source_target_pairs={{0,1},{1,0},{2,3},{3,2},{4,5},{5,4},{6,7},{7,6},{8,9},{9,8},{10,11... | collective-permute-start | bytes 280904 | tf_op jit(solution)/shard_map/ppermute | solution.py:451
  159.6 5.9 %collective-permute-start.13 = (bf16[2,77,304]{2,1,0:T(8,128)(2,1)S(1)}, bf16[2,77,304]{2,1,0:T(8,128)(2,1)S(1)}, u32[]{:S(2)}, u32[]{:S(2)}) collective-permute-start(bf16[2,77,304]{2,1,0:T(8,128)(2,1)S(1)} %get-tuple-element.70), channel_id=1, source_target_pairs={{0,32},{32,64},{64,96},{96,0},{128,160},{160,192},{192,224},{224,1... | collective-permute-start | bytes 280904 | tf_op jit(solution)/shard_map/ppermute | solution.py:456
  161.2 6.4 %collective-permute-start.14 = (bf16[2,77,304]{2,1,0:T(8,128)(2,1)S(1)}, bf16[2,77,304]{2,1,0:T(8,128)(2,1)S(1)}, u32[]{:S(2)}, u32[]{:S(2)}) collective-permute-start(bf16[2,77,304]{2,1,0:T(8,128)(2,1)S(1)} %get-tuple-element.71), channel_id=1, source_target_pairs={{0,64},{32,96},{64,0},{96,32},{128,192},{160,224},{192,128},{224,1... | collective-permute-start | bytes 280904 | tf_op jit(solution)/shard_map/ppermute | solution.py:456
  164.1 4.9 %collective-permute-start.15 = (bf16[2,77,304]{2,1,0:T(8,128)(2,1)S(1)}, bf16[2,77,304]{2,1,0:T(8,128)(2,1)S(1)}, u32[]{:S(2)}, u32[]{:S(2)}) collective-permute-start(bf16[2,77,304]{2,1,0:T(8,128)(2,1)S(1)} %get-tuple-element.72), channel_id=1, source_target_pairs={{0,96},{32,0},{64,32},{96,64},{128,224},{160,128},{192,160},{224,1... | collective-permute-start | bytes 280904 | tf_op jit(solution)/shard_map/ppermute | solution.py:456
